TPU v7x, 32 devices: a whole 2x2x4 slice. The times are simulated.
32 devices in a mesh: ctx: 8 (over z, x), tp: 4 (over y, core).
Axes of the slice: x: 2, y: 2, z: 4, core: 2. Of those that a mesh axis runs over, the one named last changes fastest.
Arguments:
- tokens: bfloat16 [6144, 4096], P('ctx'), may hold values from -6 to 6
- qkv_weight: bfloat16 [3, 4096, 4096], P(None, 'ctx', 'tp'), may hold values from -0.09375 to 0.09375
- short_filter: float32 [3, 7, 4096], P(None, None, 'tp'), may hold values from -2.4 to 2.4
- long_filter: float32 [256, 128], P('tp'), may hold values from -0.9 to 0.9
- decay_rate: float32 [256], P('tp'), may hold values from 0.004 to 0.2
- skip_gain: float32 [4096], P('tp'), may hold values from -3 to 3
- out_weight: bfloat16 [4096, 4096], P('tp', 'ctx'), may hold values from -0.09375 to 0.09375
Outputs:
- block_out: bfloat16 [6144, 4096], P(('ctx', 'tp'))
All inputs are finite; a program needn't handle non-finite values.
Results may differ from a plain program's by a relative error of at most 0.008.
Values may be sent and summed in bfloat16 or wider, within the bound.
No kernel may reach another device: no remote copies, remote signals or barrier semaphores. Data moves between devices by JAX's collectives and lax.ppermute only.
A program may use at most 128 MiB of HBM per device.

v0:
```python
import functools

import jax
import jax.numpy as jnp
from jax import lax
from jax.experimental import pallas as pl
from jax.experimental.pallas import tpu as pltpu
from jax.sharding import PartitionSpec as P

AXES = ("ctx", "tp")
BF16, F32 = jnp.bfloat16, jnp.float32
VMEM_LIMIT = 56 << 20


class Places:
    def __init__(self, ctx, tp):
        self.ctx, self.tp = ctx, tp
        self.nx = 1 << ((ctx.bit_length() - 1) // 2)
        self.nz = ctx // self.nx
        self.ny = tp // 2

    def send(self, value, target):
        pairs = []
        for i in range(self.ctx):
            for j in range(self.tp):
                to = target(i, j)
                if to is not None:
                    pairs.append((i * self.tp + j, to[0] * self.tp + to[1]))
        return lax.ppermute(value, AXES, pairs)

    def flip(self, value, ctx=0, tp=0):
        return self.send(value, lambda i, j: (i ^ ctx, j ^ tp))

    def masks(self):
        return [m * self.nx for m in range(self.nz)]


def after(value, *done):
    done = [entry for entry in done if entry is not None]
    return lax.optimization_barrier((value, *done))[0] if done else value


class Line:
    def __init__(self, places):
        self.places, self.far = places, []

    def step(self, value, mask, *done):
        result = self.places.flip(
            after(value, self.far[-3] if len(self.far) >= 3 else None, *done), ctx=mask
        )
        self.far.append(result)
        return result

    def gather(self, own, other, *last):
        nx, nz = self.places.nx, self.places.nz
        held = {0: own}
        masks = sorted(range(1, nz), key=lambda m: (m < 2, m))
        for m in masks:
            held[m] = self.step(
                other if m % 2 else own, m * nx, *(last if m == masks[-1] else ())
            )
        return held

    def cross(self, held, *done):
        nx, nz = self.places.nx, self.places.nz
        stack = after(jnp.stack([held[m] for m in range(nz)]), *done)
        groups = [[z * nx + x for x in range(nx)] for z in range(nz)]
        return [lax.all_gather(stack, "ctx", axis_index_groups=groups, tiled=True)]


def prepare_kernel(per_part, order, flags, own, *refs):
    parts, out = refs[:-1], refs[-1]
    part = order[pl.program_id(0)] // per_part
    rows = own.shape[0]
    out[:, pl.ds(pl.multiple_of(flags[0] * rows, rows), rows)] = own[...].T
    for mask, ref in enumerate(parts):

        @pl.when(part == flags[1] ^ mask)
        def _():
            out[:, pl.ds(pl.multiple_of((1 - flags[0]) * rows, rows), rows)] = ref[...].T


def prepare(order, flags, own, parts, depth):
    rows, features = own.shape
    count = features // depth
    per_part = count // len(parts)
    return pl.pallas_call(
        functools.partial(prepare_kernel, per_part),
        out_shape=jax.ShapeDtypeStruct((features, 2 * rows), BF16),
        grid_spec=pltpu.PrefetchScalarGridSpec(
            num_scalar_prefetch=2,
            grid=(count,),
            in_specs=[pl.BlockSpec((rows, depth), lambda i, o, f: (0, o[i]))]
            + [pl.BlockSpec((rows, depth), lambda i, o, f: (0, o[i] % per_part))] * len(parts),
            out_specs=pl.BlockSpec((depth, 2 * rows), lambda i, o, f: (i, 0)),
        ),
        compiler_params=pltpu.CompilerParams(vmem_limit_bytes=VMEM_LIMIT),
        cost_estimate=pl.CostEstimate(
            flops=0, bytes_accessed=8 * rows * features, transcendentals=0
        ),
    )(order, flags, own, *parts)


def project_kernel(tokens, *refs):
    stacks, out = refs[:-1], refs[-1]
    pieces = [stack[index] for stack in stacks for index in range(stack.shape[0])]
    out[...] = jnp.dot(
        jnp.concatenate(pieces, axis=1), tokens[...], preferred_element_type=F32
    ).astype(out.dtype)


def project(tokens, stacks):
    features, rows = tokens.shape
    count, width, depth = stacks[0].shape
    tile, part = min(256, width), rows // 2
    return pl.pallas_call(
        project_kernel,
        out_shape=jax.ShapeDtypeStruct((width, rows), BF16),
        grid=(2, width // tile),
        in_specs=[pl.BlockSpec((features, part), lambda t, i: (0, t))]
        + [pl.BlockSpec((count, tile, depth), lambda t, i: (0, i, 0))] * len(stacks),
        out_specs=pl.BlockSpec((tile, part), lambda t, i: (i, t)),
        compiler_params=pltpu.CompilerParams(vmem_limit_bytes=VMEM_LIMIT),
        cost_estimate=pl.CostEstimate(
            flops=2 * width * rows * features,
            bytes_accessed=2 * ((2 * width + rows) * features + width * rows),
            transcendentals=0,
        ),
    )(tokens, *stacks)


def featurize(rim, value, coefficients, first, span):
    wide = jnp.concatenate([rim, value], axis=1).astype(F32)
    total = coefficients[:, first : first + 1] * wide
    for offset in range(1, span):
        total = total + coefficients[:, first + offset : first + offset + 1] * pltpu.roll(
            wide, offset, 1
        )
    return total[:, rim.shape[1] :]


def filter_kernel(span, k, v, k_rim, v_rim, before, coefficients, bands, out):
    coef = coefficients[...]
    first = featurize(k_rim[...], k[...], coef, span, span)
    second = featurize(v_rim[...], v[...], coef, 2 * span, span)
    gated = (first * second).astype(BF16)
    wide = jnp.concatenate([before[...], gated], axis=1)
    groups, reach, taps = bands.shape
    size = wide.shape[0] // groups
    blocks = gated.shape[1] // taps
    for group in range(groups):
        rows = slice(group * size, (group + 1) * size)
        windows = jnp.concatenate(
            [wide[rows, block * taps : block * taps + reach] for block in range(blocks)], axis=0
        )
        sums = jnp.dot(windows, bands[group], preferred_element_type=F32)
        gain = coef[rows, 3 * span : 3 * span + 1]
        for block in range(blocks):
            lanes = slice(block * taps, (block + 1) * taps)
            out[rows, lanes] = sums[block * size : (block + 1) * size] + gain * gated[
                rows, lanes
            ].astype(F32)


def long_filter_part(span, k, v, k_rim, v_rim, before, coefficients, bands):
    width, rows = k.shape
    groups, reach, taps = bands.shape
    tile, part = min(128, width), rows // 2
    cell = lambda size: pl.BlockSpec((tile, size), lambda i, t: (i, t))
    return pl.pallas_call(
        functools.partial(filter_kernel, span),
        out_shape=jax.ShapeDtypeStruct((width, rows), F32),
        grid=(width // tile, 2),
        in_specs=[cell(part), cell(part), cell(taps), cell(taps), cell(taps)]
        + [
            pl.BlockSpec((tile, coefficients.shape[1]), lambda i, t: (i, 0)),
            pl.BlockSpec((groups * tile // width, reach, taps), lambda i, t: (i, 0, 0)),
        ],
        out_specs=cell(part),
        compiler_params=pltpu.CompilerParams(vmem_limit_bytes=VMEM_LIMIT),
        cost_estimate=pl.CostEstimate(
            flops=2 * width * rows * (reach + 4 * span),
            bytes_accessed=8 * width * rows + 2 * groups * reach * taps,
            transcendentals=0,
        ),
    )(k, v, k_rim, v_rim, before, coefficients, bands)


def mix_kernel(span, q, q_rim, filtered, coefficients, out):
    features = featurize(q_rim[...], q[...], coefficients[...], 0, span)
    out[...] = (features * filtered[...]).T.astype(BF16)


def mix(span, q, q_rim, filtered, coefficients):
    width, rows = q.shape
    tile, part = min(128, width), rows // 2
    cell = lambda size: pl.BlockSpec((tile, size), lambda i, t: (i, t))
    return pl.pallas_call(
        functools.partial(mix_kernel, span),
        out_shape=jax.ShapeDtypeStruct((rows, width), BF16),
        grid=(width // tile, 2),
        in_specs=[
            cell(part),
            cell(q_rim.shape[1] // 2),
            cell(part),
            pl.BlockSpec((tile, coefficients.shape[1]), lambda i, t: (i, 0)),
        ],
        out_specs=pl.BlockSpec((part, tile), lambda i, t: (t, i)),
        compiler_params=pltpu.CompilerParams(vmem_limit_bytes=VMEM_LIMIT),
        cost_estimate=pl.CostEstimate(
            flops=2 * width * rows * span, bytes_accessed=8 * width * rows, transcendentals=0
        ),
    )(q, q_rim, filtered, coefficients)


def output_kernel(count, order, *refs):
    mixed, stacks, out = refs[:count], refs[count:-1], refs[-1]
    left = jnp.concatenate([ref[...] for ref in mixed], axis=1)
    width = stacks[0].shape[2]
    place = 0
    for stack in stacks:
        pieces = [stack[index] for index in range(stack.shape[0])]
        sums = jnp.dot(left, jnp.concatenate(pieces, axis=1), preferred_element_type=F32)
        for index in range(stack.shape[0]):
            out[order[place]] = sums[:, index * width : (index + 1) * width].astype(out.dtype)
            place += 1


def output_sums(order, mixed, stacks, c, width):
    rows, part = mixed[0].shape
    count, depth, _ = stacks[0].shape
    blocks = count * len(stacks)
    tile = min(256, rows)
    return pl.pallas_call(
        functools.partial(output_kernel, len(mixed)),
        out_shape=jax.ShapeDtypeStruct((blocks, rows, width), BF16),
        grid_spec=pltpu.PrefetchScalarGridSpec(
            num_scalar_prefetch=1,
            grid=(rows // tile,),
            in_specs=[pl.BlockSpec((tile, part), lambda i, o: (i, 0))] * len(mixed)
            + [pl.BlockSpec((count, depth, width), lambda i, o: (0, 0, c))] * len(stacks),
            out_specs=pl.BlockSpec((blocks, tile, width), lambda i, o: (0, i, 0)),
        ),
        compiler_params=pltpu.CompilerParams(vmem_limit_bytes=VMEM_LIMIT),
        cost_estimate=pl.CostEstimate(
            flops=2 * rows * depth * blocks * width,
            bytes_accessed=2 * (rows * depth + depth * blocks * width + rows * blocks * width),
            transcendentals=0,
        ),
    )(order, *mixed, *stacks)


def bands_of(filters):
    taps = filters.shape[1]
    source = jnp.arange(taps)[:, None]
    target = jnp.arange(taps)[None, :]
    distance = (target - source) % taps
    picker = (distance[None] == jnp.arange(taps)[:, None, None]).astype(BF16)
    full = jnp.einsum("gk,kji->gji", filters, picker, preferred_element_type=F32)
    same = target >= source
    before, current = jnp.where(same, 0.0, full), jnp.where(same, full, 0.0)
    return jnp.concatenate([before, current], axis=1).astype(BF16)


def tail_gate(k, v, taps_k, taps_v, reach, end):
    span = taps_k.shape[0]

    def features(value, taps):
        wide = value[:, end - reach - span + 1 : end].astype(F32)
        total = taps[0][:, None] * wide[:, span - 1 :]
        for offset in range(1, span):
            start = span - 1 - offset
            total = total + taps[offset][:, None] * wide[:, start : start + reach]
        return total

    return (features(k, taps_k) * features(v, taps_v)).astype(BF16)


def pick(value, index, axis):
    return lax.dynamic_index_in_dim(value, index, axis, keepdims=False)


def per_device(
    places, tokens, qkv_weight, short_filter, long_filter, decay_rate, skip_gain, out_weight
):
    rows, in_features = tokens.shape
    depth, width = qkv_weight.shape[1:]
    features = out_weight.shape[1]
    groups, taps = long_filter.shape
    span = short_filter.shape[1]
    ny, nx, nz = places.ny, places.nx, places.nz
    i, j = lax.axis_index("ctx"), lax.axis_index("tp")
    x, zl = i % nx, (i // nx) % 2
    y, core = j // 2, j % 2
    half = width // 2
    share = features // 2
    chunks = 2 if share >= 256 else 1
    chunk = share // chunks
    order = jnp.stack([(i - x + step) ^ m for step in range(nx) for m in places.masks()])
    order = order.astype(jnp.int32)
    flags = jnp.stack([zl, j]).astype(jnp.int32)
    line = Line(places)

    def halves(s):
        return [
            lax.dynamic_slice_in_dim(qkv_weight[s], part * half, half, 1).T
            for part in (zl, 1 - zl)
        ]

    size = in_features // places.tp
    parts = {0: places.flip(lax.dynamic_slice_in_dim(tokens, j * size, size, 1), ctx=nx)}
    k_held = line.gather(*halves(1), parts[0])
    for step in range(1, ny):
        parts[2 * step] = places.flip(parts[0], tp=2 * step)
    pieces = {1: line.cross(k_held)}
    v_held = line.gather(*halves(2), *parts.values())
    for mask in list(parts):
        parts[mask ^ 1] = places.flip(parts[mask], tp=1)
    pieces[2] = line.cross(v_held)
    q_held = line.gather(*halves(0), *parts.values())
    pieces[0] = line.cross(q_held)
    tokens = prepare(
        order, flags, tokens, [parts[mask] for mask in range(places.tp)], depth
    )

    out_halves = out_weight.reshape(width, 2, share)
    rows_of = [pick(out_halves, core, 1), places.flip(pick(out_halves, 1 - core, 1), tp=1)]
    both = jnp.stack(rows_of).reshape(2, 2, half, share)
    out_own, out_other = (pick(both, part, 1).reshape(width, share) for part in (zl, 1 - zl))
    out_held = line.gather(out_own, out_other)

    tap_index = jnp.arange(taps, dtype=F32)
    filters = (long_filter * jnp.exp(-decay_rate[:, None] * tap_index[None, :])).astype(BF16)
    bands = bands_of(lax.dynamic_slice_in_dim(filters, zl * (groups // 2), groups // 2))
    short = lax.dynamic_slice_in_dim(short_filter, zl * half, half, 2)
    gain = lax.dynamic_slice_in_dim(skip_gain, zl * half, half)
    coefficients = jnp.concatenate([short.reshape(3 * span, half), gain[None, :]]).T
    coefficients = jnp.pad(coefficients, ((0, 0), (0, (-3 * span - 1) % 8)))

    def halos(tails):
        beside = places.send(tails, lambda i, j: (i - i % nx + (i + 1) % nx, j))
        below = places.send(
            tails[1],
            lambda i, j: (i + 2 * nx - nx + 1, j)
            if i % nx == nx - 1 and i + 2 * nx < places.ctx
            else None,
        )
        start = x == 0
        return [jnp.where(start, below, beside[0]), jnp.where(start, beside[0], beside[1])]

    def rim_of(value):
        return jnp.pad(value.T, ((0, 0), (taps - value.shape[0], 0)))

    def rims(values):
        return jnp.concatenate([rim_of(value) for value in values], axis=1)

    edge = 8 * -(-(span - 1) // 8)
    ends = (rows, 2 * rows)
    k = project(tokens, pieces[1])
    u = project(tokens, pieces[2])
    outs = line.cross(out_held, k, u)
    tails = [
        jnp.concatenate(
            [
                tail_gate(k, u, short[1], short[2], taps, end).T,
                k[:, end - edge : end].T,
                u[:, end - edge : end].T,
            ]
        )
        for end in ends
    ]
    before = halos(jnp.stack(tails))
    filtered = long_filter_part(
        span,
        k,
        u,
        rims([value[taps : taps + edge] for value in before]),
        rims([value[taps + edge :] for value in before]),
        rims([value[:taps] for value in before]),
        coefficients,
        bands,
    )
    q = project(tokens, [after(stack, filtered) for stack in pieces[0]])
    before = halos(jnp.stack([q[:, end - edge : end].T for end in ends]))
    mixed = mix(span, q, rims(before), filtered, coefficients)
    mixed = [mixed, places.flip(mixed, tp=1)]

    def over_y(value):
        total = pick(value, y, 1).astype(F32)
        for step in range(1, ny):
            total = total + places.flip(pick(value, y ^ step, 1), tp=2 * step).astype(F32)
        return total.astype(BF16)

    def over_z(value):
        other = places.flip(pick(value, 1 - zl, 1), ctx=nx)
        return (pick(value, zl, 1).astype(F32) + other.astype(F32)).astype(BF16)

    results = []
    blocks = places.ctx
    part = rows // ny
    sums = None
    for c in range(chunks):
        sums = output_sums(after(order, sums), mixed, outs, c, chunk)
        if c + 1 < chunks or chunks == 1:
            value = sums.reshape(blocks * 2, ny, part, chunk)
            value = over_z(over_y(value).reshape(blocks, 2, part, chunk))
        else:
            value = over_z(sums.reshape(blocks, 2, rows, chunk))
            value = over_y(value.reshape(blocks, ny, part, chunk))
        value = value.reshape(blocks, 2, part // 2, chunk)
        mine = pick(value, core, 1)
        yours = places.flip(pick(value, 1 - core, 1), tp=1)
        pair = jnp.stack(
            [jnp.where(core == 0, mine, yours), jnp.where(core == 0, yours, mine)], axis=1
        )
        results.append(pair)
    result = jnp.stack(results, axis=2)
    return result.transpose(3, 0, 1, 2, 4).reshape(part // 2, -1)


def solution(mesh):
    in_specs = (
        P("ctx", None),
        P(None, "ctx", "tp"),
        P(None, None, "tp"),
        P("tp", None),
        P("tp"),
        P("tp"),
        P("tp", "ctx"),
    )
    places = Places(mesh.shape["ctx"], mesh.shape["tp"])
    return jax.shard_map(
        functools.partial(per_device, places),
        mesh=mesh,
        in_specs=in_specs,
        out_specs=P(AXES, None),
        check_vma=False,
    )
```

profile of v0, /device:TPU:17, one launch (start us, length us, event | category | flops | bytes accessed | tf_op | source)
XLA Modules:
  0.0 433.4 jit_solution(9933345778526440912)
XLA Ops:
  16.5 49.9 %collective-permute-done.refs_0_ = bf16[768,1024]{1,0:T(8,128)(2,1)} collective-permute-done((bf16[768,1024]{1,0:T(8,128)(2,1)}, bf16[768,1024]{1,0:T(8,128)(2,1)}, u32[]{:S(2)}, u32[]{:S(2)}) %collective-permute-start) | collective-permute-done | bytes 1572896 | tf_op jit(solution)/shard_map/ppermute | solution.py:29
  68.6 10.9 %collective-permute-done.4 = bf16[512,512]{1,0:T(8,128)(2,1)S(1)} collective-permute-done((bf16[512,512]{1,0:T(8,128)(2,1)}, bf16[512,512]{1,0:T(8,128)(2,1)S(1)}, u32[]{:S(2)}, u32[]{:S(2)}) %collective-permute-start.4) | collective-permute-done | bytes 524320 | tf_op jit(solution)/shard_map/ppermute | solution.py:29
  84.1 3.3 collective-permute-start.8
  87.3 29.0 %collective-permute-done.2.refs_2_ = bf16[768,1024]{1,0:T(8,128)(2,1)} collective-permute-done((bf16[768,1024]{1,0:T(8,128)(2,1)}, bf16[768,1024]{1,0:T(8,128)(2,1)}, u32[]{:S(2)}, u32[]{:S(2)}) %collective-permute-start.2) | collective-permute-done | bytes 1572896 | tf_op jit(solution)/shard_map/ppermute | solution.py:29
  118.6 9.9 %collective-permute-done.8 = bf16[512,512]{1,0:T(8,128)(2,1)S(1)} collective-permute-done((bf16[512,512]{1,0:T(8,128)(2,1)S(1)}, bf16[512,512]{1,0:T(8,128)(2,1)S(1)}, u32[]{:S(2)}, u32[]{:S(2)}) %collective-permute-start.8) | collective-permute-done | bytes 524320 | tf_op jit(solution)/shard_map/ppermute | solution.py:29
  128.5 9.6 %collective-permute-done.5 = bf16[512,512]{1,0:T(8,128)(2,1)S(1)} collective-permute-done((bf16[512,512]{1,0:T(8,128)(2,1)S(1)}, bf16[512,512]{1,0:T(8,128)(2,1)S(1)}, u32[]{:S(2)}, u32[]{:S(2)}) %collective-permute-start.5) | collective-permute-done | bytes 524320 | tf_op jit(solution)/shard_map/ppermute | solution.py:29
  145.5 4.3 collective-permute-start.9
  152.3 29.3 %collective-permute-done.12 = bf16[512,512]{1,0:T(8,128)(2,1)} collective-permute-done((bf16[512,512]{1,0:T(8,128)(2,1)S(1)}, bf16[512,512]{1,0:T(8,128)(2,1)}, u32[]{:S(2)}, u32[]{:S(2)}) %collective-permute-start.12) | collective-permute-done | bytes 524320 | tf_op jit(solution)/shard_map/ppermute | solution.py:29
  181.6 9.0 %collective-permute-done.9 = bf16[512,512]{1,0:T(8,128)(2,1)} collective-permute-done((bf16[512,512]{1,0:T(8,128)(2,1)S(1)}, bf16[512,512]{1,0:T(8,128)(2,1)}, u32[]{:S(2)}, u32[]{:S(2)}) %collective-permute-start.9) | collective-permute-done | bytes 524320 | tf_op jit(solution)/shard_map/ppermute | solution.py:29
  200.5 4.1 collective-permute-start.20
  204.6 14.1 %shard_map.73.tokens = bf16[4096,1536]{1,0:T(8,128)(2,1)} custom-call(s32[8]{0:T(128)} %stack.155.order, s32[2]{0:T(128)} %pad_add_fusion.flags, bf16[768,4096]{1,0:T(8,128)(2,1)} %own.1, bf16[768,1024]{1,0:T(8,128)(2,1)} %collective-permute-done.refs_0_, bf16[768,1024]{1,0:T(8,128)(2,1)} %collective-permute-done.1.refs_1_, ...), custom_call_target="tpu_custom_call" | custom-call | bytes 25165824 | tf_op jit(solution)/shard_map/pallas_call | solution.py:87
  218.7 13.3 %shard_map.74.k = bf16[512,1536]{1,0:T(8,128)(2,1)} custom-call(bf16[4096,1536]{1,0:T(8,128)(2,1)} %shard_map.73.tokens, bf16[8,512,512]{2,1,0:T(8,128)(2,1)} %all-gather.7.cloned.1.call-done.refs_0_), custom_call_target="tpu_custom_call" | custom-call | flops 6442450944 | bytes 22544384 | tf_op jit(solution)/shard_map/pallas_call | solution.py:116
  234.4 13.4 %shard_map.75.v = bf16[512,1536]{1,0:T(8,128)(2,1)} custom-call(bf16[4096,1536]{1,0:T(8,128)(2,1)} %shard_map.73.tokens, bf16[8,512,512]{2,1,0:T(8,128)(2,1)} %all-gather.9.cloned.1.call-done.refs_0_), custom_call_target="tpu_custom_call" | custom-call | flops 6442450944 | bytes 22544384 | tf_op jit(solution)/shard_map/pallas_call | solution.py:116
  260.7 5.9 %collective-permute-done.13 = bf16[144,512]{0,1:T(8,128)(2,1)S(1)} collective-permute-done((bf16[144,512]{0,1:T(8,128)(2,1)}, bf16[144,512]{0,1:T(8,128)(2,1)S(1)}, u32[]{:S(2)}, u32[]{:S(2)}) %collective-permute-start.13) | collective-permute-done | bytes 147488 | tf_op jit(solution)/shard_map/ppermute | solution.py:29
  266.5 8.1 %collective-permute-done.14 = bf16[2,144,512]{1,2,0:T(8,128)(2,1)S(1)} collective-permute-done((bf16[2,144,512]{1,2,0:T(8,128)(2,1)S(1)}, bf16[2,144,512]{1,2,0:T(8,128)(2,1)S(1)}, u32[]{:S(2)}, u32[]{:S(2)}) %collective-permute-start.14) | collective-permute-done | bytes 294944 | tf_op jit(solution)/shard_map/ppermute | solution.py:29
  277.4 14.1 %shard_map.76.filtered = f32[512,1536]{1,0:T(8,128)} custom-call(bf16[512,1536]{1,0:T(8,128)(2,1)} %shard_map.74.k, bf16[512,1536]{1,0:T(8,128)(2,1)} %shard_map.75.v, bf16[512,256]{1,0:T(8,128)(2,1)} %fusion.18.k_rim, bf16[512,256]{1,0:T(8,128)(2,1)} %fusion.19.v_rim, bf16[512,256]{1,0:T(8,128)(2,1)} %pad_maximum_fusion.7.before, ...), custom_call_target="tpu_custom_call" | custom-call | flops 446693376 | bytes 8388608 | tf_op jit(solution)/shard_map/pallas_call | solution.py:170
  291.5 13.3 %shard_map.77.q = bf16[512,1536]{1,0:T(8,128)(2,1)} custom-call(bf16[4096,1536]{1,0:T(8,128)(2,1)} %shard_map.73.tokens, bf16[8,512,512]{2,1,0:T(8,128)(2,1)} %all-gather.5.cloned.1.call-done.refs_0_), custom_call_target="tpu_custom_call" | custom-call | flops 6442450944 | bytes 22544384 | tf_op jit(solution)/shard_map/pallas_call | solution.py:116
  307.6 6.1 %collective-permute-done.15 = bf16[8,512]{0,1:T(8,128)(2,1)S(1)} collective-permute-done((bf16[8,512]{0,1:T(8,128)(2,1)S(1)}, bf16[8,512]{0,1:T(8,128)(2,1)S(1)}, u32[]{:S(2)}, u32[]{:S(2)}) %collective-permute-start.15) | collective-permute-done | bytes 8224 | tf_op jit(solution)/shard_map/ppermute | solution.py:29
  313.7 8.6 %collective-permute-done.16 = bf16[2,8,512]{1,2,0:T(8,128)(2,1)S(1)} collective-permute-done((bf16[2,8,512]{1,2,0:T(8,128)(2,1)S(1)}, bf16[2,8,512]{1,2,0:T(8,128)(2,1)S(1)}, u32[]{:S(2)}, u32[]{:S(2)}) %collective-permute-start.16) | collective-permute-done | bytes 16416 | tf_op jit(solution)/shard_map/ppermute | solution.py:29
  323.2 9.5 %shard_map.78.refs_0_ = bf16[1536,512]{1,0:T(8,128)(2,1)} custom-call(bf16[512,1536]{1,0:T(8,128)(2,1)} %shard_map.77.q, bf16[512,256]{1,0:T(8,128)(2,1)} %fusion.20.q_rim, f32[512,1536]{1,0:T(8,128)} %shard_map.76.filtered, f32[512,24]{1,0:T(8,128)} %pad.27.coefficients), custom_call_target="tpu_custom_call" | custom-call | flops 11010048 | bytes 6291456 | tf_op jit(solution)/shard_map/pallas_call | solution.py:198
  339.0 8.8 %shard_map.79 = bf16[8,1536,128]{2,1,0:T(8,128)(2,1)} custom-call(s32[8]{0:T(128)} %stack.155.order, bf16[1536,512]{1,0:T(8,128)(2,1)} %shard_map.78.refs_0_, bf16[1536,512]{1,0:T(8,128)(2,1)} %copy-done.4, bf16[8,1024,256]{2,1,0:T(8,128)(2,1)} %all-gather.11.cloned.1.call-done.refs_2_), custom_call_target="tpu_custom_call" | custom-call | flops 3221225472 | bytes 8388608 | tf_op jit(solution)/shard_map/pallas_call | solution.py:234
  347.7 8.8 %shard_map.80 = bf16[8,1536,128]{2,1,0:T(8,128)(2,1)} custom-call(s32[8]{0:T(128)} %stack.155.order, bf16[1536,512]{1,0:T(8,128)(2,1)} %shard_map.78.refs_0_, bf16[1536,512]{1,0:T(8,128)(2,1)} %copy-done.4, bf16[8,1024,256]{2,1,0:T(8,128)(2,1)} %all-gather.11.cloned.1.call-done.refs_2_), custom_call_target="tpu_custom_call" | custom-call | flops 3221225472 | bytes 8388608 | tf_op jit(solution)/shard_map/pallas_call | solution.py:234
  363.0 32.2 %collective-permute-done.25 = bf16[8,768,128]{2,1,0:T(8,128)(2,1)} collective-permute-done((bf16[8,768,128]{2,1,0:T(8,128)(2,1)}, bf16[8,768,128]{2,1,0:T(8,128)(2,1)}, u32[]{:S(2)}, u32[]{:S(2)}) %collective-permute-start.25) | collective-permute-done | bytes 1572896 | tf_op jit(solution)/shard_map/ppermute | solution.py:29
  402.1 13.5 %collective-permute-done.26 = bf16[8,384,128]{2,1,0:T(8,128)(2,1)S(1)} collective-permute-done((bf16[8,384,128]{2,1,0:T(8,128)(2,1)S(1)}, bf16[8,384,128]{2,1,0:T(8,128)(2,1)S(1)}, u32[]{:S(2)}, u32[]{:S(2)}) %collective-permute-start.26) | collective-permute-done | bytes 786464 | tf_op jit(solution)/shard_map/ppermute | solution.py:29
  (140 shorter events, 90.9 us)
Async XLA Ops:
  6.5 212.2 %all-gather.7.cloned.1.call-start = ((), (), s32[]{:S(2)}) async-start(), calls=%async_computation.1 | async-start | bytes 6291456 | tf_op jit(solution)/shard_map/all_gather | solution.py:68
  9.2 57.1 %collective-permute-start = (bf16[768,1024]{1,0:T(8,128)(2,1)}, bf16[768,1024]{1,0:T(8,128)(2,1)}, u32[]{:S(2)}, u32[]{:S(2)}) collective-permute-start(bf16[768,1024]{1,0:T(8,128)(2,1)} %constant_dynamic-slice_fusion.11), channel_id=1, source_target_pairs={{0,8},{1,9},{2,10},{3,11},{4,12},{5,13},{6,14},{7,15},{8,0},{9,1},... | collective-permute-start | bytes 4718600 | tf_op jit(solution)/shard_map/ppermute | solution.py:29
  13.9 54.6 %collective-permute-start.10 = (bf16[512,512]{1,0:T(8,128)(2,1)}, bf16[512,512]{1,0:T(8,128)(2,1)}, u32[]{:S(2)}, u32[]{:S(2)}) collective-permute-start(bf16[512,512]{1,0:T(8,128)(2,1)} %bitcast.222), channel_id=1, source_target_pairs={{0,24},{1,25},{2,26},{3,27},{4,28},{5,29},{6,30},{7,31},{8,16},{9,... | collective-permute-start | bytes 1572872 | tf_op jit(solution)/shard_map/ppermute | solution.py:29
  14.1 54.4 %collective-permute-start.7 = (bf16[512,512]{1,0:T(8,128)(2,1)S(1)}, bf16[512,512]{1,0:T(8,128)(2,1)S(1)}, u32[]{:S(2)}, u32[]{:S(2)}) collective-permute-start(bf16[512,512]{1,0:T(8,128)(2,1)S(1)} %bitcast.215), channel_id=1, source_target_pairs={{0,16},{1,17},{2,18},{3,19},{4,20},{5,21},{6,22},{7,23},{8,24},{9,... | collective-permute-start | bytes 1572872 | tf_op jit(solution)/shard_map/ppermute | solution.py:29
  82.2 152.2 %all-gather.9.cloned.1.call-start = ((), (), s32[]{:S(2)}) async-start(), calls=%async_computation.2 | async-start | bytes 6291456 | tf_op jit(solution)/shard_map/all_gather | solution.py:68
  82.2 34.1 %collective-permute-start.2 = (bf16[768,1024]{1,0:T(8,128)(2,1)}, bf16[768,1024]{1,0:T(8,128)(2,1)}, u32[]{:S(2)}, u32[]{:S(2)}) collective-permute-start(bf16[768,1024]{1,0:T(8,128)(2,1)} %collective-permute-done.refs_0_), channel_id=1, source_target_pairs={{0,2},{1,3},{2,0},{3,1},{4,6},{5,7},{6,4},{7,5},{8,10},{9,11},{10,... | collective-permute-start | bytes 4718600 | tf_op jit(solution)/shard_map/ppermute | solution.py:29
  84.0 34.6 %collective-permute-start.11 = (bf16[512,512]{1,0:T(8,128)(2,1)S(1)}, bf16[512,512]{1,0:T(8,128)(2,1)S(1)}, u32[]{:S(2)}, u32[]{:S(2)}) collective-permute-start(bf16[512,512]{1,0:T(8,128)(2,1)S(1)} %bitcast.224), channel_id=1, source_target_pairs={{0,24},{1,25},{2,26},{3,27},{4,28},{5,29},{6,30},{7,31},{8,16},{9,... | collective-permute-start | bytes 1572872 | tf_op jit(solution)/shard_map/ppermute | solution.py:29
  84.1 44.4 %collective-permute-start.8 = (bf16[512,512]{1,0:T(8,128)(2,1)S(1)}, bf16[512,512]{1,0:T(8,128)(2,1)S(1)}, u32[]{:S(2)}, u32[]{:S(2)}) collective-permute-start(bf16[512,512]{1,0:T(8,128)(2,1)S(1)} %bitcast.213), channel_id=1, source_target_pairs={{0,16},{1,17},{2,18},{3,19},{4,20},{5,21},{6,22},{7,23},{8,24},{9,... | collective-permute-start | bytes 1572872 | tf_op jit(solution)/shard_map/ppermute | solution.py:29
  116.3 21.8 %collective-permute-start.5 = (bf16[512,512]{1,0:T(8,128)(2,1)S(1)}, bf16[512,512]{1,0:T(8,128)(2,1)S(1)}, u32[]{:S(2)}, u32[]{:S(2)}) collective-permute-start(bf16[512,512]{1,0:T(8,128)(2,1)S(1)} %bitcast.225), channel_id=1, source_target_pairs={{0,8},{1,9},{2,10},{3,11},{4,12},{5,13},{6,14},{7,15},{8,0},{9,1},... | collective-permute-start | bytes 1572872 | tf_op jit(solution)/shard_map/ppermute | solution.py:29
  139.7 151.8 %all-gather.5.cloned.1.call-start = ((), (), s32[]{:S(2)}) async-start(), calls=%async_computation | async-start | bytes 6291456 | tf_op jit(solution)/shard_map/all_gather | solution.py:68
  143.9 55.0 %collective-permute-start.18 = (bf16[1024,256]{1,0:T(8,128)(2,1)}, bf16[1024,256]{1,0:T(8,128)(2,1)S(1)}, u32[]{:S(2)}, u32[]{:S(2)}) collective-permute-start(bf16[1024,256]{1,0:T(8,128)(2,1)} %bitcast.83), channel_id=1, source_target_pairs={{0,1},{1,0},{2,3},{3,2},{4,5},{5,4},{6,7},{7,6},{8,9},{9,8},{10,11... | collective-permute-start | bytes 1572872 | tf_op jit(solution)/shard_map/ppermute | solution.py:29
  145.4 36.2 %collective-permute-start.12 = (bf16[512,512]{1,0:T(8,128)(2,1)S(1)}, bf16[512,512]{1,0:T(8,128)(2,1)}, u32[]{:S(2)}, u32[]{:S(2)}) collective-permute-start(bf16[512,512]{1,0:T(8,128)(2,1)S(1)} %bitcast.220), channel_id=1, source_target_pairs={{0,24},{1,25},{2,26},{3,27},{4,28},{5,29},{6,30},{7,31},{8,16},{9,... | collective-permute-start | bytes 1572872 | tf_op jit(solution)/shard_map/ppermute | solution.py:29
  145.5 45.1 %collective-permute-start.9 = (bf16[512,512]{1,0:T(8,128)(2,1)S(1)}, bf16[512,512]{1,0:T(8,128)(2,1)}, u32[]{:S(2)}, u32[]{:S(2)}) collective-permute-start(bf16[512,512]{1,0:T(8,128)(2,1)S(1)} %bitcast.211), channel_id=1, source_target_pairs={{0,16},{1,17},{2,18},{3,19},{4,20},{5,21},{6,22},{7,23},{8,24},{9,... | collective-permute-start | bytes 1572872 | tf_op jit(solution)/shard_map/ppermute | solution.py:29
  149.8 40.8 %collective-permute-start.6 = (bf16[512,512]{1,0:T(8,128)(2,1)S(1)}, bf16[512,512]{1,0:T(8,128)(2,1)}, u32[]{:S(2)}, u32[]{:S(2)}) collective-permute-start(bf16[512,512]{1,0:T(8,128)(2,1)S(1)} %bitcast.221), channel_id=1, source_target_pairs={{0,8},{1,9},{2,10},{3,11},{4,12},{5,13},{6,14},{7,15},{8,0},{9,1},... | collective-permute-start | bytes 1572872 | tf_op jit(solution)/shard_map/ppermute | solution.py:29
  193.6 144.2 %all-gather.11.cloned.1.call-start = ((), (), s32[]{:S(2)}) async-start(), calls=%async_computation.3 | async-start | bytes 6291456 | tf_op jit(solution)/shard_map/all_gather | solution.py:68
  199.0 58.9 %collective-permute-start.21 = (bf16[1024,256]{1,0:T(8,128)(2,1)S(1)}, bf16[1024,256]{1,0:T(8,128)(2,1)S(1)}, u32[]{:S(2)}, u32[]{:S(2)}) collective-permute-start(bf16[1024,256]{1,0:T(8,128)(2,1)S(1)} %bitcast.227), channel_id=1, source_target_pairs={{0,24},{1,25},{2,26},{3,27},{4,28},{5,29},{6,30},{7,31},{8,16},{9,... | collective-permute-start | bytes 1572872 | tf_op jit(solution)/shard_map/ppermute | solution.py:29
  200.5 57.4 %collective-permute-start.20 = (bf16[1024,256]{1,0:T(8,128)(2,1)S(1)}, bf16[1024,256]{1,0:T(8,128)(2,1)S(1)}, u32[]{:S(2)}, u32[]{:S(2)}) collective-permute-start(bf16[1024,256]{1,0:T(8,128)(2,1)S(1)} %bitcast.217), channel_id=1, source_target_pairs={{0,16},{1,17},{2,18},{3,19},{4,20},{5,21},{6,22},{7,23},{8,24},{9,... | collective-permute-start | bytes 1572872 | tf_op jit(solution)/shard_map/ppermute | solution.py:29
  218.7 39.2 %collective-permute-start.19 = (bf16[1024,256]{1,0:T(8,128)(2,1)S(1)}, bf16[1024,256]{1,0:T(8,128)(2,1)}, u32[]{:S(2)}, u32[]{:S(2)}) collective-permute-start(bf16[1024,256]{1,0:T(8,128)(2,1)S(1)} %bitcast.228), channel_id=1, source_target_pairs={{0,8},{1,9},{2,10},{3,11},{4,12},{5,13},{6,14},{7,15},{8,0},{9,1},... | collective-permute-start | bytes 1572872 | tf_op jit(solution)/shard_map/ppermute | solution.py:29
  254.5 20.2 %collective-permute-start.14 = (bf16[2,144,512]{1,2,0:T(8,128)(2,1)S(1)}, bf16[2,144,512]{1,2,0:T(8,128)(2,1)S(1)}, u32[]{:S(2)}, u32[]{:S(2)}) collective-permute-start(bf16[2,144,512]{1,2,0:T(8,128)(2,1)S(1)} %pad_maximum_fusion.5), channel_id=1, source_target_pairs={{0,4},{1,5},{2,6},{3,7},{4,0},{5,1},{6,2},{7,3},{8,12},{9,13},{10,... | collective-permute-start | bytes 884744 | tf_op jit(solution)/shard_map/ppermute | solution.py:29
  306.0 16.4 %collective-permute-start.16 = (bf16[2,8,512]{1,2,0:T(8,128)(2,1)S(1)}, bf16[2,8,512]{1,2,0:T(8,128)(2,1)S(1)}, u32[]{:S(2)}, u32[]{:S(2)}) collective-permute-start(bf16[2,8,512]{1,2,0:T(8,128)(2,1)S(1)} %pad_maximum_fusion.8), channel_id=1, source_target_pairs={{0,4},{1,5},{2,6},{3,7},{4,0},{5,1},{6,2},{7,3},{8,12},{9,13},{10,... | collective-permute-start | bytes 49160 | tf_op jit(solution)/shard_map/ppermute | solution.py:29
  359.3 35.9 %collective-permute-start.25 = (bf16[8,768,128]{2,1,0:T(8,128)(2,1)}, bf16[8,768,128]{2,1,0:T(8,128)(2,1)}, u32[]{:S(2)}, u32[]{:S(2)}) collective-permute-start(bf16[8,768,128]{2,1,0:T(8,128)(2,1)} %dynamic-slice_bitcast_fusion), channel_id=1, source_target_pairs={{0,8},{1,9},{2,10},{3,11},{4,12},{5,13},{6,14},{7,15},{8,0},{9,1},... | collective-permute-start | bytes 4718600 | tf_op jit(solution)/shard_map/ppermute | solution.py:29
  361.7 37.2 %collective-permute-start.22 = (bf16[16,384,128]{2,1,0:T(8,128)(2,1)}, bf16[16,384,128]{2,1,0:T(8,128)(2,1)}, u32[]{:S(2)}, u32[]{:S(2)}) collective-permute-start(bf16[16,384,128]{2,1,0:T(8,128)(2,1)} %dynamic-slice_bitcast_fusion.1), channel_id=1, source_target_pairs={{0,2},{1,3},{2,0},{3,1},{4,6},{5,7},{6,4},{7,5},{8,10},{9,11},{10,... | collective-permute-start | bytes 4718600 | tf_op jit(solution)/shard_map/ppermute | solution.py:29
  397.6 17.9 %collective-permute-start.26 = (bf16[8,384,128]{2,1,0:T(8,128)(2,1)S(1)}, bf16[8,384,128]{2,1,0:T(8,128)(2,1)S(1)}, u32[]{:S(2)}, u32[]{:S(2)}) collective-permute-start(bf16[8,384,128]{2,1,0:T(8,128)(2,1)S(1)} %dynamic-slice_bitcast_fusion.2), channel_id=1, source_target_pairs={{0,2},{1,3},{2,0},{3,1},{4,6},{5,7},{6,4},{7,5},{8,10},{9,11},{10,... | collective-permute-start | bytes 2359304 | tf_op jit(solution)/shard_map/ppermute | solution.py:29
  400.8 17.6 %collective-permute-start.23 = (bf16[8,384,128]{2,1,0:T(8,128)(2,1)S(1)}, bf16[8,384,128]{2,1,0:T(8,128)(2,1)S(1)}, u32[]{:S(2)}, u32[]{:S(2)}) collective-permute-start(bf16[8,384,128]{2,1,0:T(8,128)(2,1)S(1)} %dynamic-slice_bitcast_fusion.3), channel_id=1, source_target_pairs={{0,8},{1,9},{2,10},{3,11},{4,12},{5,13},{6,14},{7,15},{8,0},{9,1},... | collective-permute-start | bytes 2359304 | tf_op jit(solution)/shard_map/ppermute | solution.py:29
  (15 other events, 86.9 us)
Sparse Core Ops, SparseCore 0:
  82.3 59.4 all-gather.6
  143.4 56.7 all-gather.8
  201.7 57.2 all-gather.4
  260.8 68.3 all-gather.10
where the time goes:
time: 435 us; the launch traced here: 433 us
  waiting for transfers between devices  228 us (52%)
  Pallas kernels  95.2 us (22%)
  starting transfers between devices  40.9 us (9%)
  other arithmetic  28.9 us (7%)
  local copies, waits for them, and re-layouts  24.3 us (6%)
  between operations  13.6 us (3%)
    ppermute x28, waiting for transfers between devices, send(): return lax.ppermute(value, AXES, pairs)  228 us
    ppermute x28, starting transfers between devices, send(): return lax.ppermute(value, AXES, pairs)  40.6 us
    pallas_call x3, Pallas kernels, project(): pl.pallas_call(project_kernel, out_shape=jax.ShapeDtypeStruct((width, row...  39.9 us
    pallas_call x2, Pallas kernels, output_sums(): pl.pallas_call(functools.partial(output_kernel, len(mixed)), out_shape=ja...  17.5 us
    pallas_call x1, Pallas kernels, prepare(): pl.pallas_call(functools.partial(prepare_kernel, per_part), out_shape=jax...  14.1 us
    pallas_call x1, Pallas kernels, long_filter_part(): pl.pallas_call(functools.partial(filter_kernel, span), out_shape=jax.Shap...  14.1 us
    another operation x4, other arithmetic, cross(): stack = after(jnp.stack([held[m] for m in range(nz)]), *done)  9.95 us
    pallas_call x1, Pallas kernels, mix(): pl.pallas_call(functools.partial(mix_kernel, span), out_shape=jax.ShapeDt...  9.49 us
  transfers between devices with their start and end apart: 32, of which 17 were waited for; matrix products, arithmetic and copies ran while one was open for 9% of the time, Pallas kernels for 18%

commit v1 on v0

--- a/solution.py
+++ b/solution.py
@@ -32,7 +32,7 @@
         return self.send(value, lambda i, j: (i ^ ctx, j ^ tp))
 
     def masks(self):
-        return [m * self.nx for m in range(self.nz)]
+        return [m * self.nx for m in range(1, self.nz)]
 
 
 def after(value, *done):
@@ -53,7 +53,7 @@
 
     def gather(self, own, other, *last):
         nx, nz = self.places.nx, self.places.nz
-        held = {0: own}
+        held = {}
         masks = sorted(range(1, nz), key=lambda m: (m < 2, m))
         for m in masks:
             held[m] = self.step(
@@ -61,11 +61,14 @@
             )
         return held
 
+    def beside(self, own):
+        return [self.places.flip(own, ctx=step) for step in range(1, self.places.nx)]
+
     def cross(self, held, *done):
         nx, nz = self.places.nx, self.places.nz
-        stack = after(jnp.stack([held[m] for m in range(nz)]), *done)
+        stack = after(jnp.stack([held[m] for m in range(1, nz)]), *done)
         groups = [[z * nx + x for x in range(nx)] for z in range(nz)]
-        return [lax.all_gather(stack, "ctx", axis_index_groups=groups, tiled=True)]
+        return lax.all_gather(stack, "ctx", axis_index_groups=groups, tiled=True)
 
 
 def prepare_kernel(per_part, order, flags, own, *refs):
@@ -109,16 +112,17 @@
     ).astype(out.dtype)
 
 
-def project(tokens, stacks):
+def project(tokens, entries):
     features, rows = tokens.shape
-    count, width, depth = stacks[0].shape
+    width, depth = entries[0][0].shape[1:]
     tile, part = min(256, width), rows // 2
+    cell = lambda block, count: pl.BlockSpec((count, tile, depth), lambda t, i: (block, i, 0))
     return pl.pallas_call(
         project_kernel,
         out_shape=jax.ShapeDtypeStruct((width, rows), BF16),
         grid=(2, width // tile),
         in_specs=[pl.BlockSpec((features, part), lambda t, i: (0, t))]
-        + [pl.BlockSpec((count, tile, depth), lambda t, i: (0, i, 0))] * len(stacks),
+        + [cell(block, count) for _, block, count in entries],
         out_specs=pl.BlockSpec((tile, part), lambda t, i: (i, t)),
         compiler_params=pltpu.CompilerParams(vmem_limit_bytes=VMEM_LIMIT),
         cost_estimate=pl.CostEstimate(
@@ -126,7 +130,7 @@
             bytes_accessed=2 * ((2 * width + rows) * features + width * rows),
             transcendentals=0,
         ),
-    )(tokens, *stacks)
+    )(tokens, *[stack for stack, _, _ in entries])
 
 
 def featurize(rim, value, coefficients, first, span):
@@ -213,38 +217,37 @@
     )(q, q_rim, filtered, coefficients)
 
 
-def output_kernel(count, order, *refs):
-    mixed, stacks, out = refs[:count], refs[count:-1], refs[-1]
+def output_kernel(count, chunks, order, *refs):
+    mixed, stacks, outs = refs[:count], refs[count:-chunks], refs[-chunks:]
     left = jnp.concatenate([ref[...] for ref in mixed], axis=1)
-    width = stacks[0].shape[2]
-    place = 0
-    for stack in stacks:
-        pieces = [stack[index] for index in range(stack.shape[0])]
-        sums = jnp.dot(left, jnp.concatenate(pieces, axis=1), preferred_element_type=F32)
-        for index in range(stack.shape[0]):
-            out[order[place]] = sums[:, index * width : (index + 1) * width].astype(out.dtype)
-            place += 1
-
-
-def output_sums(order, mixed, stacks, c, width):
+    pieces = [stack[index] for stack in stacks for index in range(stack.shape[0])]
+    width = outs[0].shape[2]
+    for place, piece in enumerate(pieces):
+        sums = jnp.dot(left, piece, preferred_element_type=F32)
+        for c, out in enumerate(outs):
+            out[order[place]] = sums[:, c * width : (c + 1) * width].astype(out.dtype)
+
+
+def output_sums(order, mixed, stacks, chunks):
     rows, part = mixed[0].shape
-    count, depth, _ = stacks[0].shape
-    blocks = count * len(stacks)
+    depth, share = stacks[0].shape[1:]
+    width = share // chunks
+    blocks = sum(stack.shape[0] for stack in stacks)
     tile = min(256, rows)
     return pl.pallas_call(
-        functools.partial(output_kernel, len(mixed)),
-        out_shape=jax.ShapeDtypeStruct((blocks, rows, width), BF16),
+        functools.partial(output_kernel, len(mixed), chunks),
+        out_shape=[jax.ShapeDtypeStruct((blocks, rows, width), BF16)] * chunks,
         grid_spec=pltpu.PrefetchScalarGridSpec(
             num_scalar_prefetch=1,
             grid=(rows // tile,),
             in_specs=[pl.BlockSpec((tile, part), lambda i, o: (i, 0))] * len(mixed)
-            + [pl.BlockSpec((count, depth, width), lambda i, o: (0, 0, c))] * len(stacks),
-            out_specs=pl.BlockSpec((blocks, tile, width), lambda i, o: (0, i, 0)),
+            + [pl.BlockSpec(stack.shape, lambda i, o: (0, 0, 0)) for stack in stacks],
+            out_specs=[pl.BlockSpec((blocks, tile, width), lambda i, o: (0, i, 0))] * chunks,
         ),
         compiler_params=pltpu.CompilerParams(vmem_limit_bytes=VMEM_LIMIT),
         cost_estimate=pl.CostEstimate(
-            flops=2 * rows * depth * blocks * width,
-            bytes_accessed=2 * (rows * depth + depth * blocks * width + rows * blocks * width),
+            flops=2 * rows * depth * blocks * share,
+            bytes_accessed=2 * (rows * depth + depth * blocks * share + rows * blocks * share),
             transcendentals=0,
         ),
     )(order, *mixed, *stacks)
@@ -296,8 +299,9 @@
     share = features // 2
     chunks = 2 if share >= 256 else 1
     chunk = share // chunks
-    order = jnp.stack([(i - x + step) ^ m for step in range(nx) for m in places.masks()])
-    order = order.astype(jnp.int32)
+    order = [i ^ step for step in range(nx)]
+    order += [(i - x + step) ^ m for step in range(nx) for m in places.masks()]
+    order = jnp.stack(order).astype(jnp.int32)
     flags = jnp.stack([zl, j]).astype(jnp.int32)
     line = Line(places)
 
@@ -307,27 +311,41 @@
             for part in (zl, 1 - zl)
         ]
 
+    q_parts, k_parts, v_parts = (halves(s) for s in range(3))
+    own = jnp.stack([q_parts[0], k_parts[0], v_parts[0]])
+    beside = line.beside(own)
+
     size = in_features // places.tp
     parts = {0: places.flip(lax.dynamic_slice_in_dim(tokens, j * size, size, 1), ctx=nx)}
-    k_held = line.gather(*halves(1), parts[0])
+    k_held = line.gather(*k_parts, parts[0], *beside)
     for step in range(1, ny):
         parts[2 * step] = places.flip(parts[0], tp=2 * step)
-    pieces = {1: line.cross(k_held)}
-    v_held = line.gather(*halves(2), *parts.values())
-    for mask in list(parts):
-        parts[mask ^ 1] = places.flip(parts[mask], tp=1)
-    pieces[2] = line.cross(v_held)
-    q_held = line.gather(*halves(0), *parts.values())
-    pieces[0] = line.cross(q_held)
-    tokens = prepare(
-        order, flags, tokens, [parts[mask] for mask in range(places.tp)], depth
-    )
+    k_cross = line.cross(k_held)
 
     out_halves = out_weight.reshape(width, 2, share)
     rows_of = [pick(out_halves, core, 1), places.flip(pick(out_halves, 1 - core, 1), tp=1)]
     both = jnp.stack(rows_of).reshape(2, 2, half, share)
     out_own, out_other = (pick(both, part, 1).reshape(width, share) for part in (zl, 1 - zl))
-    out_held = line.gather(out_own, out_other)
+
+    v_held = line.gather(*v_parts, *parts.values())
+    for mask in list(parts):
+        parts[mask ^ 1] = places.flip(parts[mask], tp=1)
+    v_cross = line.cross(v_held)
+    tokens = prepare(
+        order, flags, tokens, [parts[mask] for mask in range(places.tp)], depth
+    )
+    q_held = line.gather(*q_parts, tokens)
+    q_cross = line.cross(q_held)
+    out_beside = line.beside(out_own)
+
+    def entries(s, crossed):
+        return [(stack, s, 1) for stack in [own] + beside] + [(crossed, 0, crossed.shape[0])]
+
+    k = project(tokens, entries(1, k_cross))
+    out_held = line.gather(out_own, out_other, k, *out_beside)
+    u = project(tokens, entries(2, v_cross))
+    outs = [stack[None] for stack in [out_own] + out_beside]
+    outs.append(line.cross(out_held, u))
 
     tap_index = jnp.arange(taps, dtype=F32)
     filters = (long_filter * jnp.exp(-decay_rate[:, None] * tap_index[None, :])).astype(BF16)
@@ -356,9 +374,6 @@
 
     edge = 8 * -(-(span - 1) // 8)
     ends = (rows, 2 * rows)
-    k = project(tokens, pieces[1])
-    u = project(tokens, pieces[2])
-    outs = line.cross(out_held, k, u)
     tails = [
         jnp.concatenate(
             [
@@ -380,7 +395,7 @@
         coefficients,
         bands,
     )
-    q = project(tokens, [after(stack, filtered) for stack in pieces[0]])
+    q = project(tokens, entries(0, after(q_cross, filtered, *out_held.values())))
     before = halos(jnp.stack([q[:, end - edge : end].T for end in ends]))
     mixed = mix(span, q, rims(before), filtered, coefficients)
     mixed = [mixed, places.flip(mixed, tp=1)]
@@ -398,9 +413,7 @@
     results = []
     blocks = places.ctx
     part = rows // ny
-    sums = None
-    for c in range(chunks):
-        sums = output_sums(after(order, sums), mixed, outs, c, chunk)
+    for c, sums in enumerate(output_sums(order, mixed, outs, chunks)):
         if c + 1 < chunks or chunks == 1:
             value = sums.reshape(blocks * 2, ny, part, chunk)
             value = over_z(over_y(value).reshape(blocks, 2, part, chunk))

time: 435 us -> 415 us (0.954)
  waiting for transfers between devices: 228 us -> 206 us
    ppermute x28 -> x30, waiting for transfers between devices: 228 us -> 206 us  [send(): return lax.ppermute(value, AXES, pairs)]
    pallas_call x2 -> x1, Pallas kernels: 17.5 us -> 12 us  [output_sums(): pl.pallas_call(functools.partial(output_kernel, len(mixed), chunks), out_...]
    ppermute x28 -> x30, starting transfers between devices: 40.6 us -> 43.3 us  [send(): return lax.ppermute(value, AXES, pairs)]
    another operation x5 -> x6, other arithmetic: 10.6 us -> 8.63 us  [the longest x4 6.58 us: cross(): stack = after(jnp.stack([held[m] for m in range(1, nz)]), *done)]
  transfers between devices with their start and end apart: 32 -> 34, of which waited for: 17 -> 16; matrix products, arithmetic and copies ran while one was open for 9% -> 11% of each run, Pallas kernels for 18% -> 19%
where the time goes in v1:
time: 415 us; the launch traced here: 413 us
  waiting for transfers between devices  206 us (50%)
  Pallas kernels  91.4 us (22%)
  starting transfers between devices  43.6 us (11%)
  local copies, waits for them, and re-layouts  28.4 us (7%)
  other arithmetic  28.1 us (7%)
  between operations  13.6 us (3%)
    ppermute x30, waiting for transfers between devices, send(): return lax.ppermute(value, AXES, pairs)  206 us
    ppermute x30, starting transfers between devices, send(): return lax.ppermute(value, AXES, pairs)  43.3 us
    pallas_call x3, Pallas kernels, project(): pl.pallas_call(project_kernel, out_shape=jax.ShapeDtypeStruct((width, row...  39.9 us
    pallas_call x1, Pallas kernels, prepare(): pl.pallas_call(functools.partial(prepare_kernel, per_part), out_shape=jax...  15.7 us
    pallas_call x1, Pallas kernels, long_filter_part(): pl.pallas_call(functools.partial(filter_kernel, span), out_shape=jax.Shap...  14.2 us
    pallas_call x1, Pallas kernels, output_sums(): pl.pallas_call(functools.partial(output_kernel, len(mixed), chunks), out_...  12 us
    pallas_call x1, Pallas kernels, mix(): pl.pallas_call(functools.partial(mix_kernel, span), out_shape=jax.ShapeDt...  9.51 us
  transfers between devices with their start and end apart: 34, of which 16 were waited for; matrix products, arithmetic and copies ran while one was open for 11% of the time, Pallas kernels for 19%

profile of v1, /device:TPU:17, one launch (start us, length us, event | category | flops | bytes accessed | tf_op | source)
XLA Modules:
  0.0 413.4 jit_solution(18417406557224929488)
XLA Ops:
  23.9 41.4 %collective-permute-done.refs_0_ = bf16[768,1024]{1,0:T(8,128)(2,1)} collective-permute-done((bf16[768,1024]{1,0:T(8,128)(2,1)}, bf16[768,1024]{1,0:T(8,128)(2,1)}, u32[]{:S(2)}, u32[]{:S(2)}) %collective-permute-start) | collective-permute-done | bytes 1572896 | tf_op jit(solution)/shard_map/ppermute | solution.py:29
  67.5 10.7 %collective-permute-done.5 = bf16[512,512]{1,0:T(8,128)(2,1)S(1)} collective-permute-done((bf16[512,512]{1,0:T(8,128)(2,1)S(1)}, bf16[512,512]{1,0:T(8,128)(2,1)S(1)}, u32[]{:S(2)}, u32[]{:S(2)}) %collective-permute-start.5) | collective-permute-done | bytes 524320 | tf_op jit(solution)/shard_map/ppermute | solution.py:29
  81.5 3.7 collective-permute-start.9
  85.2 28.5 %collective-permute-done.2.refs_2_ = bf16[768,1024]{1,0:T(8,128)(2,1)} collective-permute-done((bf16[768,1024]{1,0:T(8,128)(2,1)}, bf16[768,1024]{1,0:T(8,128)(2,1)}, u32[]{:S(2)}, u32[]{:S(2)}) %collective-permute-start.2) | collective-permute-done | bytes 1572896 | tf_op jit(solution)/shard_map/ppermute | solution.py:29
  115.7 9.3 %collective-permute-done.9 = bf16[512,512]{1,0:T(8,128)(2,1)S(1)} collective-permute-done((bf16[512,512]{1,0:T(8,128)(2,1)S(1)}, bf16[512,512]{1,0:T(8,128)(2,1)S(1)}, u32[]{:S(2)}, u32[]{:S(2)}) %collective-permute-start.9) | collective-permute-done | bytes 524320 | tf_op jit(solution)/shard_map/ppermute | solution.py:29
  125.0 10.8 %collective-permute-done.6 = bf16[512,512]{1,0:T(8,128)(2,1)S(1)} collective-permute-done((bf16[512,512]{1,0:T(8,128)(2,1)S(1)}, bf16[512,512]{1,0:T(8,128)(2,1)S(1)}, u32[]{:S(2)}, u32[]{:S(2)}) %collective-permute-start.6) | collective-permute-done | bytes 524320 | tf_op jit(solution)/shard_map/ppermute | solution.py:29
  146.7 3.9 collective-permute-start.10
  150.6 15.7 %shard_map.73.tokens = bf16[4096,1536]{1,0:T(8,128)(2,1)} custom-call(s32[8]{0:T(128)} %stack.158.order, s32[2]{0:T(128)} %pad_add_fusion.flags, bf16[768,4096]{1,0:T(8,128)(2,1)} %own.1, bf16[768,1024]{1,0:T(8,128)(2,1)} %collective-permute-done.refs_0_, bf16[768,1024]{1,0:T(8,128)(2,1)} %collective-permute-done.1.refs_1_, ...), custom_call_target="tpu_custom_call" | custom-call | bytes 25165824 | tf_op jit(solution)/shard_map/pallas_call | solution.py:90
  171.2 20.5 %collective-permute-done.10 = bf16[512,512]{1,0:T(8,128)(2,1)S(1)} collective-permute-done((bf16[512,512]{1,0:T(8,128)(2,1)S(1)}, bf16[512,512]{1,0:T(8,128)(2,1)S(1)}, u32[]{:S(2)}, u32[]{:S(2)}) %collective-permute-start.10) | collective-permute-done | bytes 524320 | tf_op jit(solution)/shard_map/ppermute | solution.py:29
  191.7 3.1 collective-permute-start.17
  197.5 13.5 %shard_map.74.k = bf16[512,1536]{1,0:T(8,128)(2,1)} custom-call(bf16[4096,1536]{1,0:T(8,128)(2,1)} %shard_map.73.tokens, bf16[3,512,512]{2,1,0:T(8,128)(2,1)} %pad_maximum_fusion.1.refs_0_, bf16[3,512,512]{2,1,0:T(8,128)(2,1)} %collective-permute-done.4.refs_1_, bf16[6,512,512]{2,1,0:T(8,128)(2,1)} %all-gather.7.cloned.1.call-done.refs_2_), custom_call_target="tpu_custom_call" | custom-call | flops 6442450944 | bytes 22544384 | tf_op jit(solution)/shard_map/pallas_call | solution.py:120
  213.6 13.2 %shard_map.75.v = bf16[512,1536]{1,0:T(8,128)(2,1)} custom-call(bf16[4096,1536]{1,0:T(8,128)(2,1)} %shard_map.73.tokens, bf16[3,512,512]{2,1,0:T(8,128)(2,1)} %pad_maximum_fusion.1.refs_0_, bf16[3,512,512]{2,1,0:T(8,128)(2,1)} %collective-permute-done.4.refs_1_, bf16[6,512,512]{2,1,0:T(8,128)(2,1)} %all-gather.9.cloned.1.call-done.refs_2_), custom_call_target="tpu_custom_call" | custom-call | flops 6442450944 | bytes 22544384 | tf_op jit(solution)/shard_map/pallas_call | solution.py:120
  238.2 2.9 collective-permute-done.18
  246.5 13.8 %collective-permute-done.15 = bf16[2,144,512]{1,2,0:T(8,128)(2,1)S(1)} collective-permute-done((bf16[2,144,512]{1,2,0:T(8,128)(2,1)S(1)}, bf16[2,144,512]{1,2,0:T(8,128)(2,1)S(1)}, u32[]{:S(2)}, u32[]{:S(2)}) %collective-permute-start.15) | collective-permute-done | bytes 294944 | tf_op jit(solution)/shard_map/ppermute | solution.py:29
  263.0 14.2 %shard_map.76.filtered = f32[512,1536]{1,0:T(8,128)} custom-call(bf16[512,1536]{1,0:T(8,128)(2,1)} %shard_map.74.k, bf16[512,1536]{1,0:T(8,128)(2,1)} %shard_map.75.v, bf16[512,256]{1,0:T(8,128)(2,1)} %fusion.18.k_rim, bf16[512,256]{1,0:T(8,128)(2,1)} %fusion.19.v_rim, bf16[512,256]{1,0:T(8,128)(2,1)} %pad_maximum_fusion.8.before, ...), custom_call_target="tpu_custom_call" | custom-call | flops 446693376 | bytes 8388608 | tf_op jit(solution)/shard_map/pallas_call | solution.py:174
  277.2 13.2 %shard_map.77.q = bf16[512,1536]{1,0:T(8,128)(2,1)} custom-call(bf16[4096,1536]{1,0:T(8,128)(2,1)} %shard_map.73.tokens, bf16[3,512,512]{2,1,0:T(8,128)(2,1)} %pad_maximum_fusion.1.refs_0_, bf16[3,512,512]{2,1,0:T(8,128)(2,1)} %collective-permute-done.4.refs_1_, bf16[6,512,512]{2,1,0:T(8,128)(2,1)} %all-gather.5.cloned.1.call-done.refs_2_), custom_call_target="tpu_custom_call" | custom-call | flops 6442450944 | bytes 22544384 | tf_op jit(solution)/shard_map/pallas_call | solution.py:120
  293.2 6.1 %collective-permute-done.21 = bf16[8,512]{0,1:T(8,128)(2,1)S(1)} collective-permute-done((bf16[8,512]{0,1:T(8,128)(2,1)S(1)}, bf16[8,512]{0,1:T(8,128)(2,1)S(1)}, u32[]{:S(2)}, u32[]{:S(2)}) %collective-permute-start.21) | collective-permute-done | bytes 8224 | tf_op jit(solution)/shard_map/ppermute | solution.py:29
  299.4 8.7 %collective-permute-done.22 = bf16[2,8,512]{1,2,0:T(8,128)(2,1)S(1)} collective-permute-done((bf16[2,8,512]{1,2,0:T(8,128)(2,1)S(1)}, bf16[2,8,512]{1,2,0:T(8,128)(2,1)S(1)}, u32[]{:S(2)}, u32[]{:S(2)}) %collective-permute-start.22) | collective-permute-done | bytes 16416 | tf_op jit(solution)/shard_map/ppermute | solution.py:29
  308.9 9.5 %shard_map.78.refs_0_ = bf16[1536,512]{1,0:T(8,128)(2,1)} custom-call(bf16[512,1536]{1,0:T(8,128)(2,1)} %shard_map.77.q, bf16[512,256]{1,0:T(8,128)(2,1)} %fusion.20.q_rim, f32[512,1536]{1,0:T(8,128)} %shard_map.76.filtered, f32[512,24]{1,0:T(8,128)} %pad.27.coefficients), custom_call_target="tpu_custom_call" | custom-call | flops 11010048 | bytes 6291456 | tf_op jit(solution)/shard_map/pallas_call | solution.py:202
  320.2 3.2 collective-permute-done.23.refs_1_
  324.5 12.0 %shard_map.79 = (bf16[8,1536,128]{2,1,0:T(8,128)(2,1)}, bf16[8,1536,128]{2,1,0:T(8,128)(2,1)}) custom-call(s32[8]{0:T(128)} %stack.158.order, bf16[1536,512]{1,0:T(8,128)(2,1)} %shard_map.78.refs_0_, bf16[1536,512]{1,0:T(8,128)(2,1)} %copy-done.7, bf16[1,1024,256]{2,1,0:T(8,128)(2,1)} %bitcast.227, bf16[1,1024,256]{2,1,0:T(8,128)(2,1)} %bitcast.267, ...), custom_call_target="tpu_custom_call" | custom-call | flops 6442450944 | bytes 13631488 | tf_op jit(solution)/shard_map/pallas_call | solution.py:237
  336.6 2.8 dynamic-slice_bitcast_fusion
  343.0 32.3 %collective-permute-done.27 = bf16[8,768,128]{2,1,0:T(8,128)(2,1)} collective-permute-done((bf16[8,768,128]{2,1,0:T(8,128)(2,1)}, bf16[8,768,128]{2,1,0:T(8,128)(2,1)}, u32[]{:S(2)}, u32[]{:S(2)}) %collective-permute-start.27) | collective-permute-done | bytes 1572896 | tf_op jit(solution)/shard_map/ppermute | solution.py:29
  382.1 13.5 %collective-permute-done.28 = bf16[8,384,128]{2,1,0:T(8,128)(2,1)S(1)} collective-permute-done((bf16[8,384,128]{2,1,0:T(8,128)(2,1)S(1)}, bf16[8,384,128]{2,1,0:T(8,128)(2,1)S(1)}, u32[]{:S(2)}, u32[]{:S(2)}) %collective-permute-start.28) | collective-permute-done | bytes 786464 | tf_op jit(solution)/shard_map/ppermute | solution.py:29
  (152 shorter events, 93.1 us)
Async XLA Ops:
  6.5 191.0 %all-gather.7.cloned.1.call-start = ((), (), s32[]{:S(2)}) async-start(), calls=%async_computation.1 | async-start | bytes 4718592 | tf_op jit(solution)/shard_map/all_gather | solution.py:71
  9.2 56.1 %collective-permute-start = (bf16[768,1024]{1,0:T(8,128)(2,1)}, bf16[768,1024]{1,0:T(8,128)(2,1)}, u32[]{:S(2)}, u32[]{:S(2)}) collective-permute-start(bf16[768,1024]{1,0:T(8,128)(2,1)} %constant_dynamic-slice_fusion.11), channel_id=1, source_target_pairs={{0,8},{1,9},{2,10},{3,11},{4,12},{5,13},{6,14},{7,15},{8,0},{9,1},... | collective-permute-start | bytes 4718600 | tf_op jit(solution)/shard_map/ppermute | solution.py:29
  20.2 45.1 %collective-permute-start.4 = (bf16[3,512,512]{2,1,0:T(8,128)(2,1)}, bf16[3,512,512]{2,1,0:T(8,128)(2,1)}, u32[]{:S(2)}, u32[]{:S(2)}) collective-permute-start(bf16[3,512,512]{2,1,0:T(8,128)(2,1)} %pad_maximum_fusion.1.refs_0_), channel_id=1, source_target_pairs={{0,4},{1,5},{2,6},{3,7},{4,0},{5,1},{6,2},{7,3},{8,12},{9,13},{10,... | collective-permute-start | bytes 4718600 | tf_op jit(solution)/shard_map/ppermute | solution.py:29
  21.6 45.9 %collective-permute-start.11 = (bf16[512,512]{1,0:T(8,128)(2,1)S(1)}, bf16[512,512]{1,0:T(8,128)(2,1)S(1)}, u32[]{:S(2)}, u32[]{:S(2)}) collective-permute-start(bf16[512,512]{1,0:T(8,128)(2,1)S(1)} %bitcast.221), channel_id=1, source_target_pairs={{0,24},{1,25},{2,26},{3,27},{4,28},{5,29},{6,30},{7,31},{8,16},{9,... | collective-permute-start | bytes 1572872 | tf_op jit(solution)/shard_map/ppermute | solution.py:29
  21.7 45.8 %collective-permute-start.8 = (bf16[512,512]{1,0:T(8,128)(2,1)S(1)}, bf16[512,512]{1,0:T(8,128)(2,1)S(1)}, u32[]{:S(2)}, u32[]{:S(2)}) collective-permute-start(bf16[512,512]{1,0:T(8,128)(2,1)S(1)} %bitcast.217), channel_id=1, source_target_pairs={{0,16},{1,17},{2,18},{3,19},{4,20},{5,21},{6,22},{7,23},{8,24},{9,... | collective-permute-start | bytes 1572872 | tf_op jit(solution)/shard_map/ppermute | solution.py:29
  79.6 134.0 %all-gather.9.cloned.1.call-start = ((), (), s32[]{:S(2)}) async-start(), calls=%async_computation.2 | async-start | bytes 4718592 | tf_op jit(solution)/shard_map/all_gather | solution.py:71
  79.6 34.1 %collective-permute-start.2 = (bf16[768,1024]{1,0:T(8,128)(2,1)}, bf16[768,1024]{1,0:T(8,128)(2,1)}, u32[]{:S(2)}, u32[]{:S(2)}) collective-permute-start(bf16[768,1024]{1,0:T(8,128)(2,1)} %collective-permute-done.refs_0_), channel_id=1, source_target_pairs={{0,2},{1,3},{2,0},{3,1},{4,6},{5,7},{6,4},{7,5},{8,10},{9,11},{10,... | collective-permute-start | bytes 4718600 | tf_op jit(solution)/shard_map/ppermute | solution.py:29
  81.1 34.5 %collective-permute-start.12 = (bf16[512,512]{1,0:T(8,128)(2,1)S(1)}, bf16[512,512]{1,0:T(8,128)(2,1)S(1)}, u32[]{:S(2)}, u32[]{:S(2)}) collective-permute-start(bf16[512,512]{1,0:T(8,128)(2,1)S(1)} %bitcast.223), channel_id=1, source_target_pairs={{0,24},{1,25},{2,26},{3,27},{4,28},{5,29},{6,30},{7,31},{8,16},{9,... | collective-permute-start | bytes 1572872 | tf_op jit(solution)/shard_map/ppermute | solution.py:29
  81.5 43.5 %collective-permute-start.9 = (bf16[512,512]{1,0:T(8,128)(2,1)S(1)}, bf16[512,512]{1,0:T(8,128)(2,1)S(1)}, u32[]{:S(2)}, u32[]{:S(2)}) collective-permute-start(bf16[512,512]{1,0:T(8,128)(2,1)S(1)} %bitcast.214), channel_id=1, source_target_pairs={{0,16},{1,17},{2,18},{3,19},{4,20},{5,21},{6,22},{7,23},{8,24},{9,... | collective-permute-start | bytes 1572872 | tf_op jit(solution)/shard_map/ppermute | solution.py:29
  113.7 22.1 %collective-permute-start.6 = (bf16[512,512]{1,0:T(8,128)(2,1)S(1)}, bf16[512,512]{1,0:T(8,128)(2,1)S(1)}, u32[]{:S(2)}, u32[]{:S(2)}) collective-permute-start(bf16[512,512]{1,0:T(8,128)(2,1)S(1)} %bitcast.224), channel_id=1, source_target_pairs={{0,8},{1,9},{2,10},{3,11},{4,12},{5,13},{6,14},{7,15},{8,0},{9,1},... | collective-permute-start | bytes 1572872 | tf_op jit(solution)/shard_map/ppermute | solution.py:29
  137.2 140.1 %all-gather.5.cloned.1.call-start = ((), (), s32[]{:S(2)}) async-start(), calls=%async_computation | async-start | bytes 4718592 | tf_op jit(solution)/shard_map/all_gather | solution.py:71
  141.1 27.4 %collective-permute-start.16 = (bf16[1024,256]{1,0:T(8,128)(2,1)}, bf16[1024,256]{1,0:T(8,128)(2,1)}, u32[]{:S(2)}, u32[]{:S(2)}) collective-permute-start(bf16[1024,256]{1,0:T(8,128)(2,1)} %bitcast.75), channel_id=1, source_target_pairs={{0,1},{1,0},{2,3},{3,2},{4,5},{5,4},{6,7},{7,6},{8,9},{9,8},{10,11... | collective-permute-start | bytes 1572872 | tf_op jit(solution)/shard_map/ppermute | solution.py:29
  146.3 48.6 %collective-permute-start.13 = (bf16[512,512]{1,0:T(8,128)(2,1)S(1)}, bf16[512,512]{1,0:T(8,128)(2,1)S(1)}, u32[]{:S(2)}, u32[]{:S(2)}) collective-permute-start(bf16[512,512]{1,0:T(8,128)(2,1)S(1)} %bitcast.219), channel_id=1, source_target_pairs={{0,24},{1,25},{2,26},{3,27},{4,28},{5,29},{6,30},{7,31},{8,16},{9,... | collective-permute-start | bytes 1572872 | tf_op jit(solution)/shard_map/ppermute | solution.py:29
  146.7 45.0 %collective-permute-start.10 = (bf16[512,512]{1,0:T(8,128)(2,1)S(1)}, bf16[512,512]{1,0:T(8,128)(2,1)S(1)}, u32[]{:S(2)}, u32[]{:S(2)}) collective-permute-start(bf16[512,512]{1,0:T(8,128)(2,1)S(1)} %bitcast.212), channel_id=1, source_target_pairs={{0,16},{1,17},{2,18},{3,19},{4,20},{5,21},{6,22},{7,23},{8,24},{9,... | collective-permute-start | bytes 1572872 | tf_op jit(solution)/shard_map/ppermute | solution.py:29
  166.3 29.6 %collective-permute-start.7 = (bf16[512,512]{1,0:T(8,128)(2,1)S(1)}, bf16[512,512]{1,0:T(8,128)(2,1)S(1)}, u32[]{:S(2)}, u32[]{:S(2)}) collective-permute-start(bf16[512,512]{1,0:T(8,128)(2,1)S(1)} %bitcast.220), channel_id=1, source_target_pairs={{0,8},{1,9},{2,10},{3,11},{4,12},{5,13},{6,14},{7,15},{8,0},{9,1},... | collective-permute-start | bytes 1572872 | tf_op jit(solution)/shard_map/ppermute | solution.py:29
  170.5 40.5 %collective-permute-start.19 = (bf16[1024,256]{1,0:T(8,128)(2,1)S(1)}, bf16[1024,256]{1,0:T(8,128)(2,1)S(1)}, u32[]{:S(2)}, u32[]{:S(2)}) collective-permute-start(bf16[1024,256]{1,0:T(8,128)(2,1)S(1)} %bitcast.225), channel_id=1, source_target_pairs={{0,4},{1,5},{2,6},{3,7},{4,0},{5,1},{6,2},{7,3},{8,12},{9,13},{10,... | collective-permute-start | bytes 1572872 | tf_op jit(solution)/shard_map/ppermute | solution.py:29
  191.7 46.5 %collective-permute-start.17 = (bf16[1024,256]{1,0:T(8,128)(2,1)S(1)}, bf16[1024,256]{1,0:T(8,128)(2,1)}, u32[]{:S(2)}, u32[]{:S(2)}) collective-permute-start(bf16[1024,256]{1,0:T(8,128)(2,1)S(1)} %bitcast.226), channel_id=1, source_target_pairs={{0,16},{1,17},{2,18},{3,19},{4,20},{5,21},{6,22},{7,23},{8,24},{9,... | collective-permute-start | bytes 1572872 | tf_op jit(solution)/shard_map/ppermute | solution.py:29
  194.8 46.2 %collective-permute-start.18 = (bf16[1024,256]{1,0:T(8,128)(2,1)}, bf16[1024,256]{1,0:T(8,128)(2,1)}, u32[]{:S(2)}, u32[]{:S(2)}) collective-permute-start(bf16[1024,256]{1,0:T(8,128)(2,1)} %bitcast.78), channel_id=1, source_target_pairs={{0,24},{1,25},{2,26},{3,27},{4,28},{5,29},{6,30},{7,31},{8,16},{9,... | collective-permute-start | bytes 1572872 | tf_op jit(solution)/shard_map/ppermute | solution.py:29
  197.3 122.9 %all-gather.11.cloned.1.call-start = ((), (), s32[]{:S(2)}) async-start(), calls=%async_computation.3 | async-start | bytes 4718592 | tf_op jit(solution)/shard_map/all_gather | solution.py:71
  211.0 30.1 %collective-permute-start.20 = (bf16[1024,256]{1,0:T(8,128)(2,1)}, bf16[1024,256]{1,0:T(8,128)(2,1)S(1)}, u32[]{:S(2)}, u32[]{:S(2)}) collective-permute-start(bf16[1024,256]{1,0:T(8,128)(2,1)} %bitcast.78), channel_id=1, source_target_pairs={{0,8},{1,9},{2,10},{3,11},{4,12},{5,13},{6,14},{7,15},{8,0},{9,1},... | collective-permute-start | bytes 1572872 | tf_op jit(solution)/shard_map/ppermute | solution.py:29
  233.5 26.7 %collective-permute-start.15 = (bf16[2,144,512]{1,2,0:T(8,128)(2,1)S(1)}, bf16[2,144,512]{1,2,0:T(8,128)(2,1)S(1)}, u32[]{:S(2)}, u32[]{:S(2)}) collective-permute-start(bf16[2,144,512]{1,2,0:T(8,128)(2,1)S(1)} %pad_maximum_fusion.6), channel_id=1, source_target_pairs={{0,4},{1,5},{2,6},{3,7},{4,0},{5,1},{6,2},{7,3},{8,12},{9,13},{10,... | collective-permute-start | bytes 884744 | tf_op jit(solution)/shard_map/ppermute | solution.py:29
  339.4 35.9 %collective-permute-start.27 = (bf16[8,768,128]{2,1,0:T(8,128)(2,1)}, bf16[8,768,128]{2,1,0:T(8,128)(2,1)}, u32[]{:S(2)}, u32[]{:S(2)}) collective-permute-start(bf16[8,768,128]{2,1,0:T(8,128)(2,1)} %dynamic-slice_bitcast_fusion), channel_id=1, source_target_pairs={{0,8},{1,9},{2,10},{3,11},{4,12},{5,13},{6,14},{7,15},{8,0},{9,1},... | collective-permute-start | bytes 4718600 | tf_op jit(solution)/shard_map/ppermute | solution.py:29
  341.8 37.1 %collective-permute-start.24 = (bf16[16,384,128]{2,1,0:T(8,128)(2,1)}, bf16[16,384,128]{2,1,0:T(8,128)(2,1)}, u32[]{:S(2)}, u32[]{:S(2)}) collective-permute-start(bf16[16,384,128]{2,1,0:T(8,128)(2,1)} %dynamic-slice_bitcast_fusion.1), channel_id=1, source_target_pairs={{0,2},{1,3},{2,0},{3,1},{4,6},{5,7},{6,4},{7,5},{8,10},{9,11},{10,... | collective-permute-start | bytes 4718600 | tf_op jit(solution)/shard_map/ppermute | solution.py:29
  377.7 17.9 %collective-permute-start.28 = (bf16[8,384,128]{2,1,0:T(8,128)(2,1)S(1)}, bf16[8,384,128]{2,1,0:T(8,128)(2,1)S(1)}, u32[]{:S(2)}, u32[]{:S(2)}) collective-permute-start(bf16[8,384,128]{2,1,0:T(8,128)(2,1)S(1)} %dynamic-slice_bitcast_fusion.2), channel_id=1, source_target_pairs={{0,2},{1,3},{2,0},{3,1},{4,6},{5,7},{6,4},{7,5},{8,10},{9,11},{10,... | collective-permute-start | bytes 2359304 | tf_op jit(solution)/shard_map/ppermute | solution.py:29
  (21 other events, 166.6 us)
Sparse Core Ops, SparseCore 0:
  79.7 48.6 all-gather.6
  137.3 60.1 all-gather.8
  199.0 56.5 all-gather.4
  257.1 53.7 all-gather.10

commit v2 on v1

--- a/solution.py
+++ b/solution.py
@@ -74,11 +74,12 @@
 def prepare_kernel(per_part, order, flags, own, *refs):
     parts, out = refs[:-1], refs[-1]
     part = order[pl.program_id(0)] // per_part
+    quarter, which = part // 2, part % 2
     rows = own.shape[0]
     out[:, pl.ds(pl.multiple_of(flags[0] * rows, rows), rows)] = own[...].T
-    for mask, ref in enumerate(parts):
-
-        @pl.when(part == flags[1] ^ mask)
+    for index, ref in enumerate(parts):
+
+        @pl.when((quarter == flags[1] ^ (index // 2)) & (which == index % 2))
         def _():
             out[:, pl.ds(pl.multiple_of((1 - flags[0]) * rows, rows), rows)] = ref[...].T
 
@@ -316,10 +317,18 @@
     beside = line.beside(own)
 
     size = in_features // places.tp
-    parts = {0: places.flip(lax.dynamic_slice_in_dim(tokens, j * size, size, 1), ctx=nx)}
-    k_held = line.gather(*k_parts, parts[0], *beside)
-    for step in range(1, ny):
-        parts[2 * step] = places.flip(parts[0], tp=2 * step)
+    parts = [
+        {
+            0: places.flip(
+                lax.dynamic_slice_in_dim(tokens, j * size + h * (size // 2), size // 2, 1), ctx=nx
+            )
+        }
+        for h in range(2)
+    ]
+    k_held = line.gather(*k_parts, parts[0][0], *beside)
+    for part in parts:
+        for step in range(1, ny):
+            part[2 * step] = places.flip(part[0], tp=2 * step)
     k_cross = line.cross(k_held)
 
     out_halves = out_weight.reshape(width, 2, share)
@@ -327,12 +336,17 @@
     both = jnp.stack(rows_of).reshape(2, 2, half, share)
     out_own, out_other = (pick(both, part, 1).reshape(width, share) for part in (zl, 1 - zl))
 
-    v_held = line.gather(*v_parts, *parts.values())
-    for mask in list(parts):
-        parts[mask ^ 1] = places.flip(parts[mask], tp=1)
+    v_held = line.gather(*v_parts, parts[1][0], *parts[0].values())
+    for part in parts:
+        for mask in list(part):
+            part[mask ^ 1] = places.flip(part[mask], tp=1)
     v_cross = line.cross(v_held)
     tokens = prepare(
-        order, flags, tokens, [parts[mask] for mask in range(places.tp)], depth
+        order,
+        flags,
+        tokens,
+        [part[mask] for mask in range(places.tp) for part in parts],
+        depth,
     )
     q_held = line.gather(*q_parts, tokens)
     q_cross = line.cross(q_held)
@@ -385,6 +399,8 @@
         for end in ends
     ]
     before = halos(jnp.stack(tails))
+    q = project(tokens, entries(0, after(q_cross, *out_held.values())))
+    edges = halos(jnp.stack([q[:, end - edge : end].T for end in ends]))
     filtered = long_filter_part(
         span,
         k,
@@ -392,12 +408,10 @@
         rims([value[taps : taps + edge] for value in before]),
         rims([value[taps + edge :] for value in before]),
         rims([value[:taps] for value in before]),
-        coefficients,
+        after(coefficients, q),
         bands,
     )
-    q = project(tokens, entries(0, after(q_cross, filtered, *out_held.values())))
-    before = halos(jnp.stack([q[:, end - edge : end].T for end in ends]))
-    mixed = mix(span, q, rims(before), filtered, coefficients)
+    mixed = mix(span, q, rims(edges), filtered, coefficients)
     mixed = [mixed, places.flip(mixed, tp=1)]
 
     def over_y(value):

time: 415 us -> 411 us (level)
  waiting for transfers between devices: 206 us -> 194 us
    ppermute x30 -> x34, waiting for transfers between devices: 206 us -> 194 us  [send(): return lax.ppermute(value, AXES, pairs)]
    ppermute x30 -> x34, starting transfers between devices: 43.3 us -> 46 us  [send(): return lax.ppermute(value, AXES, pairs)]
  transfers between devices with their start and end apart: 34 -> 38, of which waited for: 16 -> 17; matrix products, arithmetic and copies ran while one was open for 11% -> 11% of each run, Pallas kernels for 19% -> 19%
where the time goes in v2:
time: 411 us; the launch traced here: 407 us
  waiting for transfers between devices  194 us (47%)
  Pallas kernels  90.3 us (22%)
  starting transfers between devices  46.4 us (11%)
  local copies, waits for them, and re-layouts  32.4 us (8%)
  other arithmetic  28 us (7%)
  between operations  13.7 us (3%)
    ppermute x34, waiting for transfers between devices, send(): return lax.ppermute(value, AXES, pairs)  194 us
    ppermute x34, starting transfers between devices, send(): return lax.ppermute(value, AXES, pairs)  46 us
    pallas_call x3, Pallas kernels, project(): pl.pallas_call(project_kernel, out_shape=jax.ShapeDtypeStruct((width, row...  41.3 us
    pallas_call x1, Pallas kernels, long_filter_part(): pl.pallas_call(functools.partial(filter_kernel, span), out_shape=jax.Shap...  14.1 us
    pallas_call x1, Pallas kernels, prepare(): pl.pallas_call(functools.partial(prepare_kernel, per_part), out_shape=jax...  13.4 us
    pallas_call x1, Pallas kernels, output_sums(): pl.pallas_call(functools.partial(output_kernel, len(mixed), chunks), out_...  12.1 us
    pallas_call x1, Pallas kernels, mix(): pl.pallas_call(functools.partial(mix_kernel, span), out_shape=jax.ShapeDt...  9.49 us
  transfers between devices with their start and end apart: 38, of which 17 were waited for; matrix products, arithmetic and copies ran while one was open for 11% of the time, Pallas kernels for 19%

profile of v2, /device:TPU:17, one launch (start us, length us, event | category | flops | bytes accessed | tf_op | source)
XLA Modules:
  0.0 407.2 jit_solution(8469873449534352698)
XLA Ops:
  23.8 29.0 %collective-permute-done.refs_0_ = bf16[768,512]{1,0:T(8,128)(2,1)} collective-permute-done((bf16[768,512]{1,0:T(8,128)(2,1)}, bf16[768,512]{1,0:T(8,128)(2,1)}, u32[]{:S(2)}, u32[]{:S(2)}) %collective-permute-start) | collective-permute-done | bytes 786464 | tf_op jit(solution)/shard_map/ppermute | solution.py:29
  55.0 10.6 %collective-permute-done.12 = bf16[512,512]{1,0:T(8,128)(2,1)S(1)} collective-permute-done((bf16[512,512]{1,0:T(8,128)(2,1)S(1)}, bf16[512,512]{1,0:T(8,128)(2,1)S(1)}, u32[]{:S(2)}, u32[]{:S(2)}) %collective-permute-start.12) | collective-permute-done | bytes 524320 | tf_op jit(solution)/shard_map/ppermute | solution.py:29
  65.7 6.4 %collective-permute-done.9 = bf16[512,512]{1,0:T(8,128)(2,1)S(1)} collective-permute-done((bf16[512,512]{1,0:T(8,128)(2,1)S(1)}, bf16[512,512]{1,0:T(8,128)(2,1)S(1)}, u32[]{:S(2)}, u32[]{:S(2)}) %collective-permute-start.9) | collective-permute-done | bytes 524320 | tf_op jit(solution)/shard_map/ppermute | solution.py:29
  78.9 22.7 %collective-permute-done.1.refs_1_ = bf16[768,512]{1,0:T(8,128)(2,1)S(1)} collective-permute-done((bf16[768,512]{1,0:T(8,128)(2,1)}, bf16[768,512]{1,0:T(8,128)(2,1)S(1)}, u32[]{:S(2)}, u32[]{:S(2)}) %collective-permute-start.1) | collective-permute-done | bytes 786464 | tf_op jit(solution)/shard_map/ppermute | solution.py:29
  104.3 14.2 %collective-permute-done.13 = bf16[512,512]{1,0:T(8,128)(2,1)S(1)} collective-permute-done((bf16[512,512]{1,0:T(8,128)(2,1)S(1)}, bf16[512,512]{1,0:T(8,128)(2,1)S(1)}, u32[]{:S(2)}, u32[]{:S(2)}) %collective-permute-start.13) | collective-permute-done | bytes 524320 | tf_op jit(solution)/shard_map/ppermute | solution.py:29
  118.4 5.8 %collective-permute-done.10 = bf16[512,512]{1,0:T(8,128)(2,1)S(1)} collective-permute-done((bf16[512,512]{1,0:T(8,128)(2,1)S(1)}, bf16[512,512]{1,0:T(8,128)(2,1)S(1)}, u32[]{:S(2)}, u32[]{:S(2)}) %collective-permute-start.10) | collective-permute-done | bytes 524320 | tf_op jit(solution)/shard_map/ppermute | solution.py:29
  128.7 3.7 collective-permute-start.18
  133.1 8.6 %collective-permute-done.5.refs_5_ = bf16[768,512]{1,0:T(8,128)(2,1)} collective-permute-done((bf16[768,512]{1,0:T(8,128)(2,1)}, bf16[768,512]{1,0:T(8,128)(2,1)}, u32[]{:S(2)}, u32[]{:S(2)}) %collective-permute-start.5) | collective-permute-done | bytes 786464 | tf_op jit(solution)/shard_map/ppermute | solution.py:29
  141.7 4.3 %collective-permute-start.7 = (bf16[768,512]{1,0:T(8,128)(2,1)}, bf16[768,512]{1,0:T(8,128)(2,1)}, u32[]{:S(2)}, u32[]{:S(2)}) collective-permute-start(bf16[768,512]{1,0:T(8,128)(2,1)} %collective-permute-done.5.refs_5_), channel_id=1, source_target_pairs={{0,1},{1,0},{2,3},{3,2},{4,5},{5,4},{6,7},{7,6},{8,9},{9,8},{10,11... | collective-permute-start | bytes 2359304 | tf_op jit(solution)/shard_map/ppermute | solution.py:29
  155.2 13.4 %shard_map.73.tokens = bf16[4096,1536]{1,0:T(8,128)(2,1)} custom-call(s32[8]{0:T(128)} %stack.158.order, s32[2]{0:T(128)} %pad_add_fusion.flags, bf16[768,4096]{1,0:T(8,128)(2,1)} %own.1, bf16[768,512]{1,0:T(8,128)(2,1)} %collective-permute-done.refs_0_, bf16[768,512]{1,0:T(8,128)(2,1)} %copy-done.4, bf16[768,512]{1,0:T(8,128)(2,1)} %copy-done.5, ...), custom_call_target="tpu_custom_call" | custom-call | bytes 25165824 | tf_op jit(solution)/shard_map/pallas_call | solution.py:91
  174.3 25.6 %collective-permute-done.14 = bf16[512,512]{1,0:T(8,128)(2,1)S(1)} collective-permute-done((bf16[512,512]{1,0:T(8,128)(2,1)S(1)}, bf16[512,512]{1,0:T(8,128)(2,1)S(1)}, u32[]{:S(2)}, u32[]{:S(2)}) %collective-permute-start.14) | collective-permute-done | bytes 524320 | tf_op jit(solution)/shard_map/ppermute | solution.py:29
  199.9 3.1 collective-permute-start.19
  205.5 14.1 %shard_map.74.k = bf16[512,1536]{1,0:T(8,128)(2,1)} custom-call(bf16[4096,1536]{1,0:T(8,128)(2,1)} %shard_map.73.tokens, bf16[3,512,512]{2,1,0:T(8,128)(2,1)} %pad_maximum_fusion.1.refs_0_, bf16[3,512,512]{2,1,0:T(8,128)(2,1)} %collective-permute-done.8.refs_1_, bf16[6,512,512]{2,1,0:T(8,128)(2,1)} %all-gather.7.cloned.1.call-done.refs_2_), custom_call_target="tpu_custom_call" | custom-call | flops 6442450944 | bytes 22544384 | tf_op jit(solution)/shard_map/pallas_call | solution.py:121
  222.3 13.3 %shard_map.76.v = bf16[512,1536]{1,0:T(8,128)(2,1)} custom-call(bf16[4096,1536]{1,0:T(8,128)(2,1)} %shard_map.73.tokens, bf16[3,512,512]{2,1,0:T(8,128)(2,1)} %pad_maximum_fusion.1.refs_0_, bf16[3,512,512]{2,1,0:T(8,128)(2,1)} %collective-permute-done.8.refs_1_, bf16[6,512,512]{2,1,0:T(8,128)(2,1)} %all-gather.9.cloned.1.call-done.refs_2_), custom_call_target="tpu_custom_call" | custom-call | flops 6442450944 | bytes 22544384 | tf_op jit(solution)/shard_map/pallas_call | solution.py:121
  244.9 4.3 %collective-permute-done.20 = bf16[1024,256]{1,0:T(8,128)(2,1)} collective-permute-done((bf16[1024,256]{1,0:T(8,128)(2,1)}, bf16[1024,256]{1,0:T(8,128)(2,1)}, u32[]{:S(2)}, u32[]{:S(2)}) %collective-permute-start.20) | collective-permute-done | bytes 524320 | tf_op jit(solution)/shard_map/ppermute | solution.py:29
  254.0 12.2 %collective-permute-done.26 = bf16[2,144,512]{1,2,0:T(8,128)(2,1)S(1)} collective-permute-done((bf16[2,144,512]{1,2,0:T(8,128)(2,1)S(1)}, bf16[2,144,512]{1,2,0:T(8,128)(2,1)S(1)}, u32[]{:S(2)}, u32[]{:S(2)}) %collective-permute-start.26) | collective-permute-done | bytes 294944 | tf_op jit(solution)/shard_map/ppermute | solution.py:29
  268.9 13.9 %shard_map.75.q = bf16[512,1536]{1,0:T(8,128)(2,1)} custom-call(bf16[4096,1536]{1,0:T(8,128)(2,1)} %shard_map.73.tokens, bf16[3,512,512]{2,1,0:T(8,128)(2,1)} %pad_maximum_fusion.1.refs_0_, bf16[3,512,512]{2,1,0:T(8,128)(2,1)} %collective-permute-done.8.refs_1_, bf16[6,512,512]{2,1,0:T(8,128)(2,1)} %all-gather.5.cloned.1.call-done.refs_2_), custom_call_target="tpu_custom_call" | custom-call | flops 6442450944 | bytes 22544384 | tf_op jit(solution)/shard_map/pallas_call | solution.py:121
  285.5 14.1 %shard_map.77.filtered = f32[512,1536]{1,0:T(8,128)} custom-call(bf16[512,1536]{1,0:T(8,128)(2,1)} %shard_map.74.k, bf16[512,1536]{1,0:T(8,128)(2,1)} %shard_map.76.v, bf16[512,256]{1,0:T(8,128)(2,1)} %fusion.19.k_rim, bf16[512,256]{1,0:T(8,128)(2,1)} %fusion.20.v_rim, bf16[512,256]{1,0:T(8,128)(2,1)} %pad_maximum_fusion.9.before, ...), custom_call_target="tpu_custom_call" | custom-call | flops 446693376 | bytes 8388608 | tf_op jit(solution)/shard_map/pallas_call | solution.py:175
  302.8 9.5 %shard_map.78.refs_0_ = bf16[1536,512]{1,0:T(8,128)(2,1)} custom-call(bf16[512,1536]{1,0:T(8,128)(2,1)} %shard_map.75.q, bf16[512,256]{1,0:T(8,128)(2,1)} %fusion.18.q_rim, f32[512,1536]{1,0:T(8,128)} %shard_map.77.filtered, f32[512,24]{1,0:T(8,128)} %pad.29.coefficients), custom_call_target="tpu_custom_call" | custom-call | flops 11010048 | bytes 6291456 | tf_op jit(solution)/shard_map/pallas_call | solution.py:203
  313.9 3.2 collective-permute-done.27.refs_1_
  318.4 12.1 %shard_map.79 = (bf16[8,1536,128]{2,1,0:T(8,128)(2,1)}, bf16[8,1536,128]{2,1,0:T(8,128)(2,1)}) custom-call(s32[8]{0:T(128)} %stack.158.order, bf16[1536,512]{1,0:T(8,128)(2,1)} %shard_map.78.refs_0_, bf16[1536,512]{1,0:T(8,128)(2,1)} %copy-done.16, bf16[1,1024,256]{2,1,0:T(8,128)(2,1)} %bitcast.227, bf16[1,1024,256]{2,1,0:T(8,128)(2,1)} %bitcast.88.refs_3_, ...), custom_call_target="tpu_custom_call" | custom-call | flops 6442450944 | bytes 13631488 | tf_op jit(solution)/shard_map/pallas_call | solution.py:238
  330.4 2.8 dynamic-slice_bitcast_fusion
  336.9 32.2 %collective-permute-done.31 = bf16[8,768,128]{2,1,0:T(8,128)(2,1)} collective-permute-done((bf16[8,768,128]{2,1,0:T(8,128)(2,1)}, bf16[8,768,128]{2,1,0:T(8,128)(2,1)}, u32[]{:S(2)}, u32[]{:S(2)}) %collective-permute-start.31) | collective-permute-done | bytes 1572896 | tf_op jit(solution)/shard_map/ppermute | solution.py:29
  376.0 13.5 %collective-permute-done.32 = bf16[8,384,128]{2,1,0:T(8,128)(2,1)S(1)} collective-permute-done((bf16[8,384,128]{2,1,0:T(8,128)(2,1)S(1)}, bf16[8,384,128]{2,1,0:T(8,128)(2,1)S(1)}, u32[]{:S(2)}, u32[]{:S(2)}) %collective-permute-start.32) | collective-permute-done | bytes 786464 | tf_op jit(solution)/shard_map/ppermute | solution.py:29
  (176 shorter events, 101.0 us)
Async XLA Ops:
  6.5 199.0 %all-gather.7.cloned.1.call-start = ((), (), s32[]{:S(2)}) async-start(), calls=%async_computation.1 | async-start | bytes 4718592 | tf_op jit(solution)/shard_map/all_gather | solution.py:71
  16.1 36.8 %collective-permute-start.8 = (bf16[3,512,512]{2,1,0:T(8,128)(2,1)}, bf16[3,512,512]{2,1,0:T(8,128)(2,1)}, u32[]{:S(2)}, u32[]{:S(2)}) collective-permute-start(bf16[3,512,512]{2,1,0:T(8,128)(2,1)} %pad_maximum_fusion.1.refs_0_), channel_id=1, source_target_pairs={{0,4},{1,5},{2,6},{3,7},{4,0},{5,1},{6,2},{7,3},{8,12},{9,13},{10,... | collective-permute-start | bytes 4718600 | tf_op jit(solution)/shard_map/ppermute | solution.py:29
  20.0 32.8 %collective-permute-start = (bf16[768,512]{1,0:T(8,128)(2,1)}, bf16[768,512]{1,0:T(8,128)(2,1)}, u32[]{:S(2)}, u32[]{:S(2)}) collective-permute-start(bf16[768,512]{1,0:T(8,128)(2,1)} %get-tuple-element.36), channel_id=1, source_target_pairs={{0,8},{1,9},{2,10},{3,11},{4,12},{5,13},{6,14},{7,15},{8,0},{9,1},... | collective-permute-start | bytes 2359304 | tf_op jit(solution)/shard_map/ppermute | solution.py:29
  21.5 33.5 %collective-permute-start.15 = (bf16[512,512]{1,0:T(8,128)(2,1)S(1)}, bf16[512,512]{1,0:T(8,128)(2,1)S(1)}, u32[]{:S(2)}, u32[]{:S(2)}) collective-permute-start(bf16[512,512]{1,0:T(8,128)(2,1)S(1)} %bitcast.221), channel_id=1, source_target_pairs={{0,24},{1,25},{2,26},{3,27},{4,28},{5,29},{6,30},{7,31},{8,16},{9,... | collective-permute-start | bytes 1572872 | tf_op jit(solution)/shard_map/ppermute | solution.py:29
  21.6 44.1 %collective-permute-start.12 = (bf16[512,512]{1,0:T(8,128)(2,1)S(1)}, bf16[512,512]{1,0:T(8,128)(2,1)S(1)}, u32[]{:S(2)}, u32[]{:S(2)}) collective-permute-start(bf16[512,512]{1,0:T(8,128)(2,1)S(1)} %bitcast.217), channel_id=1, source_target_pairs={{0,16},{1,17},{2,18},{3,19},{4,20},{5,21},{6,22},{7,23},{8,24},{9,... | collective-permute-start | bytes 1572872 | tf_op jit(solution)/shard_map/ppermute | solution.py:29
  73.4 148.9 %all-gather.9.cloned.1.call-start = ((), (), s32[]{:S(2)}) async-start(), calls=%async_computation.2 | async-start | bytes 4718592 | tf_op jit(solution)/shard_map/all_gather | solution.py:71
  73.4 28.1 %collective-permute-start.1 = (bf16[768,512]{1,0:T(8,128)(2,1)}, bf16[768,512]{1,0:T(8,128)(2,1)S(1)}, u32[]{:S(2)}, u32[]{:S(2)}) collective-permute-start(bf16[768,512]{1,0:T(8,128)(2,1)} %get-tuple-element.35), channel_id=1, source_target_pairs={{0,8},{1,9},{2,10},{3,11},{4,12},{5,13},{6,14},{7,15},{8,0},{9,1},... | collective-permute-start | bytes 2359304 | tf_op jit(solution)/shard_map/ppermute | solution.py:29
  75.2 26.4 %collective-permute-start.4 = (bf16[768,512]{1,0:T(8,128)(2,1)}, bf16[768,512]{1,0:T(8,128)(2,1)}, u32[]{:S(2)}, u32[]{:S(2)}) collective-permute-start(bf16[768,512]{1,0:T(8,128)(2,1)} %collective-permute-done.refs_0_), channel_id=1, source_target_pairs={{0,2},{1,3},{2,0},{3,1},{4,6},{5,7},{6,4},{7,5},{8,10},{9,11},{10,... | collective-permute-start | bytes 2359304 | tf_op jit(solution)/shard_map/ppermute | solution.py:29
  76.6 27.6 %collective-permute-start.16 = (bf16[512,512]{1,0:T(8,128)(2,1)S(1)}, bf16[512,512]{1,0:T(8,128)(2,1)S(1)}, u32[]{:S(2)}, u32[]{:S(2)}) collective-permute-start(bf16[512,512]{1,0:T(8,128)(2,1)S(1)} %bitcast.223), channel_id=1, source_target_pairs={{0,24},{1,25},{2,26},{3,27},{4,28},{5,29},{6,30},{7,31},{8,16},{9,... | collective-permute-start | bytes 1572872 | tf_op jit(solution)/shard_map/ppermute | solution.py:29
  76.7 41.7 %collective-permute-start.13 = (bf16[512,512]{1,0:T(8,128)(2,1)S(1)}, bf16[512,512]{1,0:T(8,128)(2,1)S(1)}, u32[]{:S(2)}, u32[]{:S(2)}) collective-permute-start(bf16[512,512]{1,0:T(8,128)(2,1)S(1)} %bitcast.214), channel_id=1, source_target_pairs={{0,16},{1,17},{2,18},{3,19},{4,20},{5,21},{6,22},{7,23},{8,24},{9,... | collective-permute-start | bytes 1572872 | tf_op jit(solution)/shard_map/ppermute | solution.py:29
  101.6 22.6 %collective-permute-start.10 = (bf16[512,512]{1,0:T(8,128)(2,1)S(1)}, bf16[512,512]{1,0:T(8,128)(2,1)S(1)}, u32[]{:S(2)}, u32[]{:S(2)}) collective-permute-start(bf16[512,512]{1,0:T(8,128)(2,1)S(1)} %bitcast.224), channel_id=1, source_target_pairs={{0,8},{1,9},{2,10},{3,11},{4,12},{5,13},{6,14},{7,15},{8,0},{9,1},... | collective-permute-start | bytes 1572872 | tf_op jit(solution)/shard_map/ppermute | solution.py:29
  125.7 143.2 %all-gather.5.cloned.1.call-start = ((), (), s32[]{:S(2)}) async-start(), calls=%async_computation | async-start | bytes 4718592 | tf_op jit(solution)/shard_map/all_gather | solution.py:71
  128.7 43.4 %collective-permute-start.18 = (bf16[1024,256]{1,0:T(8,128)(2,1)}, bf16[1024,256]{1,0:T(8,128)(2,1)}, u32[]{:S(2)}, u32[]{:S(2)}) collective-permute-start(bf16[1024,256]{1,0:T(8,128)(2,1)} %bitcast.36), channel_id=1, source_target_pairs={{0,1},{1,0},{2,3},{3,2},{4,5},{5,4},{6,7},{7,6},{8,9},{9,8},{10,11... | collective-permute-start | bytes 1572872 | tf_op jit(solution)/shard_map/ppermute | solution.py:29
  153.8 49.1 %collective-permute-start.17 = (bf16[512,512]{1,0:T(8,128)(2,1)}, bf16[512,512]{1,0:T(8,128)(2,1)S(1)}, u32[]{:S(2)}, u32[]{:S(2)}) collective-permute-start(bf16[512,512]{1,0:T(8,128)(2,1)} %bitcast.219), channel_id=1, source_target_pairs={{0,24},{1,25},{2,26},{3,27},{4,28},{5,29},{6,30},{7,31},{8,16},{9,... | collective-permute-start | bytes 1572872 | tf_op jit(solution)/shard_map/ppermute | solution.py:29
  154.4 45.5 %collective-permute-start.14 = (bf16[512,512]{1,0:T(8,128)(2,1)S(1)}, bf16[512,512]{1,0:T(8,128)(2,1)S(1)}, u32[]{:S(2)}, u32[]{:S(2)}) collective-permute-start(bf16[512,512]{1,0:T(8,128)(2,1)S(1)} %bitcast.212), channel_id=1, source_target_pairs={{0,16},{1,17},{2,18},{3,19},{4,20},{5,21},{6,22},{7,23},{8,24},{9,... | collective-permute-start | bytes 1572872 | tf_op jit(solution)/shard_map/ppermute | solution.py:29
  168.6 35.3 %collective-permute-start.11 = (bf16[512,512]{1,0:T(8,128)(2,1)S(1)}, bf16[512,512]{1,0:T(8,128)(2,1)S(1)}, u32[]{:S(2)}, u32[]{:S(2)}) collective-permute-start(bf16[512,512]{1,0:T(8,128)(2,1)S(1)} %bitcast.220), channel_id=1, source_target_pairs={{0,8},{1,9},{2,10},{3,11},{4,12},{5,13},{6,14},{7,15},{8,0},{9,1},... | collective-permute-start | bytes 1572872 | tf_op jit(solution)/shard_map/ppermute | solution.py:29
  174.0 45.6 %collective-permute-start.21 = (bf16[1024,256]{1,0:T(8,128)(2,1)S(1)}, bf16[1024,256]{1,0:T(8,128)(2,1)}, u32[]{:S(2)}, u32[]{:S(2)}) collective-permute-start(bf16[1024,256]{1,0:T(8,128)(2,1)S(1)} %bitcast.225), channel_id=1, source_target_pairs={{0,4},{1,5},{2,6},{3,7},{4,0},{5,1},{6,2},{7,3},{8,12},{9,13},{10,... | collective-permute-start | bytes 1572872 | tf_op jit(solution)/shard_map/ppermute | solution.py:29
  199.9 45.1 %collective-permute-start.19 = (bf16[1024,256]{1,0:T(8,128)(2,1)S(1)}, bf16[1024,256]{1,0:T(8,128)(2,1)}, u32[]{:S(2)}, u32[]{:S(2)}) collective-permute-start(bf16[1024,256]{1,0:T(8,128)(2,1)S(1)} %bitcast.226), channel_id=1, source_target_pairs={{0,16},{1,17},{2,18},{3,19},{4,20},{5,21},{6,22},{7,23},{8,24},{9,... | collective-permute-start | bytes 1572872 | tf_op jit(solution)/shard_map/ppermute | solution.py:29
  203.0 46.2 %collective-permute-start.20 = (bf16[1024,256]{1,0:T(8,128)(2,1)}, bf16[1024,256]{1,0:T(8,128)(2,1)}, u32[]{:S(2)}, u32[]{:S(2)}) collective-permute-start(bf16[1024,256]{1,0:T(8,128)(2,1)} %bitcast.39), channel_id=1, source_target_pairs={{0,24},{1,25},{2,26},{3,27},{4,28},{5,29},{6,30},{7,31},{8,16},{9,... | collective-permute-start | bytes 1572872 | tf_op jit(solution)/shard_map/ppermute | solution.py:29
  205.3 111.9 %all-gather.11.cloned.1.call-start = ((), (), s32[]{:S(2)}) async-start(), calls=%async_computation.3 | async-start | bytes 4718592 | tf_op jit(solution)/shard_map/all_gather | solution.py:71
  219.7 29.6 %collective-permute-start.22 = (bf16[1024,256]{1,0:T(8,128)(2,1)}, bf16[1024,256]{1,0:T(8,128)(2,1)S(1)}, u32[]{:S(2)}, u32[]{:S(2)}) collective-permute-start(bf16[1024,256]{1,0:T(8,128)(2,1)} %bitcast.39), channel_id=1, source_target_pairs={{0,8},{1,9},{2,10},{3,11},{4,12},{5,13},{6,14},{7,15},{8,0},{9,1},... | collective-permute-start | bytes 1572872 | tf_op jit(solution)/shard_map/ppermute | solution.py:29
  242.4 23.8 %collective-permute-start.26 = (bf16[2,144,512]{1,2,0:T(8,128)(2,1)S(1)}, bf16[2,144,512]{1,2,0:T(8,128)(2,1)S(1)}, u32[]{:S(2)}, u32[]{:S(2)}) collective-permute-start(bf16[2,144,512]{1,2,0:T(8,128)(2,1)S(1)} %pad_maximum_fusion.6), channel_id=1, source_target_pairs={{0,4},{1,5},{2,6},{3,7},{4,0},{5,1},{6,2},{7,3},{8,12},{9,13},{10,... | collective-permute-start | bytes 884744 | tf_op jit(solution)/shard_map/ppermute | solution.py:29
  333.2 35.9 %collective-permute-start.31 = (bf16[8,768,128]{2,1,0:T(8,128)(2,1)}, bf16[8,768,128]{2,1,0:T(8,128)(2,1)}, u32[]{:S(2)}, u32[]{:S(2)}) collective-permute-start(bf16[8,768,128]{2,1,0:T(8,128)(2,1)} %dynamic-slice_bitcast_fusion), channel_id=1, source_target_pairs={{0,8},{1,9},{2,10},{3,11},{4,12},{5,13},{6,14},{7,15},{8,0},{9,1},... | collective-permute-start | bytes 4718600 | tf_op jit(solution)/shard_map/ppermute | solution.py:29
  335.7 37.1 %collective-permute-start.28 = (bf16[16,384,128]{2,1,0:T(8,128)(2,1)}, bf16[16,384,128]{2,1,0:T(8,128)(2,1)}, u32[]{:S(2)}, u32[]{:S(2)}) collective-permute-start(bf16[16,384,128]{2,1,0:T(8,128)(2,1)} %dynamic-slice_bitcast_fusion.1), channel_id=1, source_target_pairs={{0,2},{1,3},{2,0},{3,1},{4,6},{5,7},{6,4},{7,5},{8,10},{9,11},{10,... | collective-permute-start | bytes 4718600 | tf_op jit(solution)/shard_map/ppermute | solution.py:29
  (33 other events, 333.1 us)
Sparse Core Ops, SparseCore 0:
  73.5 47.5 all-gather.6
  125.8 47.9 all-gather.8
  205.4 53.9 all-gather.4
  260.8 52.8 all-gather.10

commit v3 on v2

--- a/solution.py
+++ b/solution.py
@@ -51,13 +51,13 @@
         self.far.append(result)
         return result
 
-    def gather(self, own, other, *last):
+    def gather(self, own, other, *last, first=()):
         nx, nz = self.places.nx, self.places.nz
         held = {}
         masks = sorted(range(1, nz), key=lambda m: (m < 2, m))
         for m in masks:
             held[m] = self.step(
-                other if m % 2 else own, m * nx, *(last if m == masks[-1] else ())
+                other if m % 2 else own, m * nx, *(last if m == masks[-1] else first)
             )
         return held
 
@@ -325,16 +325,15 @@
         }
         for h in range(2)
     ]
-    k_held = line.gather(*k_parts, parts[0][0], *beside)
+    out_halves = out_weight.reshape(width, 2, share)
+    rows_of = [pick(out_halves, core, 1), places.flip(pick(out_halves, 1 - core, 1), tp=1)]
+    both = jnp.stack(rows_of).reshape(2, 2, half, share)
+    out_own, out_other = (pick(both, part, 1).reshape(width, share) for part in (zl, 1 - zl))
+    k_held = line.gather(*k_parts, parts[0][0], *beside, rows_of[1])
     for part in parts:
         for step in range(1, ny):
             part[2 * step] = places.flip(part[0], tp=2 * step)
     k_cross = line.cross(k_held)
-
-    out_halves = out_weight.reshape(width, 2, share)
-    rows_of = [pick(out_halves, core, 1), places.flip(pick(out_halves, 1 - core, 1), tp=1)]
-    both = jnp.stack(rows_of).reshape(2, 2, half, share)
-    out_own, out_other = (pick(both, part, 1).reshape(width, share) for part in (zl, 1 - zl))
 
     v_held = line.gather(*v_parts, parts[1][0], *parts[0].values())
     for part in parts:
@@ -348,8 +347,9 @@
         [part[mask] for mask in range(places.tp) for part in parts],
         depth,
     )
-    q_held = line.gather(*q_parts, tokens)
-    q_cross = line.cross(q_held)
+    near, far = ([part[mask] for mask in part if mask % 2] for part in parts)
+    q_held = line.gather(*q_parts, *far, first=near)
+    q_cross = line.cross(q_held, tokens)
     out_beside = line.beside(out_own)
 
     def entries(s, crossed):
@@ -369,7 +369,7 @@
     coefficients = jnp.concatenate([short.reshape(3 * span, half), gain[None, :]]).T
     coefficients = jnp.pad(coefficients, ((0, 0), (0, (-3 * span - 1) % 8)))
 
-    def halos(tails):
+    def halos(tails, *done):
         beside = places.send(tails, lambda i, j: (i - i % nx + (i + 1) % nx, j))
         below = places.send(
             tails[1],
@@ -377,6 +377,7 @@
             if i % nx == nx - 1 and i + 2 * nx < places.ctx
             else None,
         )
+        beside, below = after(beside, *done), after(below, *done)
         start = x == 0
         return [jnp.where(start, below, beside[0]), jnp.where(start, beside[0], beside[1])]
 
@@ -398,8 +399,8 @@
         )
         for end in ends
     ]
-    before = halos(jnp.stack(tails))
     q = project(tokens, entries(0, after(q_cross, *out_held.values())))
+    before = halos(jnp.stack(tails), q)
     edges = halos(jnp.stack([q[:, end - edge : end].T for end in ends]))
     filtered = long_filter_part(
         span,

time: 411 us -> 424 us (1.032)
  waiting for transfers between devices: 194 us -> 209 us
  starting transfers between devices: 46.4 us -> 50.7 us
    ppermute x34, waiting for transfers between devices: 194 us -> 206 us  [send(): return lax.ppermute(value, AXES, pairs)]
    ppermute x34, starting transfers between devices: 46 us -> 50.3 us  [send(): return lax.ppermute(value, AXES, pairs)]
  transfers between devices with their start and end apart: 38 -> 38, of which waited for: 17 -> 18; matrix products, arithmetic and copies ran while one was open for 11% -> 10% of each run, Pallas kernels for 19% -> 18%
where the time goes in v3:
time: 424 us; the launch traced here: 423 us
  waiting for transfers between devices  209 us (49%)
  Pallas kernels  89.5 us (21%)
  starting transfers between devices  50.7 us (12%)
  local copies, waits for them, and re-layouts  31 us (7%)
  other arithmetic  27.3 us (6%)
  between operations  13.7 us (3%)
    ppermute x34, waiting for transfers between devices, send(): return lax.ppermute(value, AXES, pairs)  206 us
    ppermute x34, starting transfers between devices, send(): return lax.ppermute(value, AXES, pairs)  50.3 us
    pallas_call x3, Pallas kernels, project(): pl.pallas_call(project_kernel, out_shape=jax.ShapeDtypeStruct((width, row...  40.6 us
    pallas_call x1, Pallas kernels, long_filter_part(): pl.pallas_call(functools.partial(filter_kernel, span), out_shape=jax.Shap...  14 us
    pallas_call x1, Pallas kernels, prepare(): pl.pallas_call(functools.partial(prepare_kernel, per_part), out_shape=jax...  13.4 us
    pallas_call x1, Pallas kernels, output_sums(): pl.pallas_call(functools.partial(output_kernel, len(mixed), chunks), out_...  12 us
    pallas_call x1, Pallas kernels, mix(): pl.pallas_call(functools.partial(mix_kernel, span), out_shape=jax.ShapeDt...  9.49 us
  transfers between devices with their start and end apart: 38, of which 18 were waited for; matrix products, arithmetic and copies ran while one was open for 10% of the time, Pallas kernels for 18%

profile of v3, /device:TPU:17, one launch (start us, length us, event | category | flops | bytes accessed | tf_op | source)
XLA Modules:
  0.0 423.0 jit_solution(16669557536250485128)
XLA Ops:
  29.8 8.6 %collective-permute-done.refs_0_ = bf16[768,512]{1,0:T(8,128)(2,1)} collective-permute-done((bf16[768,512]{1,0:T(8,128)(2,1)}, bf16[768,512]{1,0:T(8,128)(2,1)}, u32[]{:S(2)}, u32[]{:S(2)}) %collective-permute-start) | collective-permute-done | bytes 786464 | tf_op jit(solution)/shard_map/ppermute | solution.py:29
  38.4 13.3 %collective-permute-done.8.refs_1_ = bf16[3,512,512]{2,1,0:T(8,128)(2,1)} collective-permute-done((bf16[3,512,512]{2,1,0:T(8,128)(2,1)}, bf16[3,512,512]{2,1,0:T(8,128)(2,1)}, u32[]{:S(2)}, u32[]{:S(2)}) %collective-permute-start.8) | collective-permute-done | bytes 1572896 | tf_op jit(solution)/shard_map/ppermute | solution.py:29
  53.0 10.4 %collective-permute-done.16 = bf16[512,512]{1,0:T(8,128)(2,1)S(1)} collective-permute-done((bf16[512,512]{1,0:T(8,128)(2,1)S(1)}, bf16[512,512]{1,0:T(8,128)(2,1)S(1)}, u32[]{:S(2)}, u32[]{:S(2)}) %collective-permute-start.16) | collective-permute-done | bytes 524320 | tf_op jit(solution)/shard_map/ppermute | solution.py:29
  63.5 9.4 %collective-permute-done.13 = bf16[512,512]{1,0:T(8,128)(2,1)S(1)} collective-permute-done((bf16[512,512]{1,0:T(8,128)(2,1)S(1)}, bf16[512,512]{1,0:T(8,128)(2,1)S(1)}, u32[]{:S(2)}, u32[]{:S(2)}) %collective-permute-start.13) | collective-permute-done | bytes 524320 | tf_op jit(solution)/shard_map/ppermute | solution.py:29
  82.0 13.4 %collective-permute-done.1.refs_1_ = bf16[768,512]{1,0:T(8,128)(2,1)} collective-permute-done((bf16[768,512]{1,0:T(8,128)(2,1)}, bf16[768,512]{1,0:T(8,128)(2,1)}, u32[]{:S(2)}, u32[]{:S(2)}) %collective-permute-start.1) | collective-permute-done | bytes 786464 | tf_op jit(solution)/shard_map/ppermute | solution.py:29
  95.4 3.4 collective-permute-start.11
  98.8 23.8 %collective-permute-done.14 = bf16[512,512]{1,0:T(8,128)(2,1)S(1)} collective-permute-done((bf16[512,512]{1,0:T(8,128)(2,1)S(1)}, bf16[512,512]{1,0:T(8,128)(2,1)S(1)}, u32[]{:S(2)}, u32[]{:S(2)}) %collective-permute-start.14) | collective-permute-done | bytes 524320 | tf_op jit(solution)/shard_map/ppermute | solution.py:29
  122.6 4.2 %collective-permute-done.11 = bf16[512,512]{1,0:T(8,128)(2,1)S(1)} collective-permute-done((bf16[512,512]{1,0:T(8,128)(2,1)}, bf16[512,512]{1,0:T(8,128)(2,1)S(1)}, u32[]{:S(2)}, u32[]{:S(2)}) %collective-permute-start.11) | collective-permute-done | bytes 524320 | tf_op jit(solution)/shard_map/ppermute | solution.py:29
  130.1 3.5 collective-permute-start.2
  134.1 9.9 %collective-permute-done.5.refs_5_ = bf16[768,512]{1,0:T(8,128)(2,1)} collective-permute-done((bf16[768,512]{1,0:T(8,128)(2,1)}, bf16[768,512]{1,0:T(8,128)(2,1)}, u32[]{:S(2)}, u32[]{:S(2)}) %collective-permute-start.5) | collective-permute-done | bytes 786464 | tf_op jit(solution)/shard_map/ppermute | solution.py:29
  144.0 4.6 %collective-permute-start.7 = (bf16[768,512]{1,0:T(8,128)(2,1)}, bf16[768,512]{1,0:T(8,128)(2,1)}, u32[]{:S(2)}, u32[]{:S(2)}) collective-permute-start(bf16[768,512]{1,0:T(8,128)(2,1)} %collective-permute-done.5.refs_5_), channel_id=1, source_target_pairs={{0,1},{1,0},{2,3},{3,2},{4,5},{5,4},{6,7},{7,6},{8,9},{9,8},{10,11... | collective-permute-start | bytes 2359304 | tf_op jit(solution)/shard_map/ppermute | solution.py:29
  159.8 13.4 %shard_map.73.tokens = bf16[4096,1536]{1,0:T(8,128)(2,1)} custom-call(s32[8]{0:T(128)} %stack.158.order, s32[2]{0:T(128)} %pad_add_fusion.flags, bf16[768,4096]{1,0:T(8,128)(2,1)} %own.1, bf16[768,512]{1,0:T(8,128)(2,1)} %collective-permute-done.refs_0_, bf16[768,512]{1,0:T(8,128)(2,1)} %collective-permute-done.1.refs_1_, ...), custom_call_target="tpu_custom_call" | custom-call | bytes 25165824 | tf_op jit(solution)/shard_map/pallas_call | solution.py:91
  173.1 25.7 %collective-permute-done.15 = bf16[512,512]{1,0:T(8,128)(2,1)S(1)} collective-permute-done((bf16[512,512]{1,0:T(8,128)(2,1)S(1)}, bf16[512,512]{1,0:T(8,128)(2,1)S(1)}, u32[]{:S(2)}, u32[]{:S(2)}) %collective-permute-start.15) | collective-permute-done | bytes 524320 | tf_op jit(solution)/shard_map/ppermute | solution.py:29
  203.8 14.0 %shard_map.74.k = bf16[512,1536]{1,0:T(8,128)(2,1)} custom-call(bf16[4096,1536]{1,0:T(8,128)(2,1)} %shard_map.73.tokens, bf16[3,512,512]{2,1,0:T(8,128)(2,1)} %pad_maximum_fusion.1.refs_0_, bf16[3,512,512]{2,1,0:T(8,128)(2,1)} %collective-permute-done.8.refs_1_, bf16[6,512,512]{2,1,0:T(8,128)(2,1)} %all-gather.7.cloned.1.call-done.refs_2_), custom_call_target="tpu_custom_call" | custom-call | flops 6442450944 | bytes 22544384 | tf_op jit(solution)/shard_map/pallas_call | solution.py:121
  222.3 12.6 %collective-permute-done.19 = bf16[1024,256]{1,0:T(8,128)(2,1)S(1)} collective-permute-done((bf16[1024,256]{1,0:T(8,128)(2,1)S(1)}, bf16[1024,256]{1,0:T(8,128)(2,1)S(1)}, u32[]{:S(2)}, u32[]{:S(2)}) %collective-permute-start.19) | collective-permute-done | bytes 524320 | tf_op jit(solution)/shard_map/ppermute | solution.py:29
  234.9 13.3 %collective-permute-done.20 = bf16[1024,256]{1,0:T(8,128)(2,1)} collective-permute-done((bf16[1024,256]{1,0:T(8,128)(2,1)S(1)}, bf16[1024,256]{1,0:T(8,128)(2,1)}, u32[]{:S(2)}, u32[]{:S(2)}) %collective-permute-start.20) | collective-permute-done | bytes 524320 | tf_op jit(solution)/shard_map/ppermute | solution.py:29
  250.8 13.3 %shard_map.76.v = bf16[512,1536]{1,0:T(8,128)(2,1)} custom-call(bf16[4096,1536]{1,0:T(8,128)(2,1)} %shard_map.73.tokens, bf16[3,512,512]{2,1,0:T(8,128)(2,1)} %pad_maximum_fusion.1.refs_0_, bf16[3,512,512]{2,1,0:T(8,128)(2,1)} %collective-permute-done.8.refs_1_, bf16[6,512,512]{2,1,0:T(8,128)(2,1)} %all-gather.9.cloned.1.call-done.refs_2_), custom_call_target="tpu_custom_call" | custom-call | flops 6442450944 | bytes 22544384 | tf_op jit(solution)/shard_map/pallas_call | solution.py:121
  272.3 13.3 %shard_map.75.q = bf16[512,1536]{1,0:T(8,128)(2,1)} custom-call(bf16[4096,1536]{1,0:T(8,128)(2,1)} %shard_map.73.tokens, bf16[3,512,512]{2,1,0:T(8,128)(2,1)} %pad_maximum_fusion.1.refs_0_, bf16[3,512,512]{2,1,0:T(8,128)(2,1)} %collective-permute-done.8.refs_1_, bf16[6,512,512]{2,1,0:T(8,128)(2,1)} %all-gather.5.cloned.1.call-done.refs_2_), custom_call_target="tpu_custom_call" | custom-call | flops 6442450944 | bytes 22544384 | tf_op jit(solution)/shard_map/pallas_call | solution.py:121
  289.2 10.7 %collective-permute-done.26 = bf16[2,144,512]{1,2,0:T(8,128)(2,1)S(1)} collective-permute-done((bf16[2,144,512]{1,2,0:T(8,128)(2,1)S(1)}, bf16[2,144,512]{1,2,0:T(8,128)(2,1)S(1)}, u32[]{:S(2)}, u32[]{:S(2)}) %collective-permute-start.26) | collective-permute-done | bytes 294944 | tf_op jit(solution)/shard_map/ppermute | solution.py:29
  302.6 14.0 %shard_map.77.filtered = f32[512,1536]{1,0:T(8,128)} custom-call(bf16[512,1536]{1,0:T(8,128)(2,1)} %shard_map.74.k, bf16[512,1536]{1,0:T(8,128)(2,1)} %shard_map.76.v, bf16[512,256]{1,0:T(8,128)(2,1)} %fusion.19.k_rim, bf16[512,256]{1,0:T(8,128)(2,1)} %fusion.20.v_rim, bf16[512,256]{1,0:T(8,128)(2,1)} %pad_maximum_fusion.9.before, ...), custom_call_target="tpu_custom_call" | custom-call | flops 446693376 | bytes 8388608 | tf_op jit(solution)/shard_map/pallas_call | solution.py:175
  317.5 9.5 %shard_map.78.refs_0_ = bf16[1536,512]{1,0:T(8,128)(2,1)} custom-call(bf16[512,1536]{1,0:T(8,128)(2,1)} %shard_map.75.q, bf16[512,256]{1,0:T(8,128)(2,1)} %fusion.18.q_rim, f32[512,1536]{1,0:T(8,128)} %shard_map.77.filtered, f32[512,24]{1,0:T(8,128)} %pad.29.coefficients), custom_call_target="tpu_custom_call" | custom-call | flops 11010048 | bytes 6291456 | tf_op jit(solution)/shard_map/pallas_call | solution.py:203
  334.1 12.0 %shard_map.79 = (bf16[8,1536,128]{2,1,0:T(8,128)(2,1)}, bf16[8,1536,128]{2,1,0:T(8,128)(2,1)}) custom-call(s32[8]{0:T(128)} %stack.158.order, bf16[1536,512]{1,0:T(8,128)(2,1)} %shard_map.78.refs_0_, bf16[1536,512]{1,0:T(8,128)(2,1)} %copy-done.11, bf16[1,1024,256]{2,1,0:T(8,128)(2,1)} %bitcast.222, bf16[1,1024,256]{2,1,0:T(8,128)(2,1)} %bitcast.264, ...), custom_call_target="tpu_custom_call" | custom-call | flops 6442450944 | bytes 13631488 | tf_op jit(solution)/shard_map/pallas_call | solution.py:238
  352.7 32.1 %collective-permute-done.31 = bf16[8,768,128]{2,1,0:T(8,128)(2,1)} collective-permute-done((bf16[8,768,128]{2,1,0:T(8,128)(2,1)}, bf16[8,768,128]{2,1,0:T(8,128)(2,1)}, u32[]{:S(2)}, u32[]{:S(2)}) %collective-permute-start.31) | collective-permute-done | bytes 1572896 | tf_op jit(solution)/shard_map/ppermute | solution.py:29
  391.6 13.4 %collective-permute-done.32 = bf16[8,384,128]{2,1,0:T(8,128)(2,1)S(1)} collective-permute-done((bf16[8,384,128]{2,1,0:T(8,128)(2,1)S(1)}, bf16[8,384,128]{2,1,0:T(8,128)(2,1)S(1)}, u32[]{:S(2)}, u32[]{:S(2)}) %collective-permute-start.32) | collective-permute-done | bytes 786464 | tf_op jit(solution)/shard_map/ppermute | solution.py:29
  (168 shorter events, 107.3 us)
Async XLA Ops:
  6.5 197.3 %all-gather.7.cloned.1.call-start = ((), (), s32[]{:S(2)}) async-start(), calls=%async_computation.1 | async-start | bytes 4718592 | tf_op jit(solution)/shard_map/all_gather | solution.py:71
  16.1 35.6 %collective-permute-start.8 = (bf16[3,512,512]{2,1,0:T(8,128)(2,1)}, bf16[3,512,512]{2,1,0:T(8,128)(2,1)}, u32[]{:S(2)}, u32[]{:S(2)}) collective-permute-start(bf16[3,512,512]{2,1,0:T(8,128)(2,1)} %pad_maximum_fusion.1.refs_0_), channel_id=1, source_target_pairs={{0,4},{1,5},{2,6},{3,7},{4,0},{5,1},{6,2},{7,3},{8,12},{9,13},{10,... | collective-permute-start | bytes 4718600 | tf_op jit(solution)/shard_map/ppermute | solution.py:29
  27.5 36.0 %collective-permute-start.16 = (bf16[512,512]{1,0:T(8,128)(2,1)S(1)}, bf16[512,512]{1,0:T(8,128)(2,1)S(1)}, u32[]{:S(2)}, u32[]{:S(2)}) collective-permute-start(bf16[512,512]{1,0:T(8,128)(2,1)S(1)} %bitcast.216), channel_id=1, source_target_pairs={{0,24},{1,25},{2,26},{3,27},{4,28},{5,29},{6,30},{7,31},{8,16},{9,... | collective-permute-start | bytes 1572872 | tf_op jit(solution)/shard_map/ppermute | solution.py:29
  27.6 45.3 %collective-permute-start.13 = (bf16[512,512]{1,0:T(8,128)(2,1)S(1)}, bf16[512,512]{1,0:T(8,128)(2,1)S(1)}, u32[]{:S(2)}, u32[]{:S(2)}) collective-permute-start(bf16[512,512]{1,0:T(8,128)(2,1)S(1)} %bitcast.211), channel_id=1, source_target_pairs={{0,16},{1,17},{2,18},{3,19},{4,20},{5,21},{6,22},{7,23},{8,24},{9,... | collective-permute-start | bytes 1572872 | tf_op jit(solution)/shard_map/ppermute | solution.py:29
  51.7 21.1 %collective-permute-start.10 = (bf16[512,512]{1,0:T(8,128)(2,1)S(1)}, bf16[512,512]{1,0:T(8,128)(2,1)S(1)}, u32[]{:S(2)}, u32[]{:S(2)}) collective-permute-start(bf16[512,512]{1,0:T(8,128)(2,1)S(1)} %bitcast.217), channel_id=1, source_target_pairs={{0,8},{1,9},{2,10},{3,11},{4,12},{5,13},{6,14},{7,15},{8,0},{9,1},... | collective-permute-start | bytes 1572872 | tf_op jit(solution)/shard_map/ppermute | solution.py:29
  74.3 176.5 %all-gather.9.cloned.1.call-start = ((), (), s32[]{:S(2)}) async-start(), calls=%async_computation.2 | async-start | bytes 4718592 | tf_op jit(solution)/shard_map/all_gather | solution.py:71
  74.3 21.1 %collective-permute-start.1 = (bf16[768,512]{1,0:T(8,128)(2,1)}, bf16[768,512]{1,0:T(8,128)(2,1)}, u32[]{:S(2)}, u32[]{:S(2)}) collective-permute-start(bf16[768,512]{1,0:T(8,128)(2,1)} %get-tuple-element.41), channel_id=1, source_target_pairs={{0,8},{1,9},{2,10},{3,11},{4,12},{5,13},{6,14},{7,15},{8,0},{9,1},... | collective-permute-start | bytes 2359304 | tf_op jit(solution)/shard_map/ppermute | solution.py:29
  80.1 42.5 %collective-permute-start.14 = (bf16[512,512]{1,0:T(8,128)(2,1)S(1)}, bf16[512,512]{1,0:T(8,128)(2,1)S(1)}, u32[]{:S(2)}, u32[]{:S(2)}) collective-permute-start(bf16[512,512]{1,0:T(8,128)(2,1)S(1)} %bitcast.209), channel_id=1, source_target_pairs={{0,16},{1,17},{2,18},{3,19},{4,20},{5,21},{6,22},{7,23},{8,24},{9,... | collective-permute-start | bytes 1572872 | tf_op jit(solution)/shard_map/ppermute | solution.py:29
  95.4 31.4 %collective-permute-start.11 = (bf16[512,512]{1,0:T(8,128)(2,1)}, bf16[512,512]{1,0:T(8,128)(2,1)S(1)}, u32[]{:S(2)}, u32[]{:S(2)}) collective-permute-start(bf16[512,512]{1,0:T(8,128)(2,1)} %bitcast.219), channel_id=1, source_target_pairs={{0,8},{1,9},{2,10},{3,11},{4,12},{5,13},{6,14},{7,15},{8,0},{9,1},... | collective-permute-start | bytes 1572872 | tf_op jit(solution)/shard_map/ppermute | solution.py:29
  128.2 144.1 %all-gather.5.cloned.1.call-start = ((), (), s32[]{:S(2)}) async-start(), calls=%async_computation | async-start | bytes 4718592 | tf_op jit(solution)/shard_map/all_gather | solution.py:71
  130.1 22.1 %collective-permute-start.2 = (bf16[768,512]{1,0:T(8,128)(2,1)}, bf16[768,512]{1,0:T(8,128)(2,1)}, u32[]{:S(2)}, u32[]{:S(2)}) collective-permute-start(bf16[768,512]{1,0:T(8,128)(2,1)} %collective-permute-done.refs_0_), channel_id=1, source_target_pairs={{0,1},{1,0},{2,3},{3,2},{4,5},{5,4},{6,7},{7,6},{8,9},{9,8},{10,11... | collective-permute-start | bytes 2359304 | tf_op jit(solution)/shard_map/ppermute | solution.py:29
  152.2 49.8 %collective-permute-start.18 = (bf16[512,512]{1,0:T(8,128)(2,1)S(1)}, bf16[512,512]{1,0:T(8,128)(2,1)S(1)}, u32[]{:S(2)}, u32[]{:S(2)}) collective-permute-start(bf16[512,512]{1,0:T(8,128)(2,1)S(1)} %bitcast.214), channel_id=1, source_target_pairs={{0,24},{1,25},{2,26},{3,27},{4,28},{5,29},{6,30},{7,31},{8,16},{9,... | collective-permute-start | bytes 1572872 | tf_op jit(solution)/shard_map/ppermute | solution.py:29
  153.5 45.4 %collective-permute-start.15 = (bf16[512,512]{1,0:T(8,128)(2,1)S(1)}, bf16[512,512]{1,0:T(8,128)(2,1)S(1)}, u32[]{:S(2)}, u32[]{:S(2)}) collective-permute-start(bf16[512,512]{1,0:T(8,128)(2,1)S(1)} %bitcast.207), channel_id=1, source_target_pairs={{0,16},{1,17},{2,18},{3,19},{4,20},{5,21},{6,22},{7,23},{8,24},{9,... | collective-permute-start | bytes 1572872 | tf_op jit(solution)/shard_map/ppermute | solution.py:29
  153.7 48.5 %collective-permute-start.12 = (bf16[512,512]{1,0:T(8,128)(2,1)S(1)}, bf16[512,512]{1,0:T(8,128)(2,1)S(1)}, u32[]{:S(2)}, u32[]{:S(2)}) collective-permute-start(bf16[512,512]{1,0:T(8,128)(2,1)S(1)} %bitcast.215), channel_id=1, source_target_pairs={{0,8},{1,9},{2,10},{3,11},{4,12},{5,13},{6,14},{7,15},{8,0},{9,1},... | collective-permute-start | bytes 1572872 | tf_op jit(solution)/shard_map/ppermute | solution.py:29
  158.3 59.5 %collective-permute-start.21 = (bf16[1024,256]{1,0:T(8,128)(2,1)S(1)}, bf16[1024,256]{1,0:T(8,128)(2,1)S(1)}, u32[]{:S(2)}, u32[]{:S(2)}) collective-permute-start(bf16[1024,256]{1,0:T(8,128)(2,1)S(1)} %bitcast.220), channel_id=1, source_target_pairs={{0,4},{1,5},{2,6},{3,7},{4,0},{5,1},{6,2},{7,3},{8,12},{9,13},{10,... | collective-permute-start | bytes 1572872 | tf_op jit(solution)/shard_map/ppermute | solution.py:29
  198.9 36.0 %collective-permute-start.19 = (bf16[1024,256]{1,0:T(8,128)(2,1)S(1)}, bf16[1024,256]{1,0:T(8,128)(2,1)S(1)}, u32[]{:S(2)}, u32[]{:S(2)}) collective-permute-start(bf16[1024,256]{1,0:T(8,128)(2,1)S(1)} %bitcast.221), channel_id=1, source_target_pairs={{0,16},{1,17},{2,18},{3,19},{4,20},{5,21},{6,22},{7,23},{8,24},{9,... | collective-permute-start | bytes 1572872 | tf_op jit(solution)/shard_map/ppermute | solution.py:29
  202.0 46.2 %collective-permute-start.20 = (bf16[1024,256]{1,0:T(8,128)(2,1)S(1)}, bf16[1024,256]{1,0:T(8,128)(2,1)}, u32[]{:S(2)}, u32[]{:S(2)}) collective-permute-start(bf16[1024,256]{1,0:T(8,128)(2,1)S(1)} %bitcast.223), channel_id=1, source_target_pairs={{0,24},{1,25},{2,26},{3,27},{4,28},{5,29},{6,30},{7,31},{8,16},{9,... | collective-permute-start | bytes 1572872 | tf_op jit(solution)/shard_map/ppermute | solution.py:29
  203.6 130.6 %all-gather.11.cloned.1.call-start = ((), (), s32[]{:S(2)}) async-start(), calls=%async_computation.3 | async-start | bytes 4718592 | tf_op jit(solution)/shard_map/all_gather | solution.py:71
  217.8 30.4 %collective-permute-start.22 = (bf16[1024,256]{1,0:T(8,128)(2,1)S(1)}, bf16[1024,256]{1,0:T(8,128)(2,1)}, u32[]{:S(2)}, u32[]{:S(2)}) collective-permute-start(bf16[1024,256]{1,0:T(8,128)(2,1)S(1)} %bitcast.224), channel_id=1, source_target_pairs={{0,8},{1,9},{2,10},{3,11},{4,12},{5,13},{6,14},{7,15},{8,0},{9,1},... | collective-permute-start | bytes 1572872 | tf_op jit(solution)/shard_map/ppermute | solution.py:29
  272.2 27.7 %collective-permute-start.26 = (bf16[2,144,512]{1,2,0:T(8,128)(2,1)S(1)}, bf16[2,144,512]{1,2,0:T(8,128)(2,1)S(1)}, u32[]{:S(2)}, u32[]{:S(2)}) collective-permute-start(bf16[2,144,512]{1,2,0:T(8,128)(2,1)S(1)} %pad_maximum_fusion.6), channel_id=1, source_target_pairs={{0,4},{1,5},{2,6},{3,7},{4,0},{5,1},{6,2},{7,3},{8,12},{9,13},{10,... | collective-permute-start | bytes 884744 | tf_op jit(solution)/shard_map/ppermute | solution.py:29
  286.7 29.9 %collective-permute-start.23 = (bf16[8,512]{0,1:T(8,128)(2,1)S(1)}, bf16[8,512]{0,1:T(8,128)(2,1)S(1)}, u32[]{:S(2)}, u32[]{:S(2)}) collective-permute-start(bf16[8,512]{0,1:T(8,128)(2,1)S(1)} %get-tuple-element.54), channel_id=1, source_target_pairs={{4,16},{5,17},{6,18},{7,19},{12,24},{13,25},{14,26},{15,27}} | collective-permute-start | bytes 24584 | tf_op jit(solution)/shard_map/ppermute | solution.py:29
  288.3 28.4 %collective-permute-start.24 = (bf16[2,8,512]{1,2,0:T(8,128)(2,1)S(1)}, bf16[2,8,512]{1,2,0:T(8,128)(2,1)S(1)}, u32[]{:S(2)}, u32[]{:S(2)}) collective-permute-start(bf16[2,8,512]{1,2,0:T(8,128)(2,1)S(1)} %pad_maximum_fusion.7), channel_id=1, source_target_pairs={{0,4},{1,5},{2,6},{3,7},{4,0},{5,1},{6,2},{7,3},{8,12},{9,13},{10,... | collective-permute-start | bytes 49160 | tf_op jit(solution)/shard_map/ppermute | solution.py:29
  349.0 35.8 %collective-permute-start.31 = (bf16[8,768,128]{2,1,0:T(8,128)(2,1)}, bf16[8,768,128]{2,1,0:T(8,128)(2,1)}, u32[]{:S(2)}, u32[]{:S(2)}) collective-permute-start(bf16[8,768,128]{2,1,0:T(8,128)(2,1)} %dynamic-slice_bitcast_fusion), channel_id=1, source_target_pairs={{0,8},{1,9},{2,10},{3,11},{4,12},{5,13},{6,14},{7,15},{8,0},{9,1},... | collective-permute-start | bytes 4718600 | tf_op jit(solution)/shard_map/ppermute | solution.py:29
  351.4 37.1 %collective-permute-start.28 = (bf16[16,384,128]{2,1,0:T(8,128)(2,1)}, bf16[16,384,128]{2,1,0:T(8,128)(2,1)}, u32[]{:S(2)}, u32[]{:S(2)}) collective-permute-start(bf16[16,384,128]{2,1,0:T(8,128)(2,1)} %dynamic-slice_bitcast_fusion.1), channel_id=1, source_target_pairs={{0,2},{1,3},{2,0},{3,1},{4,6},{5,7},{6,4},{7,5},{8,10},{9,11},{10,... | collective-permute-start | bytes 4718600 | tf_op jit(solution)/shard_map/ppermute | solution.py:29
  (29 other events, 361.6 us)
Sparse Core Ops, SparseCore 0:
  74.4 49.7 all-gather.6
  128.3 59.9 all-gather.8
  203.7 45.4 all-gather.4
  272.4 61.6 all-gather.10

commit v4 on v1

--- a/solution.py
+++ b/solution.py
@@ -51,22 +51,24 @@
         self.far.append(result)
         return result
 
-    def gather(self, own, other, *last):
+    def gather(self, own, other, *last, first=()):
         nx, nz = self.places.nx, self.places.nz
         held = {}
         masks = sorted(range(1, nz), key=lambda m: (m < 2, m))
         for m in masks:
             held[m] = self.step(
-                other if m % 2 else own, m * nx, *(last if m == masks[-1] else ())
+                other if m % 2 else own, m * nx, *(last if m == masks[-1] else first)
             )
         return held
 
     def beside(self, own):
         return [self.places.flip(own, ctx=step) for step in range(1, self.places.nx)]
 
-    def cross(self, held, *done):
+    def stack(self, held):
+        return jnp.stack([held[m] for m in range(1, self.places.nz)])
+
+    def cross(self, stack):
         nx, nz = self.places.nx, self.places.nz
-        stack = after(jnp.stack([held[m] for m in range(1, nz)]), *done)
         groups = [[z * nx + x for x in range(nx)] for z in range(nz)]
         return lax.all_gather(stack, "ctx", axis_index_groups=groups, tiled=True)
 
@@ -317,35 +319,36 @@
 
     size = in_features // places.tp
     parts = {0: places.flip(lax.dynamic_slice_in_dim(tokens, j * size, size, 1), ctx=nx)}
-    k_held = line.gather(*k_parts, parts[0], *beside)
-    for step in range(1, ny):
-        parts[2 * step] = places.flip(parts[0], tp=2 * step)
-    k_cross = line.cross(k_held)
 
     out_halves = out_weight.reshape(width, 2, share)
     rows_of = [pick(out_halves, core, 1), places.flip(pick(out_halves, 1 - core, 1), tp=1)]
     both = jnp.stack(rows_of).reshape(2, 2, half, share)
     out_own, out_other = (pick(both, part, 1).reshape(width, share) for part in (zl, 1 - zl))
-
+    k_held = line.gather(*k_parts, parts[0], rows_of[1])
+    k_cross = line.cross(line.stack(k_held))
+    mine = after(parts[0], *k_held.values(), *beside)
+    for step in range(1, ny):
+        parts[2 * step] = places.flip(mine, tp=2 * step)
+    for mask in list(parts):
+        parts[mask ^ 1] = places.flip(parts[mask] if mask else mine, tp=1)
     v_held = line.gather(*v_parts, *parts.values())
-    for mask in list(parts):
-        parts[mask ^ 1] = places.flip(parts[mask], tp=1)
-    v_cross = line.cross(v_held)
+    v_cross = line.cross(line.stack(v_held))
     tokens = prepare(
         order, flags, tokens, [parts[mask] for mask in range(places.tp)], depth
     )
     q_held = line.gather(*q_parts, tokens)
-    q_cross = line.cross(q_held)
+    q_cross = line.cross(line.stack(q_held))
     out_beside = line.beside(out_own)
 
     def entries(s, crossed):
         return [(stack, s, 1) for stack in [own] + beside] + [(crossed, 0, crossed.shape[0])]
 
     k = project(tokens, entries(1, k_cross))
-    out_held = line.gather(out_own, out_other, k, *out_beside)
     u = project(tokens, entries(2, v_cross))
+    out_held = line.gather(out_own, out_other, k, u, *out_beside)
     outs = [stack[None] for stack in [out_own] + out_beside]
-    outs.append(line.cross(out_held, u))
+    out_stack = line.stack(out_held)
+    outs.append(line.cross(out_stack))
 
     tap_index = jnp.arange(taps, dtype=F32)
     filters = (long_filter * jnp.exp(-decay_rate[:, None] * tap_index[None, :])).astype(BF16)
@@ -355,7 +358,7 @@
     coefficients = jnp.concatenate([short.reshape(3 * span, half), gain[None, :]]).T
     coefficients = jnp.pad(coefficients, ((0, 0), (0, (-3 * span - 1) % 8)))
 
-    def halos(tails):
+    def halos(tails, *done):
         beside = places.send(tails, lambda i, j: (i - i % nx + (i + 1) % nx, j))
         below = places.send(
             tails[1],
@@ -363,6 +366,7 @@
             if i % nx == nx - 1 and i + 2 * nx < places.ctx
             else None,
         )
+        beside, below = after(beside, *done), after(below, *done)
         start = x == 0
         return [jnp.where(start, below, beside[0]), jnp.where(start, beside[0], beside[1])]
 
@@ -384,7 +388,9 @@
         )
         for end in ends
     ]
-    before = halos(jnp.stack(tails))
+    q = project(tokens, entries(0, after(q_cross, out_stack)))
+    before = halos(jnp.stack(tails), q)
+    edges = halos(jnp.stack([q[:, end - edge : end].T for end in ends]))
     filtered = long_filter_part(
         span,
         k,
@@ -392,12 +398,10 @@
         rims([value[taps : taps + edge] for value in before]),
         rims([value[taps + edge :] for value in before]),
         rims([value[:taps] for value in before]),
-        coefficients,
+        after(coefficients, q),
         bands,
     )
-    q = project(tokens, entries(0, after(q_cross, filtered, *out_held.values())))
-    before = halos(jnp.stack([q[:, end - edge : end].T for end in ends]))
-    mixed = mix(span, q, rims(before), filtered, coefficients)
+    mixed = mix(span, q, rims(edges), filtered, coefficients)
     mixed = [mixed, places.flip(mixed, tp=1)]
 
     def over_y(value):

time: 415 us -> 448 us (1.080)
  waiting for transfers between devices: 206 us -> 239 us
    all_gather x4, waiting for transfers between devices: 0.04 us -> 41.3 us  [cross(): return lax.all_gather(stack, 'ctx', axis_index_groups=groups, tiled=True)]
    ppermute x30, waiting for transfers between devices: 206 us -> 198 us  [send(): return lax.ppermute(value, AXES, pairs)]
  transfers between devices with their start and end apart: 34 -> 34, of which waited for: 16 -> 16; matrix products, arithmetic and copies ran while one was open for 11% -> 11% of each run, Pallas kernels for 19% -> 18%
where the time goes in v4:
time: 448 us; the launch traced here: 447 us
  waiting for transfers between devices  239 us (53%)
  Pallas kernels  91.9 us (21%)
  starting transfers between devices  42.6 us (10%)
  local copies, waits for them, and re-layouts  29.8 us (7%)
  other arithmetic  28.2 us (6%)
  between operations  13.7 us (3%)
    ppermute x30, waiting for transfers between devices, send(): return lax.ppermute(value, AXES, pairs)  198 us
    ppermute x30, starting transfers between devices, send(): return lax.ppermute(value, AXES, pairs)  42.3 us
    all_gather x4, waiting for transfers between devices, cross(): return lax.all_gather(stack, 'ctx', axis_index_groups=groups, tiled=True)  41.3 us
    pallas_call x3, Pallas kernels, project(): pl.pallas_call(project_kernel, out_shape=jax.ShapeDtypeStruct((width, row...  40.7 us
    pallas_call x1, Pallas kernels, prepare(): pl.pallas_call(functools.partial(prepare_kernel, per_part), out_shape=jax...  15.7 us
    pallas_call x1, Pallas kernels, long_filter_part(): pl.pallas_call(functools.partial(filter_kernel, span), out_shape=jax.Shap...  14 us
    pallas_call x1, Pallas kernels, output_sums(): pl.pallas_call(functools.partial(output_kernel, len(mixed), chunks), out_...  12 us
    pallas_call x1, Pallas kernels, mix(): pl.pallas_call(functools.partial(mix_kernel, span), out_shape=jax.ShapeDt...  9.51 us
  transfers between devices with their start and end apart: 34, of which 16 were waited for; matrix products, arithmetic and copies ran while one was open for 11% of the time, Pallas kernels for 18%

profile of v4, /device:TPU:17, one launch (start us, length us, event | category | flops | bytes accessed | tf_op | source)
XLA Modules:
  0.0 447.2 jit_solution(18281675453468559944)
XLA Ops:
  28.4 27.0 %collective-permute-done.refs_0_ = bf16[768,1024]{1,0:T(8,128)(2,1)} collective-permute-done((bf16[768,1024]{1,0:T(8,128)(2,1)}, bf16[768,1024]{1,0:T(8,128)(2,1)}, u32[]{:S(2)}, u32[]{:S(2)}) %collective-permute-start) | collective-permute-done | bytes 1572896 | tf_op jit(solution)/shard_map/ppermute | solution.py:29
  57.6 15.4 %collective-permute-done.2 = bf16[512,512]{1,0:T(8,128)(2,1)S(1)} collective-permute-done((bf16[512,512]{1,0:T(8,128)(2,1)S(1)}, bf16[512,512]{1,0:T(8,128)(2,1)S(1)}, u32[]{:S(2)}, u32[]{:S(2)}) %collective-permute-start.2) | collective-permute-done | bytes 524320 | tf_op jit(solution)/shard_map/ppermute | solution.py:29
  73.0 4.6 %collective-permute-done.4 = bf16[512,512]{1,0:T(8,128)(2,1)S(1)} collective-permute-done((bf16[512,512]{1,0:T(8,128)(2,1)S(1)}, bf16[512,512]{1,0:T(8,128)(2,1)S(1)}, u32[]{:S(2)}, u32[]{:S(2)}) %collective-permute-start.4) | collective-permute-done | bytes 524320 | tf_op jit(solution)/shard_map/ppermute | solution.py:29
  81.3 2.9 collective-permute-start.6
  84.3 27.0 %collective-permute-done.7.refs_2_ = bf16[768,1024]{1,0:T(8,128)(2,1)} collective-permute-done((bf16[768,1024]{1,0:T(8,128)(2,1)}, bf16[768,1024]{1,0:T(8,128)(2,1)}, u32[]{:S(2)}, u32[]{:S(2)}) %collective-permute-start.7) | collective-permute-done | bytes 1572896 | tf_op jit(solution)/shard_map/ppermute | solution.py:29
  111.2 3.5 collective-permute-start.8
  118.9 32.1 %collective-permute-done.13 = bf16[512,512]{1,0:T(8,128)(2,1)S(1)} collective-permute-done((bf16[512,512]{1,0:T(8,128)(2,1)S(1)}, bf16[512,512]{1,0:T(8,128)(2,1)S(1)}, u32[]{:S(2)}, u32[]{:S(2)}) %collective-permute-start.13) | collective-permute-done | bytes 524320 | tf_op jit(solution)/shard_map/ppermute | solution.py:29
  151.0 10.2 %collective-permute-done.11 = bf16[512,512]{1,0:T(8,128)(2,1)S(1)} collective-permute-done((bf16[512,512]{1,0:T(8,128)(2,1)S(1)}, bf16[512,512]{1,0:T(8,128)(2,1)S(1)}, u32[]{:S(2)}, u32[]{:S(2)}) %collective-permute-start.11) | collective-permute-done | bytes 524320 | tf_op jit(solution)/shard_map/ppermute | solution.py:29
  168.3 4.0 collective-permute-start.12
  172.3 15.7 %shard_map.73.tokens = bf16[4096,1536]{1,0:T(8,128)(2,1)} custom-call(s32[8]{0:T(128)} %stack.158.order, s32[2]{0:T(128)} %pad_add_fusion.flags, bf16[768,4096]{1,0:T(8,128)(2,1)} %own.1, bf16[768,1024]{1,0:T(8,128)(2,1)} %collective-permute-done.refs_0_, bf16[768,1024]{1,0:T(8,128)(2,1)} %collective-permute-done.6.refs_1_, ...), custom_call_target="tpu_custom_call" | custom-call | bytes 25165824 | tf_op jit(solution)/shard_map/pallas_call | solution.py:92
  192.0 11.3 %collective-permute-done.14 = bf16[512,512]{1,0:T(8,128)(2,1)S(1)} collective-permute-done((bf16[512,512]{1,0:T(8,128)(2,1)S(1)}, bf16[512,512]{1,0:T(8,128)(2,1)S(1)}, u32[]{:S(2)}, u32[]{:S(2)}) %collective-permute-start.14) | collective-permute-done | bytes 524320 | tf_op jit(solution)/shard_map/ppermute | solution.py:29
  203.5 20.2 %collective-permute-done.12 = bf16[512,512]{1,0:T(8,128)(2,1)S(1)} collective-permute-done((bf16[512,512]{1,0:T(8,128)(2,1)S(1)}, bf16[512,512]{1,0:T(8,128)(2,1)S(1)}, u32[]{:S(2)}, u32[]{:S(2)}) %collective-permute-start.12) | collective-permute-done | bytes 524320 | tf_op jit(solution)/shard_map/ppermute | solution.py:29
  223.7 3.1 collective-permute-start.17
  228.4 13.3 %shard_map.74.k = bf16[512,1536]{1,0:T(8,128)(2,1)} custom-call(bf16[4096,1536]{1,0:T(8,128)(2,1)} %shard_map.73.tokens, bf16[3,512,512]{2,1,0:T(8,128)(2,1)} %pad_maximum_fusion.1.refs_0_, bf16[3,512,512]{2,1,0:T(8,128)(2,1)} %collective-permute-done.5.refs_1_, bf16[6,512,512]{2,1,0:T(8,128)(2,1)} %all-gather.7.cloned.1.call-done.refs_2_), custom_call_target="tpu_custom_call" | custom-call | flops 6442450944 | bytes 22544384 | tf_op jit(solution)/shard_map/pallas_call | solution.py:122
  244.2 14.0 %shard_map.75.v = bf16[512,1536]{1,0:T(8,128)(2,1)} custom-call(bf16[4096,1536]{1,0:T(8,128)(2,1)} %shard_map.73.tokens, bf16[3,512,512]{2,1,0:T(8,128)(2,1)} %pad_maximum_fusion.1.refs_0_, bf16[3,512,512]{2,1,0:T(8,128)(2,1)} %collective-permute-done.5.refs_1_, bf16[6,512,512]{2,1,0:T(8,128)(2,1)} %all-gather.9.cloned.1.call-done.refs_2_), custom_call_target="tpu_custom_call" | custom-call | flops 6442450944 | bytes 22544384 | tf_op jit(solution)/shard_map/pallas_call | solution.py:122
  269.6 33.7 %all-gather.5.cloned.1.call-done.refs_2_ = bf16[6,512,512]{2,1,0:T(8,128)(2,1)} async-done(((bf16[3,512,512]{2,1,0:T(8,128)(2,1)}), bf16[6,512,512]{2,1,0:T(8,128)(2,1)}) %all-gather.5.cloned.1.call-update) | async-done | bytes 3145744 | tf_op jit(solution)/shard_map/all_gather | solution.py:73
  303.3 13.3 %shard_map.76.q = bf16[512,1536]{1,0:T(8,128)(2,1)} custom-call(bf16[4096,1536]{1,0:T(8,128)(2,1)} %shard_map.73.tokens, bf16[3,512,512]{2,1,0:T(8,128)(2,1)} %pad_maximum_fusion.1.refs_0_, bf16[3,512,512]{2,1,0:T(8,128)(2,1)} %collective-permute-done.5.refs_1_, bf16[6,512,512]{2,1,0:T(8,128)(2,1)} %all-gather.5.cloned.1.call-done.refs_2_), custom_call_target="tpu_custom_call" | custom-call | flops 6442450944 | bytes 22544384 | tf_op jit(solution)/shard_map/pallas_call | solution.py:122
  322.2 14.0 %shard_map.77.filtered = f32[512,1536]{1,0:T(8,128)} custom-call(bf16[512,1536]{1,0:T(8,128)(2,1)} %shard_map.74.k, bf16[512,1536]{1,0:T(8,128)(2,1)} %shard_map.75.v, bf16[512,256]{1,0:T(8,128)(2,1)} %fusion.19.k_rim, bf16[512,256]{1,0:T(8,128)(2,1)} %fusion.20.v_rim, bf16[512,256]{1,0:T(8,128)(2,1)} %pad_maximum_fusion.9.before, ...), custom_call_target="tpu_custom_call" | custom-call | flops 446693376 | bytes 8388608 | tf_op jit(solution)/shard_map/pallas_call | solution.py:176
  337.1 9.5 %shard_map.78.refs_0_ = bf16[1536,512]{1,0:T(8,128)(2,1)} custom-call(bf16[512,1536]{1,0:T(8,128)(2,1)} %shard_map.76.q, bf16[512,256]{1,0:T(8,128)(2,1)} %fusion.18.q_rim, f32[512,1536]{1,0:T(8,128)} %shard_map.77.filtered, f32[512,24]{1,0:T(8,128)} %pad.29.coefficients), custom_call_target="tpu_custom_call" | custom-call | flops 11010048 | bytes 6291456 | tf_op jit(solution)/shard_map/pallas_call | solution.py:204
  347.9 3.2 collective-permute-done.23.refs_1_
  351.1 7.6 %all-gather.11.cloned.1.call-done.refs_4_ = bf16[6,1024,256]{2,1,0:T(8,128)(2,1)} async-done(((bf16[3,1024,256]{2,1,0:T(8,128)(2,1)}), bf16[6,1024,256]{2,1,0:T(8,128)(2,1)}) %all-gather.11.cloned.1.call-update) | async-done | bytes 3145744 | tf_op jit(solution)/shard_map/all_gather | solution.py:73
  358.7 12.0 %shard_map.79 = (bf16[8,1536,128]{2,1,0:T(8,128)(2,1)}, bf16[8,1536,128]{2,1,0:T(8,128)(2,1)}) custom-call(s32[8]{0:T(128)} %stack.158.order, bf16[1536,512]{1,0:T(8,128)(2,1)} %shard_map.78.refs_0_, bf16[1536,512]{1,0:T(8,128)(2,1)} %copy-done.8, bf16[1,1024,256]{2,1,0:T(8,128)(2,1)} %bitcast.223, bf16[1,1024,256]{2,1,0:T(8,128)(2,1)} %bitcast.91.refs_3_, ...), custom_call_target="tpu_custom_call" | custom-call | flops 6442450944 | bytes 13631488 | tf_op jit(solution)/shard_map/pallas_call | solution.py:239
  377.2 31.9 %collective-permute-done.27 = bf16[8,768,128]{2,1,0:T(8,128)(2,1)} collective-permute-done((bf16[8,768,128]{2,1,0:T(8,128)(2,1)}, bf16[8,768,128]{2,1,0:T(8,128)(2,1)}, u32[]{:S(2)}, u32[]{:S(2)}) %collective-permute-start.27) | collective-permute-done | bytes 1572896 | tf_op jit(solution)/shard_map/ppermute | solution.py:29
  416.0 13.1 %collective-permute-done.28 = bf16[8,384,128]{2,1,0:T(8,128)(2,1)S(1)} collective-permute-done((bf16[8,384,128]{2,1,0:T(8,128)(2,1)S(1)}, bf16[8,384,128]{2,1,0:T(8,128)(2,1)S(1)}, u32[]{:S(2)}, u32[]{:S(2)}) %collective-permute-start.28) | collective-permute-done | bytes 786464 | tf_op jit(solution)/shard_map/ppermute | solution.py:29
  (152 shorter events, 90.8 us)
Async XLA Ops:
  6.5 221.8 %all-gather.7.cloned.1.call-start = ((), (), s32[]{:S(2)}) async-start(), calls=%async_computation.1 | async-start | bytes 4718592 | tf_op jit(solution)/shard_map/all_gather | solution.py:73
  9.4 46.0 %collective-permute-start = (bf16[768,1024]{1,0:T(8,128)(2,1)}, bf16[768,1024]{1,0:T(8,128)(2,1)}, u32[]{:S(2)}, u32[]{:S(2)}) collective-permute-start(bf16[768,1024]{1,0:T(8,128)(2,1)} %constant_dynamic-slice_fusion.11), channel_id=1, source_target_pairs={{0,8},{1,9},{2,10},{3,11},{4,12},{5,13},{6,14},{7,15},{8,0},{9,1},... | collective-permute-start | bytes 4718600 | tf_op jit(solution)/shard_map/ppermute | solution.py:29
  19.6 53.5 %collective-permute-start.5 = (bf16[3,512,512]{2,1,0:T(8,128)(2,1)}, bf16[3,512,512]{2,1,0:T(8,128)(2,1)}, u32[]{:S(2)}, u32[]{:S(2)}) collective-permute-start(bf16[3,512,512]{2,1,0:T(8,128)(2,1)} %pad_maximum_fusion.1.refs_0_), channel_id=1, source_target_pairs={{0,4},{1,5},{2,6},{3,7},{4,0},{5,1},{6,2},{7,3},{8,12},{9,13},{10,... | collective-permute-start | bytes 4718600 | tf_op jit(solution)/shard_map/ppermute | solution.py:29
  25.7 31.9 %collective-permute-start.1 = (bf16[512,512]{1,0:T(8,128)(2,1)}, bf16[512,512]{1,0:T(8,128)(2,1)}, u32[]{:S(2)}, u32[]{:S(2)}) collective-permute-start(bf16[512,512]{1,0:T(8,128)(2,1)} %bitcast.211), channel_id=1, source_target_pairs={{0,16},{1,17},{2,18},{3,19},{4,20},{5,21},{6,22},{7,23},{8,24},{9,... | collective-permute-start | bytes 1572872 | tf_op jit(solution)/shard_map/ppermute | solution.py:29
  27.0 46.0 %collective-permute-start.2 = (bf16[512,512]{1,0:T(8,128)(2,1)S(1)}, bf16[512,512]{1,0:T(8,128)(2,1)S(1)}, u32[]{:S(2)}, u32[]{:S(2)}) collective-permute-start(bf16[512,512]{1,0:T(8,128)(2,1)S(1)} %bitcast.216), channel_id=1, source_target_pairs={{0,24},{1,25},{2,26},{3,27},{4,28},{5,29},{6,30},{7,31},{8,16},{9,... | collective-permute-start | bytes 1572872 | tf_op jit(solution)/shard_map/ppermute | solution.py:29
  55.4 22.2 %collective-permute-start.4 = (bf16[512,512]{1,0:T(8,128)(2,1)S(1)}, bf16[512,512]{1,0:T(8,128)(2,1)S(1)}, u32[]{:S(2)}, u32[]{:S(2)}) collective-permute-start(bf16[512,512]{1,0:T(8,128)(2,1)S(1)} %bitcast.217), channel_id=1, source_target_pairs={{0,8},{1,9},{2,10},{3,11},{4,12},{5,13},{6,14},{7,15},{8,0},{9,1},... | collective-permute-start | bytes 1572872 | tf_op jit(solution)/shard_map/ppermute | solution.py:29
  77.6 33.6 %collective-permute-start.7 = (bf16[768,1024]{1,0:T(8,128)(2,1)}, bf16[768,1024]{1,0:T(8,128)(2,1)}, u32[]{:S(2)}, u32[]{:S(2)}) collective-permute-start(bf16[768,1024]{1,0:T(8,128)(2,1)} %collective-permute-done.refs_0_), channel_id=1, source_target_pairs={{0,2},{1,3},{2,0},{3,1},{4,6},{5,7},{6,4},{7,5},{8,10},{9,11},{10,... | collective-permute-start | bytes 4718600 | tf_op jit(solution)/shard_map/ppermute | solution.py:29
  81.3 162.9 %all-gather.9.cloned.1.call-start = ((), (), s32[]{:S(2)}) async-start(), calls=%async_computation.2 | async-start | bytes 4718592 | tf_op jit(solution)/shard_map/all_gather | solution.py:73
  81.3 36.4 %collective-permute-start.6 = (bf16[768,1024]{1,0:T(8,128)(2,1)}, bf16[768,1024]{1,0:T(8,128)(2,1)}, u32[]{:S(2)}, u32[]{:S(2)}) collective-permute-start(bf16[768,1024]{1,0:T(8,128)(2,1)} %collective-permute-done.refs_0_), channel_id=1, source_target_pairs={{0,1},{1,0},{2,3},{3,2},{4,5},{5,4},{6,7},{7,6},{8,9},{9,8},{10,11... | collective-permute-start | bytes 4718600 | tf_op jit(solution)/shard_map/ppermute | solution.py:29
  114.9 36.1 %collective-permute-start.13 = (bf16[512,512]{1,0:T(8,128)(2,1)S(1)}, bf16[512,512]{1,0:T(8,128)(2,1)S(1)}, u32[]{:S(2)}, u32[]{:S(2)}) collective-permute-start(bf16[512,512]{1,0:T(8,128)(2,1)S(1)} %bitcast.218), channel_id=1, source_target_pairs={{0,24},{1,25},{2,26},{3,27},{4,28},{5,29},{6,30},{7,31},{8,16},{9,... | collective-permute-start | bytes 1572872 | tf_op jit(solution)/shard_map/ppermute | solution.py:29
  116.2 45.1 %collective-permute-start.11 = (bf16[512,512]{1,0:T(8,128)(2,1)S(1)}, bf16[512,512]{1,0:T(8,128)(2,1)S(1)}, u32[]{:S(2)}, u32[]{:S(2)}) collective-permute-start(bf16[512,512]{1,0:T(8,128)(2,1)S(1)} %bitcast.209), channel_id=1, source_target_pairs={{0,16},{1,17},{2,18},{3,19},{4,20},{5,21},{6,22},{7,23},{8,24},{9,... | collective-permute-start | bytes 1572872 | tf_op jit(solution)/shard_map/ppermute | solution.py:29
  118.1 43.2 %collective-permute-start.9 = (bf16[512,512]{1,0:T(8,128)(2,1)S(1)}, bf16[512,512]{1,0:T(8,128)(2,1)S(1)}, u32[]{:S(2)}, u32[]{:S(2)}) collective-permute-start(bf16[512,512]{1,0:T(8,128)(2,1)S(1)} %bitcast.219), channel_id=1, source_target_pairs={{0,8},{1,9},{2,10},{3,11},{4,12},{5,13},{6,14},{7,15},{8,0},{9,1},... | collective-permute-start | bytes 1572872 | tf_op jit(solution)/shard_map/ppermute | solution.py:29
  162.6 140.7 %all-gather.5.cloned.1.call-start = ((), (), s32[]{:S(2)}) async-start(), calls=%async_computation | async-start | bytes 4718592 | tf_op jit(solution)/shard_map/all_gather | solution.py:73
  168.0 35.3 %collective-permute-start.14 = (bf16[512,512]{1,0:T(8,128)(2,1)S(1)}, bf16[512,512]{1,0:T(8,128)(2,1)S(1)}, u32[]{:S(2)}, u32[]{:S(2)}) collective-permute-start(bf16[512,512]{1,0:T(8,128)(2,1)S(1)} %bitcast.214), channel_id=1, source_target_pairs={{0,24},{1,25},{2,26},{3,27},{4,28},{5,29},{6,30},{7,31},{8,16},{9,... | collective-permute-start | bytes 1572872 | tf_op jit(solution)/shard_map/ppermute | solution.py:29
  168.3 55.4 %collective-permute-start.12 = (bf16[512,512]{1,0:T(8,128)(2,1)S(1)}, bf16[512,512]{1,0:T(8,128)(2,1)S(1)}, u32[]{:S(2)}, u32[]{:S(2)}) collective-permute-start(bf16[512,512]{1,0:T(8,128)(2,1)S(1)} %bitcast.207), channel_id=1, source_target_pairs={{0,16},{1,17},{2,18},{3,19},{4,20},{5,21},{6,22},{7,23},{8,24},{9,... | collective-permute-start | bytes 1572872 | tf_op jit(solution)/shard_map/ppermute | solution.py:29
  188.0 38.8 %collective-permute-start.10 = (bf16[512,512]{1,0:T(8,128)(2,1)S(1)}, bf16[512,512]{1,0:T(8,128)(2,1)S(1)}, u32[]{:S(2)}, u32[]{:S(2)}) collective-permute-start(bf16[512,512]{1,0:T(8,128)(2,1)S(1)} %bitcast.215), channel_id=1, source_target_pairs={{0,8},{1,9},{2,10},{3,11},{4,12},{5,13},{6,14},{7,15},{8,0},{9,1},... | collective-permute-start | bytes 1572872 | tf_op jit(solution)/shard_map/ppermute | solution.py:29
  191.8 66.4 %collective-permute-start.15 = (bf16[1024,256]{1,0:T(8,128)(2,1)S(1)}, bf16[1024,256]{1,0:T(8,128)(2,1)}, u32[]{:S(2)}, u32[]{:S(2)}) collective-permute-start(bf16[1024,256]{1,0:T(8,128)(2,1)S(1)} %bitcast.221), channel_id=1, source_target_pairs={{0,4},{1,5},{2,6},{3,7},{4,0},{5,1},{6,2},{7,3},{8,12},{9,13},{10,... | collective-permute-start | bytes 1572872 | tf_op jit(solution)/shard_map/ppermute | solution.py:29
  203.3 63.8 %collective-permute-start.18 = (bf16[1024,256]{1,0:T(8,128)(2,1)S(1)}, bf16[1024,256]{1,0:T(8,128)(2,1)}, u32[]{:S(2)}, u32[]{:S(2)}) collective-permute-start(bf16[1024,256]{1,0:T(8,128)(2,1)S(1)} %bitcast.224), channel_id=1, source_target_pairs={{0,24},{1,25},{2,26},{3,27},{4,28},{5,29},{6,30},{7,31},{8,16},{9,... | collective-permute-start | bytes 1572872 | tf_op jit(solution)/shard_map/ppermute | solution.py:29
  223.7 43.4 %collective-permute-start.17 = (bf16[1024,256]{1,0:T(8,128)(2,1)S(1)}, bf16[1024,256]{1,0:T(8,128)(2,1)}, u32[]{:S(2)}, u32[]{:S(2)}) collective-permute-start(bf16[1024,256]{1,0:T(8,128)(2,1)S(1)} %bitcast.222), channel_id=1, source_target_pairs={{0,16},{1,17},{2,18},{3,19},{4,20},{5,21},{6,22},{7,23},{8,24},{9,... | collective-permute-start | bytes 1572872 | tf_op jit(solution)/shard_map/ppermute | solution.py:29
  228.1 130.6 %all-gather.11.cloned.1.call-start = ((), (), s32[]{:S(2)}) async-start(), calls=%async_computation.3 | async-start | bytes 4718592 | tf_op jit(solution)/shard_map/all_gather | solution.py:73
  262.9 56.5 %collective-permute-start.21 = (bf16[144,512]{0,1:T(8,128)(2,1)S(1)}, bf16[144,512]{0,1:T(8,128)(2,1)S(1)}, u32[]{:S(2)}, u32[]{:S(2)}) collective-permute-start(bf16[144,512]{0,1:T(8,128)(2,1)S(1)} %pad_maximum_fusion.8), channel_id=1, source_target_pairs={{4,16},{5,17},{6,18},{7,19},{12,24},{13,25},{14,26},{15,27}} | collective-permute-start | bytes 442376 | tf_op jit(solution)/shard_map/ppermute | solution.py:29
  266.4 53.1 %collective-permute-start.22 = (bf16[2,144,512]{1,2,0:T(8,128)(2,1)S(1)}, bf16[2,144,512]{1,2,0:T(8,128)(2,1)S(1)}, u32[]{:S(2)}, u32[]{:S(2)}) collective-permute-start(bf16[2,144,512]{1,2,0:T(8,128)(2,1)S(1)} %pad_maximum_fusion.6), channel_id=1, source_target_pairs={{0,4},{1,5},{2,6},{3,7},{4,0},{5,1},{6,2},{7,3},{8,12},{9,13},{10,... | collective-permute-start | bytes 884744 | tf_op jit(solution)/shard_map/ppermute | solution.py:29
  373.6 35.6 %collective-permute-start.27 = (bf16[8,768,128]{2,1,0:T(8,128)(2,1)}, bf16[8,768,128]{2,1,0:T(8,128)(2,1)}, u32[]{:S(2)}, u32[]{:S(2)}) collective-permute-start(bf16[8,768,128]{2,1,0:T(8,128)(2,1)} %dynamic-slice_bitcast_fusion), channel_id=1, source_target_pairs={{0,8},{1,9},{2,10},{3,11},{4,12},{5,13},{6,14},{7,15},{8,0},{9,1},... | collective-permute-start | bytes 4718600 | tf_op jit(solution)/shard_map/ppermute | solution.py:29
  376.1 36.7 %collective-permute-start.24 = (bf16[16,384,128]{2,1,0:T(8,128)(2,1)}, bf16[16,384,128]{2,1,0:T(8,128)(2,1)}, u32[]{:S(2)}, u32[]{:S(2)}) collective-permute-start(bf16[16,384,128]{2,1,0:T(8,128)(2,1)} %dynamic-slice_bitcast_fusion.1), channel_id=1, source_target_pairs={{0,2},{1,3},{2,0},{3,1},{4,6},{5,7},{6,4},{7,5},{8,10},{9,11},{10,... | collective-permute-start | bytes 4718600 | tf_op jit(solution)/shard_map/ppermute | solution.py:29
  (21 other events, 202.8 us)
Sparse Core Ops, SparseCore 0:
  81.4 47.1 all-gather.6
  162.7 58.2 all-gather.8
  228.2 75.0 all-gather.4
  304.7 53.9 all-gather.10

commit v5 on v3

--- a/solution.py
+++ b/solution.py
@@ -51,15 +51,15 @@
         self.far.append(result)
         return result
 
-    def gather(self, own, other, *last, first=()):
-        nx, nz = self.places.nx, self.places.nz
-        held = {}
-        masks = sorted(range(1, nz), key=lambda m: (m < 2, m))
-        for m in masks:
-            held[m] = self.step(
-                other if m % 2 else own, m * nx, *(last if m == masks[-1] else first)
-            )
-        return held
+    def gather(self, own, other, *last):
+        return self.finish(self.begin(own, other), own, other, *last)
+
+    def begin(self, own, other):
+        masks = sorted(range(2, self.places.nz))
+        return {m: self.step(other if m % 2 else own, m * self.places.nx) for m in masks}
+
+    def finish(self, held, own, other, *last):
+        return {**held, 1: self.step(other, self.places.nx, *last)}
 
     def beside(self, own):
         return [self.places.flip(own, ctx=step) for step in range(1, self.places.nx)]
@@ -336,10 +336,11 @@
     k_cross = line.cross(k_held)
 
     v_held = line.gather(*v_parts, parts[1][0], *parts[0].values())
-    for part in parts:
+    v_cross = line.cross(v_held)
+    q_held = line.begin(*q_parts)
+    for part, done in zip(parts, ((), (q_held[nz - 1],))):
         for mask in list(part):
-            part[mask ^ 1] = places.flip(part[mask], tp=1)
-    v_cross = line.cross(v_held)
+            part[mask ^ 1] = places.flip(after(part[mask], *done), tp=1)
     tokens = prepare(
         order,
         flags,
@@ -347,17 +348,16 @@
         [part[mask] for mask in range(places.tp) for part in parts],
         depth,
     )
-    near, far = ([part[mask] for mask in part if mask % 2] for part in parts)
-    q_held = line.gather(*q_parts, *far, first=near)
-    q_cross = line.cross(q_held, tokens)
+    q_held = line.finish(q_held, *q_parts, tokens)
+    q_cross = line.cross(q_held)
     out_beside = line.beside(out_own)
 
     def entries(s, crossed):
         return [(stack, s, 1) for stack in [own] + beside] + [(crossed, 0, crossed.shape[0])]
 
     k = project(tokens, entries(1, k_cross))
-    out_held = line.gather(out_own, out_other, k, *out_beside)
     u = project(tokens, entries(2, v_cross))
+    out_held = line.gather(out_own, out_other, k, u, *out_beside)
     outs = [stack[None] for stack in [out_own] + out_beside]
     outs.append(line.cross(out_held, u))
 

time: 424 us -> 412 us (0.972)
  waiting for transfers between devices: 209 us -> 197 us
    ppermute x34, waiting for transfers between devices: 206 us -> 165 us  [send(): return lax.ppermute(value, AXES, pairs)]
    all_gather x4, waiting for transfers between devices: 2.88 us -> 32 us  [cross(): return lax.all_gather(stack, 'ctx', axis_index_groups=groups, tiled=True)]
  transfers between devices with their start and end apart: 38 -> 38, of which waited for: 18 -> 17; matrix products, arithmetic and copies ran while one was open for 10% -> 11% of each run, Pallas kernels for 18% -> 19%
where the time goes in v5:
time: 412 us; the launch traced here: 410 us
  waiting for transfers between devices  197 us (48%)
  Pallas kernels  89.4 us (22%)
  starting transfers between devices  48.3 us (12%)
  local copies, waits for them, and re-layouts  30.7 us (7%)
  other arithmetic  29 us (7%)
  between operations  13.7 us (3%)
    ppermute x34, waiting for transfers between devices, send(): return lax.ppermute(value, AXES, pairs)  165 us
    ppermute x34, starting transfers between devices, send(): return lax.ppermute(value, AXES, pairs)  47.9 us
    pallas_call x3, Pallas kernels, project(): pl.pallas_call(project_kernel, out_shape=jax.ShapeDtypeStruct((width, row...  40.3 us
    all_gather x4, waiting for transfers between devices, cross(): return lax.all_gather(stack, 'ctx', axis_index_groups=groups, tiled=True)  32 us
    pallas_call x1, Pallas kernels, long_filter_part(): pl.pallas_call(functools.partial(filter_kernel, span), out_shape=jax.Shap...  14.1 us
    pallas_call x1, Pallas kernels, prepare(): pl.pallas_call(functools.partial(prepare_kernel, per_part), out_shape=jax...  13.5 us
    pallas_call x1, Pallas kernels, output_sums(): pl.pallas_call(functools.partial(output_kernel, len(mixed), chunks), out_...  12 us
    pallas_call x1, Pallas kernels, mix(): pl.pallas_call(functools.partial(mix_kernel, span), out_shape=jax.ShapeDt...  9.49 us
  transfers between devices with their start and end apart: 38, of which 17 were waited for; matrix products, arithmetic and copies ran while one was open for 11% of the time, Pallas kernels for 19%

profile of v5, /device:TPU:17, one launch (start us, length us, event | category | flops | bytes accessed | tf_op | source)
XLA Modules:
  0.0 409.9 jit_solution(6001496117495637576)
XLA Ops:
  28.8 8.7 %collective-permute-done.refs_0_ = bf16[768,512]{1,0:T(8,128)(2,1)} collective-permute-done((bf16[768,512]{1,0:T(8,128)(2,1)}, bf16[768,512]{1,0:T(8,128)(2,1)}, u32[]{:S(2)}, u32[]{:S(2)}) %collective-permute-start) | collective-permute-done | bytes 786464 | tf_op jit(solution)/shard_map/ppermute | solution.py:29
  37.4 13.3 %collective-permute-done.11.refs_1_ = bf16[3,512,512]{2,1,0:T(8,128)(2,1)} collective-permute-done((bf16[3,512,512]{2,1,0:T(8,128)(2,1)}, bf16[3,512,512]{2,1,0:T(8,128)(2,1)}, u32[]{:S(2)}, u32[]{:S(2)}) %collective-permute-start.11) | collective-permute-done | bytes 1572896 | tf_op jit(solution)/shard_map/ppermute | solution.py:29
  52.0 10.4 %collective-permute-done.3 = bf16[512,512]{1,0:T(8,128)(2,1)S(1)} collective-permute-done((bf16[512,512]{1,0:T(8,128)(2,1)S(1)}, bf16[512,512]{1,0:T(8,128)(2,1)S(1)}, u32[]{:S(2)}, u32[]{:S(2)}) %collective-permute-start.3) | collective-permute-done | bytes 524320 | tf_op jit(solution)/shard_map/ppermute | solution.py:29
  62.4 9.4 %collective-permute-done.16 = bf16[512,512]{1,0:T(8,128)(2,1)S(1)} collective-permute-done((bf16[512,512]{1,0:T(8,128)(2,1)S(1)}, bf16[512,512]{1,0:T(8,128)(2,1)S(1)}, u32[]{:S(2)}, u32[]{:S(2)}) %collective-permute-start.16) | collective-permute-done | bytes 524320 | tf_op jit(solution)/shard_map/ppermute | solution.py:29
  73.2 3.2 collective-permute-start.1
  80.9 13.5 %collective-permute-done.1.refs_1_ = bf16[768,512]{1,0:T(8,128)(2,1)S(1)} collective-permute-done((bf16[768,512]{1,0:T(8,128)(2,1)}, bf16[768,512]{1,0:T(8,128)(2,1)S(1)}, u32[]{:S(2)}, u32[]{:S(2)}) %collective-permute-start.1) | collective-permute-done | bytes 786464 | tf_op jit(solution)/shard_map/ppermute | solution.py:29
  94.4 3.5 collective-permute-start.14
  97.8 23.6 %collective-permute-done.17 = bf16[512,512]{1,0:T(8,128)(2,1)S(1)} collective-permute-done((bf16[512,512]{1,0:T(8,128)(2,1)S(1)}, bf16[512,512]{1,0:T(8,128)(2,1)S(1)}, u32[]{:S(2)}, u32[]{:S(2)}) %collective-permute-start.17) | collective-permute-done | bytes 524320 | tf_op jit(solution)/shard_map/ppermute | solution.py:29
  121.4 4.3 %collective-permute-done.14 = bf16[512,512]{1,0:T(8,128)(2,1)S(1)} collective-permute-done((bf16[512,512]{1,0:T(8,128)(2,1)}, bf16[512,512]{1,0:T(8,128)(2,1)S(1)}, u32[]{:S(2)}, u32[]{:S(2)}) %collective-permute-start.14) | collective-permute-done | bytes 524320 | tf_op jit(solution)/shard_map/ppermute | solution.py:29
  134.0 21.0 %collective-permute-done.5 = bf16[512,512]{1,0:T(8,128)(2,1)} collective-permute-done((bf16[512,512]{1,0:T(8,128)(2,1)}, bf16[512,512]{1,0:T(8,128)(2,1)}, u32[]{:S(2)}, u32[]{:S(2)}) %collective-permute-start.5) | collective-permute-done | bytes 524320 | tf_op jit(solution)/shard_map/ppermute | solution.py:29
  160.6 13.5 %shard_map.73.tokens = bf16[4096,1536]{1,0:T(8,128)(2,1)} custom-call(s32[8]{0:T(128)} %stack.158.order, s32[2]{0:T(128)} %pad_add_fusion.flags, bf16[768,4096]{1,0:T(8,128)(2,1)} %own.1, bf16[768,512]{1,0:T(8,128)(2,1)} %collective-permute-done.refs_0_, bf16[768,512]{1,0:T(8,128)(2,1)} %copy-done.6, bf16[768,512]{1,0:T(8,128)(2,1)} %collective-permute-done.2.refs_2_, ...), custom_call_target="tpu_custom_call" | custom-call | bytes 25165824 | tf_op jit(solution)/shard_map/pallas_call | solution.py:91
  183.3 3.1 collective-permute-start.19
  187.7 8.4 %collective-permute-done.15 = bf16[512,512]{1,0:T(8,128)(2,1)S(1)} collective-permute-done((bf16[512,512]{1,0:T(8,128)(2,1)S(1)}, bf16[512,512]{1,0:T(8,128)(2,1)S(1)}, u32[]{:S(2)}, u32[]{:S(2)}) %collective-permute-start.15) | collective-permute-done | bytes 524320 | tf_op jit(solution)/shard_map/ppermute | solution.py:29
  198.7 13.7 %shard_map.74.k = bf16[512,1536]{1,0:T(8,128)(2,1)} custom-call(bf16[4096,1536]{1,0:T(8,128)(2,1)} %shard_map.73.tokens, bf16[3,512,512]{2,1,0:T(8,128)(2,1)} %pad_maximum_fusion.1.refs_0_, bf16[3,512,512]{2,1,0:T(8,128)(2,1)} %collective-permute-done.11.refs_1_, bf16[6,512,512]{2,1,0:T(8,128)(2,1)} %all-gather.7.cloned.1.call-done.refs_2_), custom_call_target="tpu_custom_call" | custom-call | flops 6442450944 | bytes 22544384 | tf_op jit(solution)/shard_map/pallas_call | solution.py:121
  214.8 13.3 %shard_map.75.v = bf16[512,1536]{1,0:T(8,128)(2,1)} custom-call(bf16[4096,1536]{1,0:T(8,128)(2,1)} %shard_map.73.tokens, bf16[3,512,512]{2,1,0:T(8,128)(2,1)} %pad_maximum_fusion.1.refs_0_, bf16[3,512,512]{2,1,0:T(8,128)(2,1)} %collective-permute-done.11.refs_1_, bf16[6,512,512]{2,1,0:T(8,128)(2,1)} %all-gather.9.cloned.1.call-done.refs_2_), custom_call_target="tpu_custom_call" | custom-call | flops 6442450944 | bytes 22544384 | tf_op jit(solution)/shard_map/pallas_call | solution.py:121
  239.3 13.5 %all-gather.5.cloned.1.call-done.refs_2_ = bf16[6,512,512]{2,1,0:T(8,128)(2,1)} async-done(((bf16[3,512,512]{2,1,0:T(8,128)(2,1)}), bf16[6,512,512]{2,1,0:T(8,128)(2,1)}) %all-gather.5.cloned.1.call-update) | async-done | bytes 3145744 | tf_op jit(solution)/shard_map/all_gather | solution.py:71
  252.8 13.2 %shard_map.76.q = bf16[512,1536]{1,0:T(8,128)(2,1)} custom-call(bf16[4096,1536]{1,0:T(8,128)(2,1)} %shard_map.73.tokens, bf16[3,512,512]{2,1,0:T(8,128)(2,1)} %pad_maximum_fusion.1.refs_0_, bf16[3,512,512]{2,1,0:T(8,128)(2,1)} %collective-permute-done.11.refs_1_, bf16[6,512,512]{2,1,0:T(8,128)(2,1)} %all-gather.5.cloned.1.call-done.refs_2_), custom_call_target="tpu_custom_call" | custom-call | flops 6442450944 | bytes 22544384 | tf_op jit(solution)/shard_map/pallas_call | solution.py:121
  274.0 14.1 %shard_map.77.filtered = f32[512,1536]{1,0:T(8,128)} custom-call(bf16[512,1536]{1,0:T(8,128)(2,1)} %shard_map.74.k, bf16[512,1536]{1,0:T(8,128)(2,1)} %shard_map.75.v, bf16[512,256]{1,0:T(8,128)(2,1)} %fusion.19.k_rim, bf16[512,256]{1,0:T(8,128)(2,1)} %fusion.20.v_rim, bf16[512,256]{1,0:T(8,128)(2,1)} %pad_maximum_fusion.9.before, ...), custom_call_target="tpu_custom_call" | custom-call | flops 446693376 | bytes 8388608 | tf_op jit(solution)/shard_map/pallas_call | solution.py:175
  289.0 9.5 %shard_map.78.refs_0_ = bf16[1536,512]{1,0:T(8,128)(2,1)} custom-call(bf16[512,1536]{1,0:T(8,128)(2,1)} %shard_map.76.q, bf16[512,256]{1,0:T(8,128)(2,1)} %fusion.18.q_rim, f32[512,1536]{1,0:T(8,128)} %shard_map.77.filtered, f32[512,24]{1,0:T(8,128)} %pad.29.coefficients), custom_call_target="tpu_custom_call" | custom-call | flops 11010048 | bytes 6291456 | tf_op jit(solution)/shard_map/pallas_call | solution.py:203
  299.7 3.2 collective-permute-done.27.refs_1_
  302.9 18.5 %all-gather.11.cloned.1.call-done.refs_4_ = bf16[6,1024,256]{2,1,0:T(8,128)(2,1)} async-done(((bf16[3,1024,256]{2,1,0:T(8,128)(2,1)}), bf16[6,1024,256]{2,1,0:T(8,128)(2,1)}) %all-gather.11.cloned.1.call-update) | async-done | bytes 3145744 | tf_op jit(solution)/shard_map/all_gather | solution.py:71
  321.4 12.0 %shard_map.79 = (bf16[8,1536,128]{2,1,0:T(8,128)(2,1)}, bf16[8,1536,128]{2,1,0:T(8,128)(2,1)}) custom-call(s32[8]{0:T(128)} %stack.158.order, bf16[1536,512]{1,0:T(8,128)(2,1)} %shard_map.78.refs_0_, bf16[1536,512]{1,0:T(8,128)(2,1)} %copy-done.13, bf16[1,1024,256]{2,1,0:T(8,128)(2,1)} %bitcast.222, bf16[1,1024,256]{2,1,0:T(8,128)(2,1)} %bitcast.88.refs_3_, ...), custom_call_target="tpu_custom_call" | custom-call | flops 6442450944 | bytes 13631488 | tf_op jit(solution)/shard_map/pallas_call | solution.py:238
  340.0 31.9 %collective-permute-done.31 = bf16[8,768,128]{2,1,0:T(8,128)(2,1)} collective-permute-done((bf16[8,768,128]{2,1,0:T(8,128)(2,1)}, bf16[8,768,128]{2,1,0:T(8,128)(2,1)}, u32[]{:S(2)}, u32[]{:S(2)}) %collective-permute-start.31) | collective-permute-done | bytes 1572896 | tf_op jit(solution)/shard_map/ppermute | solution.py:29
  378.7 13.1 %collective-permute-done.32 = bf16[8,384,128]{2,1,0:T(8,128)(2,1)S(1)} collective-permute-done((bf16[8,384,128]{2,1,0:T(8,128)(2,1)S(1)}, bf16[8,384,128]{2,1,0:T(8,128)(2,1)S(1)}, u32[]{:S(2)}, u32[]{:S(2)}) %collective-permute-start.32) | collective-permute-done | bytes 786464 | tf_op jit(solution)/shard_map/ppermute | solution.py:29
  (170 shorter events, 104.4 us)
Async XLA Ops:
  6.5 192.2 %all-gather.7.cloned.1.call-start = ((), (), s32[]{:S(2)}) async-start(), calls=%async_computation.1 | async-start | bytes 4718592 | tf_op jit(solution)/shard_map/all_gather | solution.py:71
  15.1 35.6 %collective-permute-start.11 = (bf16[3,512,512]{2,1,0:T(8,128)(2,1)}, bf16[3,512,512]{2,1,0:T(8,128)(2,1)}, u32[]{:S(2)}, u32[]{:S(2)}) collective-permute-start(bf16[3,512,512]{2,1,0:T(8,128)(2,1)} %pad_maximum_fusion.1.refs_0_), channel_id=1, source_target_pairs={{0,4},{1,5},{2,6},{3,7},{4,0},{5,1},{6,2},{7,3},{8,12},{9,13},{10,... | collective-permute-start | bytes 4718600 | tf_op jit(solution)/shard_map/ppermute | solution.py:29
  26.4 36.0 %collective-permute-start.3 = (bf16[512,512]{1,0:T(8,128)(2,1)S(1)}, bf16[512,512]{1,0:T(8,128)(2,1)S(1)}, u32[]{:S(2)}, u32[]{:S(2)}) collective-permute-start(bf16[512,512]{1,0:T(8,128)(2,1)S(1)} %bitcast.216), channel_id=1, source_target_pairs={{0,24},{1,25},{2,26},{3,27},{4,28},{5,29},{6,30},{7,31},{8,16},{9,... | collective-permute-start | bytes 1572872 | tf_op jit(solution)/shard_map/ppermute | solution.py:29
  26.5 45.3 %collective-permute-start.16 = (bf16[512,512]{1,0:T(8,128)(2,1)S(1)}, bf16[512,512]{1,0:T(8,128)(2,1)S(1)}, u32[]{:S(2)}, u32[]{:S(2)}) collective-permute-start(bf16[512,512]{1,0:T(8,128)(2,1)S(1)} %bitcast.212), channel_id=1, source_target_pairs={{0,16},{1,17},{2,18},{3,19},{4,20},{5,21},{6,22},{7,23},{8,24},{9,... | collective-permute-start | bytes 1572872 | tf_op jit(solution)/shard_map/ppermute | solution.py:29
  50.7 21.1 %collective-permute-start.13 = (bf16[512,512]{1,0:T(8,128)(2,1)S(1)}, bf16[512,512]{1,0:T(8,128)(2,1)S(1)}, u32[]{:S(2)}, u32[]{:S(2)}) collective-permute-start(bf16[512,512]{1,0:T(8,128)(2,1)S(1)} %bitcast.217), channel_id=1, source_target_pairs={{0,8},{1,9},{2,10},{3,11},{4,12},{5,13},{6,14},{7,15},{8,0},{9,1},... | collective-permute-start | bytes 1572872 | tf_op jit(solution)/shard_map/ppermute | solution.py:29
  73.2 141.6 %all-gather.9.cloned.1.call-start = ((), (), s32[]{:S(2)}) async-start(), calls=%async_computation.2 | async-start | bytes 4718592 | tf_op jit(solution)/shard_map/all_gather | solution.py:71
  73.2 21.1 %collective-permute-start.1 = (bf16[768,512]{1,0:T(8,128)(2,1)}, bf16[768,512]{1,0:T(8,128)(2,1)S(1)}, u32[]{:S(2)}, u32[]{:S(2)}) collective-permute-start(bf16[768,512]{1,0:T(8,128)(2,1)} %get-tuple-element.43), channel_id=1, source_target_pairs={{0,8},{1,9},{2,10},{3,11},{4,12},{5,13},{6,14},{7,15},{8,0},{9,1},... | collective-permute-start | bytes 2359304 | tf_op jit(solution)/shard_map/ppermute | solution.py:29
  78.9 42.5 %collective-permute-start.17 = (bf16[512,512]{1,0:T(8,128)(2,1)S(1)}, bf16[512,512]{1,0:T(8,128)(2,1)S(1)}, u32[]{:S(2)}, u32[]{:S(2)}) collective-permute-start(bf16[512,512]{1,0:T(8,128)(2,1)S(1)} %bitcast.209), channel_id=1, source_target_pairs={{0,16},{1,17},{2,18},{3,19},{4,20},{5,21},{6,22},{7,23},{8,24},{9,... | collective-permute-start | bytes 1572872 | tf_op jit(solution)/shard_map/ppermute | solution.py:29
  94.4 31.3 %collective-permute-start.14 = (bf16[512,512]{1,0:T(8,128)(2,1)}, bf16[512,512]{1,0:T(8,128)(2,1)S(1)}, u32[]{:S(2)}, u32[]{:S(2)}) collective-permute-start(bf16[512,512]{1,0:T(8,128)(2,1)} %bitcast.219), channel_id=1, source_target_pairs={{0,8},{1,9},{2,10},{3,11},{4,12},{5,13},{6,14},{7,15},{8,0},{9,1},... | collective-permute-start | bytes 1572872 | tf_op jit(solution)/shard_map/ppermute | solution.py:29
  127.2 125.6 %all-gather.5.cloned.1.call-start = ((), (), s32[]{:S(2)}) async-start(), calls=%async_computation | async-start | bytes 4718592 | tf_op jit(solution)/shard_map/all_gather | solution.py:71
  127.2 28.3 %collective-permute-start.8 = (bf16[768,512]{1,0:T(8,128)(2,1)S(1)}, bf16[768,512]{1,0:T(8,128)(2,1)}, u32[]{:S(2)}, u32[]{:S(2)}) collective-permute-start(bf16[768,512]{1,0:T(8,128)(2,1)S(1)} %collective-permute-done.1.refs_1_), channel_id=1, source_target_pairs={{0,2},{1,3},{2,0},{3,1},{4,6},{5,7},{6,4},{7,5},{8,10},{9,11},{10,... | collective-permute-start | bytes 2359304 | tf_op jit(solution)/shard_map/ppermute | solution.py:29
  129.6 25.4 %collective-permute-start.5 = (bf16[512,512]{1,0:T(8,128)(2,1)}, bf16[512,512]{1,0:T(8,128)(2,1)}, u32[]{:S(2)}, u32[]{:S(2)}) collective-permute-start(bf16[512,512]{1,0:T(8,128)(2,1)} %bitcast.214), channel_id=1, source_target_pairs={{0,24},{1,25},{2,26},{3,27},{4,28},{5,29},{6,30},{7,31},{8,16},{9,... | collective-permute-start | bytes 1572872 | tf_op jit(solution)/shard_map/ppermute | solution.py:29
  131.2 29.4 %collective-permute-start.2 = (bf16[768,512]{1,0:T(8,128)(2,1)}, bf16[768,512]{1,0:T(8,128)(2,1)}, u32[]{:S(2)}, u32[]{:S(2)}) collective-permute-start(bf16[768,512]{1,0:T(8,128)(2,1)} %collective-permute-done.refs_0_), channel_id=1, source_target_pairs={{0,1},{1,0},{2,3},{3,2},{4,5},{5,4},{6,7},{7,6},{8,9},{9,8},{10,11... | collective-permute-start | bytes 2359304 | tf_op jit(solution)/shard_map/ppermute | solution.py:29
  160.5 22.8 %collective-permute-start.18 = (bf16[512,512]{1,0:T(8,128)(2,1)S(1)}, bf16[512,512]{1,0:T(8,128)(2,1)S(1)}, u32[]{:S(2)}, u32[]{:S(2)}) collective-permute-start(bf16[512,512]{1,0:T(8,128)(2,1)S(1)} %bitcast.207), channel_id=1, source_target_pairs={{0,16},{1,17},{2,18},{3,19},{4,20},{5,21},{6,22},{7,23},{8,24},{9,... | collective-permute-start | bytes 1572872 | tf_op jit(solution)/shard_map/ppermute | solution.py:29
  174.1 22.0 %collective-permute-start.15 = (bf16[512,512]{1,0:T(8,128)(2,1)S(1)}, bf16[512,512]{1,0:T(8,128)(2,1)S(1)}, u32[]{:S(2)}, u32[]{:S(2)}) collective-permute-start(bf16[512,512]{1,0:T(8,128)(2,1)S(1)} %bitcast.215), channel_id=1, source_target_pairs={{0,8},{1,9},{2,10},{3,11},{4,12},{5,13},{6,14},{7,15},{8,0},{9,1},... | collective-permute-start | bytes 1572872 | tf_op jit(solution)/shard_map/ppermute | solution.py:29
  180.6 47.6 %collective-permute-start.21 = (bf16[1024,256]{1,0:T(8,128)(2,1)S(1)}, bf16[1024,256]{1,0:T(8,128)(2,1)}, u32[]{:S(2)}, u32[]{:S(2)}) collective-permute-start(bf16[1024,256]{1,0:T(8,128)(2,1)S(1)} %bitcast.220), channel_id=1, source_target_pairs={{0,4},{1,5},{2,6},{3,7},{4,0},{5,1},{6,2},{7,3},{8,12},{9,13},{10,... | collective-permute-start | bytes 1572872 | tf_op jit(solution)/shard_map/ppermute | solution.py:29
  183.3 56.0 %collective-permute-start.19 = (bf16[1024,256]{1,0:T(8,128)(2,1)S(1)}, bf16[1024,256]{1,0:T(8,128)(2,1)S(1)}, u32[]{:S(2)}, u32[]{:S(2)}) collective-permute-start(bf16[1024,256]{1,0:T(8,128)(2,1)S(1)} %bitcast.221), channel_id=1, source_target_pairs={{0,16},{1,17},{2,18},{3,19},{4,20},{5,21},{6,22},{7,23},{8,24},{9,... | collective-permute-start | bytes 1572872 | tf_op jit(solution)/shard_map/ppermute | solution.py:29
  186.4 52.9 %collective-permute-start.20 = (bf16[1024,256]{1,0:T(8,128)(2,1)}, bf16[1024,256]{1,0:T(8,128)(2,1)S(1)}, u32[]{:S(2)}, u32[]{:S(2)}) collective-permute-start(bf16[1024,256]{1,0:T(8,128)(2,1)} %bitcast.39), channel_id=1, source_target_pairs={{0,24},{1,25},{2,26},{3,27},{4,28},{5,29},{6,30},{7,31},{8,16},{9,... | collective-permute-start | bytes 1572872 | tf_op jit(solution)/shard_map/ppermute | solution.py:29
  198.4 123.0 %all-gather.11.cloned.1.call-start = ((), (), s32[]{:S(2)}) async-start(), calls=%async_computation.3 | async-start | bytes 4718592 | tf_op jit(solution)/shard_map/all_gather | solution.py:71
  228.2 24.6 %collective-permute-start.22 = (bf16[1024,256]{1,0:T(8,128)(2,1)}, bf16[1024,256]{1,0:T(8,128)(2,1)}, u32[]{:S(2)}, u32[]{:S(2)}) collective-permute-start(bf16[1024,256]{1,0:T(8,128)(2,1)} %bitcast.39), channel_id=1, source_target_pairs={{0,8},{1,9},{2,10},{3,11},{4,12},{5,13},{6,14},{7,15},{8,0},{9,1},... | collective-permute-start | bytes 1572872 | tf_op jit(solution)/shard_map/ppermute | solution.py:29
  235.4 33.4 %collective-permute-start.25 = (bf16[144,512]{0,1:T(8,128)(2,1)S(1)}, bf16[144,512]{0,1:T(8,128)(2,1)S(1)}, u32[]{:S(2)}, u32[]{:S(2)}) collective-permute-start(bf16[144,512]{0,1:T(8,128)(2,1)S(1)} %pad_maximum_fusion.8), channel_id=1, source_target_pairs={{4,16},{5,17},{6,18},{7,19},{12,24},{13,25},{14,26},{15,27}} | collective-permute-start | bytes 442376 | tf_op jit(solution)/shard_map/ppermute | solution.py:29
  238.9 29.9 %collective-permute-start.26 = (bf16[2,144,512]{1,2,0:T(8,128)(2,1)S(1)}, bf16[2,144,512]{1,2,0:T(8,128)(2,1)S(1)}, u32[]{:S(2)}, u32[]{:S(2)}) collective-permute-start(bf16[2,144,512]{1,2,0:T(8,128)(2,1)S(1)} %pad_maximum_fusion.6), channel_id=1, source_target_pairs={{0,4},{1,5},{2,6},{3,7},{4,0},{5,1},{6,2},{7,3},{8,12},{9,13},{10,... | collective-permute-start | bytes 884744 | tf_op jit(solution)/shard_map/ppermute | solution.py:29
  336.3 35.6 %collective-permute-start.31 = (bf16[8,768,128]{2,1,0:T(8,128)(2,1)}, bf16[8,768,128]{2,1,0:T(8,128)(2,1)}, u32[]{:S(2)}, u32[]{:S(2)}) collective-permute-start(bf16[8,768,128]{2,1,0:T(8,128)(2,1)} %dynamic-slice_bitcast_fusion), channel_id=1, source_target_pairs={{0,8},{1,9},{2,10},{3,11},{4,12},{5,13},{6,14},{7,15},{8,0},{9,1},... | collective-permute-start | bytes 4718600 | tf_op jit(solution)/shard_map/ppermute | solution.py:29
  338.8 36.7 %collective-permute-start.28 = (bf16[16,384,128]{2,1,0:T(8,128)(2,1)}, bf16[16,384,128]{2,1,0:T(8,128)(2,1)}, u32[]{:S(2)}, u32[]{:S(2)}) collective-permute-start(bf16[16,384,128]{2,1,0:T(8,128)(2,1)} %dynamic-slice_bitcast_fusion.1), channel_id=1, source_target_pairs={{0,2},{1,3},{2,0},{3,1},{4,6},{5,7},{6,4},{7,5},{8,10},{9,11},{10,... | collective-permute-start | bytes 4718600 | tf_op jit(solution)/shard_map/ppermute | solution.py:29
  (30 other events, 418.7 us)
Sparse Core Ops, SparseCore 0:
  73.3 49.7 all-gather.6
  127.3 48.8 all-gather.8
  198.6 54.1 all-gather.4
  271.4 49.9 all-gather.10

commit v6 on v5

--- a/solution.py
+++ b/solution.py
@@ -399,8 +399,8 @@
         )
         for end in ends
     ]
-    q = project(tokens, entries(0, after(q_cross, *out_held.values())))
-    before = halos(jnp.stack(tails), q)
+    before = halos(jnp.stack(tails))
+    q = project(tokens, entries(0, after(q_cross, *out_held.values(), *before)))
     edges = halos(jnp.stack([q[:, end - edge : end].T for end in ends]))
     filtered = long_filter_part(
         span,

time: 412 us -> 446 us (1.083)
  waiting for transfers between devices: 197 us -> 221 us
  local copies, waits for them, and re-layouts: 30.7 us -> 35.8 us
  starting transfers between devices: 48.3 us -> 53.2 us
    ppermute x34, waiting for transfers between devices: 165 us -> 216 us  [send(): return lax.ppermute(value, AXES, pairs)]
    all_gather x4, waiting for transfers between devices: 32 us -> 5.53 us  [cross(): return lax.all_gather(stack, 'ctx', axis_index_groups=groups, tiled=True)]
    ppermute x34, starting transfers between devices: 47.9 us -> 52.9 us  [send(): return lax.ppermute(value, AXES, pairs)]
  transfers between devices with their start and end apart: 38 -> 38, of which waited for: 17 -> 20; matrix products, arithmetic and copies ran while one was open for 11% -> 10% of each run, Pallas kernels for 19% -> 17%
where the time goes in v6:
time: 446 us; the launch traced here: 444 us
  waiting for transfers between devices  221 us (50%)
  Pallas kernels  89.7 us (20%)
  starting transfers between devices  53.2 us (12%)
  local copies, waits for them, and re-layouts  35.8 us (8%)
  other arithmetic  28.7 us (6%)
  between operations  13.8 us (3%)
    ppermute x34, waiting for transfers between devices, send(): return lax.ppermute(value, AXES, pairs)  216 us
    ppermute x34, starting transfers between devices, send(): return lax.ppermute(value, AXES, pairs)  52.9 us
    pallas_call x3, Pallas kernels, project(): pl.pallas_call(project_kernel, out_shape=jax.ShapeDtypeStruct((width, row...  40.8 us
    pallas_call x1, Pallas kernels, long_filter_part(): pl.pallas_call(functools.partial(filter_kernel, span), out_shape=jax.Shap...  14 us
    pallas_call x1, Pallas kernels, prepare(): pl.pallas_call(functools.partial(prepare_kernel, per_part), out_shape=jax...  13.4 us
    pallas_call x1, Pallas kernels, output_sums(): pl.pallas_call(functools.partial(output_kernel, len(mixed), chunks), out_...  12.1 us
    pallas_call x1, Pallas kernels, mix(): pl.pallas_call(functools.partial(mix_kernel, span), out_shape=jax.ShapeDt...  9.49 us
  transfers between devices with their start and end apart: 38, of which 20 were waited for; matrix products, arithmetic and copies ran while one was open for 10% of the time, Pallas kernels for 17%

profile of v6, /device:TPU:17, one launch (start us, length us, event | category | flops | bytes accessed | tf_op | source)
XLA Modules:
  0.0 444.4 jit_solution(2921284748056200585)
XLA Ops:
  30.5 8.8 %collective-permute-done.refs_0_ = bf16[768,512]{1,0:T(8,128)(2,1)} collective-permute-done((bf16[768,512]{1,0:T(8,128)(2,1)}, bf16[768,512]{1,0:T(8,128)(2,1)}, u32[]{:S(2)}, u32[]{:S(2)}) %collective-permute-start) | collective-permute-done | bytes 786464 | tf_op jit(solution)/shard_map/ppermute | solution.py:29
  39.3 13.3 %collective-permute-done.11.refs_1_ = bf16[3,512,512]{2,1,0:T(8,128)(2,1)} collective-permute-done((bf16[3,512,512]{2,1,0:T(8,128)(2,1)}, bf16[3,512,512]{2,1,0:T(8,128)(2,1)}, u32[]{:S(2)}, u32[]{:S(2)}) %collective-permute-start.11) | collective-permute-done | bytes 1572896 | tf_op jit(solution)/shard_map/ppermute | solution.py:29
  53.8 10.1 %collective-permute-done.3 = bf16[512,512]{1,0:T(8,128)(2,1)S(1)} collective-permute-done((bf16[512,512]{1,0:T(8,128)(2,1)S(1)}, bf16[512,512]{1,0:T(8,128)(2,1)S(1)}, u32[]{:S(2)}, u32[]{:S(2)}) %collective-permute-start.3) | collective-permute-done | bytes 524320 | tf_op jit(solution)/shard_map/ppermute | solution.py:29
  63.9 9.6 %collective-permute-done.16 = bf16[512,512]{1,0:T(8,128)(2,1)S(1)} collective-permute-done((bf16[512,512]{1,0:T(8,128)(2,1)S(1)}, bf16[512,512]{1,0:T(8,128)(2,1)S(1)}, u32[]{:S(2)}, u32[]{:S(2)}) %collective-permute-start.16) | collective-permute-done | bytes 524320 | tf_op jit(solution)/shard_map/ppermute | solution.py:29
  83.5 12.5 %collective-permute-done.1.refs_1_ = bf16[768,512]{1,0:T(8,128)(2,1)S(1)} collective-permute-done((bf16[768,512]{1,0:T(8,128)(2,1)S(1)}, bf16[768,512]{1,0:T(8,128)(2,1)S(1)}, u32[]{:S(2)}, u32[]{:S(2)}) %collective-permute-start.1) | collective-permute-done | bytes 786464 | tf_op jit(solution)/shard_map/ppermute | solution.py:29
  99.6 24.4 %collective-permute-done.17 = bf16[512,512]{1,0:T(8,128)(2,1)S(1)} collective-permute-done((bf16[512,512]{1,0:T(8,128)(2,1)S(1)}, bf16[512,512]{1,0:T(8,128)(2,1)S(1)}, u32[]{:S(2)}, u32[]{:S(2)}) %collective-permute-start.17) | collective-permute-done | bytes 524320 | tf_op jit(solution)/shard_map/ppermute | solution.py:29
  124.0 4.0 collective-permute-done.14
  136.0 21.2 %collective-permute-done.5 = bf16[512,512]{1,0:T(8,128)(2,1)S(1)} collective-permute-done((bf16[512,512]{1,0:T(8,128)(2,1)}, bf16[512,512]{1,0:T(8,128)(2,1)S(1)}, u32[]{:S(2)}, u32[]{:S(2)}) %collective-permute-start.5) | collective-permute-done | bytes 524320 | tf_op jit(solution)/shard_map/ppermute | solution.py:29
  164.6 13.4 %shard_map.73.tokens = bf16[4096,1536]{1,0:T(8,128)(2,1)} custom-call(s32[8]{0:T(128)} %stack.158.order, s32[2]{0:T(128)} %pad_add_fusion.flags, bf16[768,4096]{1,0:T(8,128)(2,1)} %own.1, bf16[768,512]{1,0:T(8,128)(2,1)} %collective-permute-done.refs_0_, bf16[768,512]{1,0:T(8,128)(2,1)} %copy-done.5, bf16[768,512]{1,0:T(8,128)(2,1)} %copy-done.6, ...), custom_call_target="tpu_custom_call" | custom-call | bytes 25165824 | tf_op jit(solution)/shard_map/pallas_call | solution.py:91
  186.7 12.4 %collective-permute-done.15 = bf16[512,512]{1,0:T(8,128)(2,1)S(1)} collective-permute-done((bf16[512,512]{1,0:T(8,128)(2,1)}, bf16[512,512]{1,0:T(8,128)(2,1)S(1)}, u32[]{:S(2)}, u32[]{:S(2)}) %collective-permute-start.15) | collective-permute-done | bytes 524320 | tf_op jit(solution)/shard_map/ppermute | solution.py:29
  200.7 14.1 %shard_map.74.k = bf16[512,1536]{1,0:T(8,128)(2,1)} custom-call(bf16[4096,1536]{1,0:T(8,128)(2,1)} %shard_map.73.tokens, bf16[3,512,512]{2,1,0:T(8,128)(2,1)} %pad_maximum_fusion.1.refs_0_, bf16[3,512,512]{2,1,0:T(8,128)(2,1)} %collective-permute-done.11.refs_1_, bf16[6,512,512]{2,1,0:T(8,128)(2,1)} %all-gather.7.cloned.1.call-done.refs_2_), custom_call_target="tpu_custom_call" | custom-call | flops 6442450944 | bytes 22544384 | tf_op jit(solution)/shard_map/pallas_call | solution.py:121
  217.8 13.5 %shard_map.75.v = bf16[512,1536]{1,0:T(8,128)(2,1)} custom-call(bf16[4096,1536]{1,0:T(8,128)(2,1)} %shard_map.73.tokens, bf16[3,512,512]{2,1,0:T(8,128)(2,1)} %pad_maximum_fusion.1.refs_0_, bf16[3,512,512]{2,1,0:T(8,128)(2,1)} %collective-permute-done.11.refs_1_, bf16[6,512,512]{2,1,0:T(8,128)(2,1)} %all-gather.9.cloned.1.call-done.refs_2_), custom_call_target="tpu_custom_call" | custom-call | flops 6442450944 | bytes 22544384 | tf_op jit(solution)/shard_map/pallas_call | solution.py:121
  247.2 3.9 collective-permute-done.23
  251.1 11.3 %collective-permute-done.24 = bf16[2,144,512]{1,2,0:T(8,128)(2,1)S(1)} collective-permute-done((bf16[2,144,512]{1,2,0:T(8,128)(2,1)}, bf16[2,144,512]{1,2,0:T(8,128)(2,1)S(1)}, u32[]{:S(2)}, u32[]{:S(2)}) %collective-permute-start.24) | collective-permute-done | bytes 294944 | tf_op jit(solution)/shard_map/ppermute | solution.py:29
  263.6 16.0 %collective-permute-done.19 = bf16[1024,256]{1,0:T(8,128)(2,1)S(1)} collective-permute-done((bf16[1024,256]{1,0:T(8,128)(2,1)}, bf16[1024,256]{1,0:T(8,128)(2,1)S(1)}, u32[]{:S(2)}, u32[]{:S(2)}) %collective-permute-start.19) | collective-permute-done | bytes 524320 | tf_op jit(solution)/shard_map/ppermute | solution.py:29
  279.7 12.7 %collective-permute-done.20 = bf16[1024,256]{1,0:T(8,128)(2,1)S(1)} collective-permute-done((bf16[1024,256]{1,0:T(8,128)(2,1)S(1)}, bf16[1024,256]{1,0:T(8,128)(2,1)S(1)}, u32[]{:S(2)}, u32[]{:S(2)}) %collective-permute-start.20) | collective-permute-done | bytes 524320 | tf_op jit(solution)/shard_map/ppermute | solution.py:29
  295.3 13.2 %shard_map.76.q = bf16[512,1536]{1,0:T(8,128)(2,1)} custom-call(bf16[4096,1536]{1,0:T(8,128)(2,1)} %shard_map.73.tokens, bf16[3,512,512]{2,1,0:T(8,128)(2,1)} %pad_maximum_fusion.1.refs_0_, bf16[3,512,512]{2,1,0:T(8,128)(2,1)} %collective-permute-done.11.refs_1_, bf16[6,512,512]{2,1,0:T(8,128)(2,1)} %all-gather.5.cloned.1.call-done.refs_2_), custom_call_target="tpu_custom_call" | custom-call | flops 6442450944 | bytes 22544384 | tf_op jit(solution)/shard_map/pallas_call | solution.py:121
  311.3 10.7 %collective-permute-start.26 = (bf16[2,8,512]{1,2,0:T(8,128)(2,1)S(1)}, bf16[2,8,512]{1,2,0:T(8,128)(2,1)S(1)}, u32[]{:S(2)}, u32[]{:S(2)}) collective-permute-start(bf16[2,8,512]{1,2,0:T(8,128)(2,1)S(1)} %pad_maximum_fusion.8), channel_id=1, source_target_pairs={{0,4},{1,5},{2,6},{3,7},{4,0},{5,1},{6,2},{7,3},{8,12},{9,13},{10,... | collective-permute-start | bytes 49160 | tf_op jit(solution)/shard_map/ppermute | solution.py:29
  321.9 14.0 %shard_map.77.filtered = f32[512,1536]{1,0:T(8,128)} custom-call(bf16[512,1536]{1,0:T(8,128)(2,1)} %shard_map.74.k, bf16[512,1536]{1,0:T(8,128)(2,1)} %shard_map.75.v, bf16[512,256]{1,0:T(8,128)(2,1)} %fusion.19.k_rim, bf16[512,256]{1,0:T(8,128)(2,1)} %fusion.20.v_rim, bf16[512,256]{1,0:T(8,128)(2,1)} %pad_maximum_fusion.9.before, ...), custom_call_target="tpu_custom_call" | custom-call | flops 446693376 | bytes 8388608 | tf_op jit(solution)/shard_map/pallas_call | solution.py:175
  336.8 9.5 %shard_map.78.refs_0_ = bf16[1536,512]{1,0:T(8,128)(2,1)} custom-call(bf16[512,1536]{1,0:T(8,128)(2,1)} %shard_map.76.q, bf16[512,256]{1,0:T(8,128)(2,1)} %fusion.18.q_rim, f32[512,1536]{1,0:T(8,128)} %shard_map.77.filtered, f32[512,24]{1,0:T(8,128)} %pad.29.coefficients), custom_call_target="tpu_custom_call" | custom-call | flops 11010048 | bytes 6291456 | tf_op jit(solution)/shard_map/pallas_call | solution.py:203
  350.3 5.5 %all-gather.11.cloned.1.call-done.refs_4_ = bf16[6,1024,256]{2,1,0:T(8,128)(2,1)} async-done(((bf16[3,1024,256]{2,1,0:T(8,128)(2,1)}), bf16[6,1024,256]{2,1,0:T(8,128)(2,1)}) %all-gather.11.cloned.1.call-update) | async-done | bytes 3145744 | tf_op jit(solution)/shard_map/all_gather | solution.py:71
  355.8 12.1 %shard_map.79 = (bf16[8,1536,128]{2,1,0:T(8,128)(2,1)}, bf16[8,1536,128]{2,1,0:T(8,128)(2,1)}) custom-call(s32[8]{0:T(128)} %stack.158.order, bf16[1536,512]{1,0:T(8,128)(2,1)} %shard_map.78.refs_0_, bf16[1536,512]{1,0:T(8,128)(2,1)} %copy-done.26, bf16[1,1024,256]{2,1,0:T(8,128)(2,1)} %bitcast.87.refs_2_, bf16[1,1024,256]{2,1,0:T(8,128)(2,1)} %bitcast.88.refs_3_, ...), custom_call_target="tpu_custom_call" | custom-call | flops 6442450944 | bytes 13631488 | tf_op jit(solution)/shard_map/pallas_call | solution.py:238
  373.2 33.1 %collective-permute-done.31 = bf16[8,768,128]{2,1,0:T(8,128)(2,1)} collective-permute-done((bf16[8,768,128]{2,1,0:T(8,128)(2,1)}, bf16[8,768,128]{2,1,0:T(8,128)(2,1)}, u32[]{:S(2)}, u32[]{:S(2)}) %collective-permute-start.31) | collective-permute-done | bytes 1572896 | tf_op jit(solution)/shard_map/ppermute | solution.py:29
  412.2 14.0 %collective-permute-done.32 = bf16[8,384,128]{2,1,0:T(8,128)(2,1)S(1)} collective-permute-done((bf16[8,384,128]{2,1,0:T(8,128)(2,1)S(1)}, bf16[8,384,128]{2,1,0:T(8,128)(2,1)S(1)}, u32[]{:S(2)}, u32[]{:S(2)}) %collective-permute-start.32) | collective-permute-done | bytes 786464 | tf_op jit(solution)/shard_map/ppermute | solution.py:29
  (196 shorter events, 117.2 us)
Async XLA Ops:
  6.5 194.2 %all-gather.7.cloned.1.call-start = ((), (), s32[]{:S(2)}) async-start(), calls=%async_computation.1 | async-start | bytes 4718592 | tf_op jit(solution)/shard_map/all_gather | solution.py:71
  17.0 35.6 %collective-permute-start.11 = (bf16[3,512,512]{2,1,0:T(8,128)(2,1)}, bf16[3,512,512]{2,1,0:T(8,128)(2,1)}, u32[]{:S(2)}, u32[]{:S(2)}) collective-permute-start(bf16[3,512,512]{2,1,0:T(8,128)(2,1)} %pad_maximum_fusion.1.refs_0_), channel_id=1, source_target_pairs={{0,4},{1,5},{2,6},{3,7},{4,0},{5,1},{6,2},{7,3},{8,12},{9,13},{10,... | collective-permute-start | bytes 4718600 | tf_op jit(solution)/shard_map/ppermute | solution.py:29
  28.1 35.8 %collective-permute-start.3 = (bf16[512,512]{1,0:T(8,128)(2,1)S(1)}, bf16[512,512]{1,0:T(8,128)(2,1)S(1)}, u32[]{:S(2)}, u32[]{:S(2)}) collective-permute-start(bf16[512,512]{1,0:T(8,128)(2,1)S(1)} %bitcast.217), channel_id=1, source_target_pairs={{0,24},{1,25},{2,26},{3,27},{4,28},{5,29},{6,30},{7,31},{8,16},{9,... | collective-permute-start | bytes 1572872 | tf_op jit(solution)/shard_map/ppermute | solution.py:29
  28.2 45.3 %collective-permute-start.16 = (bf16[512,512]{1,0:T(8,128)(2,1)S(1)}, bf16[512,512]{1,0:T(8,128)(2,1)S(1)}, u32[]{:S(2)}, u32[]{:S(2)}) collective-permute-start(bf16[512,512]{1,0:T(8,128)(2,1)S(1)} %bitcast.215), channel_id=1, source_target_pairs={{0,16},{1,17},{2,18},{3,19},{4,20},{5,21},{6,22},{7,23},{8,24},{9,... | collective-permute-start | bytes 1572872 | tf_op jit(solution)/shard_map/ppermute | solution.py:29
  52.5 21.0 %collective-permute-start.13 = (bf16[512,512]{1,0:T(8,128)(2,1)S(1)}, bf16[512,512]{1,0:T(8,128)(2,1)S(1)}, u32[]{:S(2)}, u32[]{:S(2)}) collective-permute-start(bf16[512,512]{1,0:T(8,128)(2,1)S(1)} %bitcast.218), channel_id=1, source_target_pairs={{0,8},{1,9},{2,10},{3,11},{4,12},{5,13},{6,14},{7,15},{8,0},{9,1},... | collective-permute-start | bytes 1572872 | tf_op jit(solution)/shard_map/ppermute | solution.py:29
  74.9 143.0 %all-gather.9.cloned.1.call-start = ((), (), s32[]{:S(2)}) async-start(), calls=%async_computation.2 | async-start | bytes 4718592 | tf_op jit(solution)/shard_map/all_gather | solution.py:71
  81.6 42.4 %collective-permute-start.17 = (bf16[512,512]{1,0:T(8,128)(2,1)S(1)}, bf16[512,512]{1,0:T(8,128)(2,1)S(1)}, u32[]{:S(2)}, u32[]{:S(2)}) collective-permute-start(bf16[512,512]{1,0:T(8,128)(2,1)S(1)} %bitcast.212), channel_id=1, source_target_pairs={{0,16},{1,17},{2,18},{3,19},{4,20},{5,21},{6,22},{7,23},{8,24},{9,... | collective-permute-start | bytes 1572872 | tf_op jit(solution)/shard_map/ppermute | solution.py:29
  96.1 31.9 %collective-permute-start.14 = (bf16[512,512]{1,0:T(8,128)(2,1)}, bf16[512,512]{1,0:T(8,128)(2,1)S(1)}, u32[]{:S(2)}, u32[]{:S(2)}) collective-permute-start(bf16[512,512]{1,0:T(8,128)(2,1)} %bitcast.220), channel_id=1, source_target_pairs={{0,8},{1,9},{2,10},{3,11},{4,12},{5,13},{6,14},{7,15},{8,0},{9,1},... | collective-permute-start | bytes 1572872 | tf_op jit(solution)/shard_map/ppermute | solution.py:29
  129.4 165.8 %all-gather.5.cloned.1.call-start = ((), (), s32[]{:S(2)}) async-start(), calls=%async_computation | async-start | bytes 4718592 | tf_op jit(solution)/shard_map/all_gather | solution.py:71
  129.5 28.1 %collective-permute-start.8 = (bf16[768,512]{1,0:T(8,128)(2,1)S(1)}, bf16[768,512]{1,0:T(8,128)(2,1)}, u32[]{:S(2)}, u32[]{:S(2)}) collective-permute-start(bf16[768,512]{1,0:T(8,128)(2,1)S(1)} %collective-permute-done.1.refs_1_), channel_id=1, source_target_pairs={{0,2},{1,3},{2,0},{3,1},{4,6},{5,7},{6,4},{7,5},{8,10},{9,11},{10,... | collective-permute-start | bytes 2359304 | tf_op jit(solution)/shard_map/ppermute | solution.py:29
  131.8 25.4 %collective-permute-start.5 = (bf16[512,512]{1,0:T(8,128)(2,1)}, bf16[512,512]{1,0:T(8,128)(2,1)S(1)}, u32[]{:S(2)}, u32[]{:S(2)}) collective-permute-start(bf16[512,512]{1,0:T(8,128)(2,1)} %bitcast.11), channel_id=1, source_target_pairs={{0,24},{1,25},{2,26},{3,27},{4,28},{5,29},{6,30},{7,31},{8,16},{9,... | collective-permute-start | bytes 1572872 | tf_op jit(solution)/shard_map/ppermute | solution.py:29
  133.1 30.6 %collective-permute-start.2 = (bf16[768,512]{1,0:T(8,128)(2,1)}, bf16[768,512]{1,0:T(8,128)(2,1)S(1)}, u32[]{:S(2)}, u32[]{:S(2)}) collective-permute-start(bf16[768,512]{1,0:T(8,128)(2,1)} %collective-permute-done.refs_0_), channel_id=1, source_target_pairs={{0,1},{1,0},{2,3},{3,2},{4,5},{5,4},{6,7},{7,6},{8,9},{9,8},{10,11... | collective-permute-start | bytes 2359304 | tf_op jit(solution)/shard_map/ppermute | solution.py:29
  163.6 23.1 %collective-permute-start.18 = (bf16[512,512]{1,0:T(8,128)(2,1)}, bf16[512,512]{1,0:T(8,128)(2,1)S(1)}, u32[]{:S(2)}, u32[]{:S(2)}) collective-permute-start(bf16[512,512]{1,0:T(8,128)(2,1)} %bitcast.17), channel_id=1, source_target_pairs={{0,16},{1,17},{2,18},{3,19},{4,20},{5,21},{6,22},{7,23},{8,24},{9,... | collective-permute-start | bytes 1572872 | tf_op jit(solution)/shard_map/ppermute | solution.py:29
  178.0 21.1 %collective-permute-start.15 = (bf16[512,512]{1,0:T(8,128)(2,1)}, bf16[512,512]{1,0:T(8,128)(2,1)S(1)}, u32[]{:S(2)}, u32[]{:S(2)}) collective-permute-start(bf16[512,512]{1,0:T(8,128)(2,1)} %bitcast.11), channel_id=1, source_target_pairs={{0,8},{1,9},{2,10},{3,11},{4,12},{5,13},{6,14},{7,15},{8,0},{9,1},... | collective-permute-start | bytes 1572872 | tf_op jit(solution)/shard_map/ppermute | solution.py:29
  183.2 63.0 %collective-permute-start.21 = (bf16[1024,256]{1,0:T(8,128)(2,1)}, bf16[1024,256]{1,0:T(8,128)(2,1)}, u32[]{:S(2)}, u32[]{:S(2)}) collective-permute-start(bf16[1024,256]{1,0:T(8,128)(2,1)} %bitcast.38), channel_id=1, source_target_pairs={{0,4},{1,5},{2,6},{3,7},{4,0},{5,1},{6,2},{7,3},{8,12},{9,13},{10,... | collective-permute-start | bytes 1572872 | tf_op jit(solution)/shard_map/ppermute | solution.py:29
  200.5 155.4 %all-gather.11.cloned.1.call-start = ((), (), s32[]{:S(2)}) async-start(), calls=%async_computation.3 | async-start | bytes 4718592 | tf_op jit(solution)/shard_map/all_gather | solution.py:71
  239.0 23.4 %collective-permute-start.24 = (bf16[2,144,512]{1,2,0:T(8,128)(2,1)}, bf16[2,144,512]{1,2,0:T(8,128)(2,1)S(1)}, u32[]{:S(2)}, u32[]{:S(2)}) collective-permute-start(bf16[2,144,512]{1,2,0:T(8,128)(2,1)} %pad_maximum_fusion.6), channel_id=1, source_target_pairs={{0,4},{1,5},{2,6},{3,7},{4,0},{5,1},{6,2},{7,3},{8,12},{9,13},{10,... | collective-permute-start | bytes 884744 | tf_op jit(solution)/shard_map/ppermute | solution.py:29
  242.9 36.8 %collective-permute-start.19 = (bf16[1024,256]{1,0:T(8,128)(2,1)}, bf16[1024,256]{1,0:T(8,128)(2,1)S(1)}, u32[]{:S(2)}, u32[]{:S(2)}) collective-permute-start(bf16[1024,256]{1,0:T(8,128)(2,1)} %bitcast.38), channel_id=1, source_target_pairs={{0,16},{1,17},{2,18},{3,19},{4,20},{5,21},{6,22},{7,23},{8,24},{9,... | collective-permute-start | bytes 1572872 | tf_op jit(solution)/shard_map/ppermute | solution.py:29
  246.0 46.4 %collective-permute-start.20 = (bf16[1024,256]{1,0:T(8,128)(2,1)S(1)}, bf16[1024,256]{1,0:T(8,128)(2,1)S(1)}, u32[]{:S(2)}, u32[]{:S(2)}) collective-permute-start(bf16[1024,256]{1,0:T(8,128)(2,1)S(1)} %bitcast.222), channel_id=1, source_target_pairs={{0,24},{1,25},{2,26},{3,27},{4,28},{5,29},{6,30},{7,31},{8,16},{9,... | collective-permute-start | bytes 1572872 | tf_op jit(solution)/shard_map/ppermute | solution.py:29
  246.3 46.1 %collective-permute-start.22 = (bf16[1024,256]{1,0:T(8,128)(2,1)S(1)}, bf16[1024,256]{1,0:T(8,128)(2,1)S(1)}, u32[]{:S(2)}, u32[]{:S(2)}) collective-permute-start(bf16[1024,256]{1,0:T(8,128)(2,1)S(1)} %bitcast.223), channel_id=1, source_target_pairs={{0,8},{1,9},{2,10},{3,11},{4,12},{5,13},{6,14},{7,15},{8,0},{9,1},... | collective-permute-start | bytes 1572872 | tf_op jit(solution)/shard_map/ppermute | solution.py:29
  309.7 26.3 %collective-permute-start.25 = (bf16[8,512]{0,1:T(8,128)(2,1)S(1)}, bf16[8,512]{0,1:T(8,128)(2,1)S(1)}, u32[]{:S(2)}, u32[]{:S(2)}) collective-permute-start(bf16[8,512]{0,1:T(8,128)(2,1)S(1)} %get-tuple-element.44), channel_id=1, source_target_pairs={{4,16},{5,17},{6,18},{7,19},{12,24},{13,25},{14,26},{15,27}} | collective-permute-start | bytes 24584 | tf_op jit(solution)/shard_map/ppermute | solution.py:29
  311.3 24.7 %collective-permute-start.26 = (bf16[2,8,512]{1,2,0:T(8,128)(2,1)S(1)}, bf16[2,8,512]{1,2,0:T(8,128)(2,1)S(1)}, u32[]{:S(2)}, u32[]{:S(2)}) collective-permute-start(bf16[2,8,512]{1,2,0:T(8,128)(2,1)S(1)} %pad_maximum_fusion.8), channel_id=1, source_target_pairs={{0,4},{1,5},{2,6},{3,7},{4,0},{5,1},{6,2},{7,3},{8,12},{9,13},{10,... | collective-permute-start | bytes 49160 | tf_op jit(solution)/shard_map/ppermute | solution.py:29
  370.7 35.6 %collective-permute-start.31 = (bf16[8,768,128]{2,1,0:T(8,128)(2,1)}, bf16[8,768,128]{2,1,0:T(8,128)(2,1)}, u32[]{:S(2)}, u32[]{:S(2)}) collective-permute-start(bf16[8,768,128]{2,1,0:T(8,128)(2,1)} %dynamic-slice_bitcast_fusion), channel_id=1, source_target_pairs={{0,8},{1,9},{2,10},{3,11},{4,12},{5,13},{6,14},{7,15},{8,0},{9,1},... | collective-permute-start | bytes 4718600 | tf_op jit(solution)/shard_map/ppermute | solution.py:29
  372.0 38.0 %collective-permute-start.28 = (bf16[16,384,128]{2,1,0:T(8,128)(2,1)}, bf16[16,384,128]{2,1,0:T(8,128)(2,1)}, u32[]{:S(2)}, u32[]{:S(2)}) collective-permute-start(bf16[16,384,128]{2,1,0:T(8,128)(2,1)} %dynamic-slice_bitcast_fusion.1), channel_id=1, source_target_pairs={{0,2},{1,3},{2,0},{3,1},{4,6},{5,7},{6,4},{7,5},{8,10},{9,11},{10,... | collective-permute-start | bytes 4718600 | tf_op jit(solution)/shard_map/ppermute | solution.py:29
  (43 other events, 417.4 us)
Sparse Core Ops, SparseCore 0:
  75.0 49.9 all-gather.6
  129.5 49.0 all-gather.8
  200.6 54.3 all-gather.4
  293.8 61.9 all-gather.10

commit v7 on v5

--- a/solution.py
+++ b/solution.py
@@ -412,7 +412,7 @@
         after(coefficients, q),
         bands,
     )
-    mixed = mix(span, q, rims(edges), filtered, coefficients)
+    mixed = mix(span, q, rims(edges), filtered, after(coefficients, outs[-1]))
     mixed = [mixed, places.flip(mixed, tp=1)]
 
     def over_y(value):

time: 412 us -> 419 us (1.017)
  waiting for transfers between devices: 197 us -> 204 us
    ppermute x34, waiting for transfers between devices: 165 us -> 184 us  [send(): return lax.ppermute(value, AXES, pairs)]
    all_gather x4, waiting for transfers between devices: 32 us -> 20.2 us  [cross(): return lax.all_gather(stack, 'ctx', axis_index_groups=groups, tiled=True)]
  transfers between devices with their start and end apart: 38 -> 38, of which waited for: 17 -> 20; matrix products, arithmetic and copies ran while one was open for 11% -> 10% of each run, Pallas kernels for 19% -> 16%
where the time goes in v7:
time: 419 us; the launch traced here: 418 us
  waiting for transfers between devices  204 us (49%)
  Pallas kernels  90.3 us (22%)
  starting transfers between devices  46.8 us (11%)
  local copies, waits for them, and re-layouts  32.7 us (8%)
  other arithmetic  28.5 us (7%)
  between operations  14 us (3%)
    ppermute x34, waiting for transfers between devices, send(): return lax.ppermute(value, AXES, pairs)  184 us
    ppermute x34, starting transfers between devices, send(): return lax.ppermute(value, AXES, pairs)  46.5 us
    pallas_call x3, Pallas kernels, project(): pl.pallas_call(project_kernel, out_shape=jax.ShapeDtypeStruct((width, row...  41.3 us
    all_gather x4, waiting for transfers between devices, cross(): return lax.all_gather(stack, 'ctx', axis_index_groups=groups, tiled=True)  20.2 us
    pallas_call x1, Pallas kernels, long_filter_part(): pl.pallas_call(functools.partial(filter_kernel, span), out_shape=jax.Shap...  14.1 us
    pallas_call x1, Pallas kernels, prepare(): pl.pallas_call(functools.partial(prepare_kernel, per_part), out_shape=jax...  13.4 us
    pallas_call x1, Pallas kernels, output_sums(): pl.pallas_call(functools.partial(output_kernel, len(mixed), chunks), out_...  12.1 us
    pallas_call x1, Pallas kernels, mix(): pl.pallas_call(functools.partial(mix_kernel, span), out_shape=jax.ShapeDt...  9.49 us
  transfers between devices with their start and end apart: 38, of which 20 were waited for; matrix products, arithmetic and copies ran while one was open for 10% of the time, Pallas kernels for 16%

profile of v7, /device:TPU:17, one launch (start us, length us, event | category | flops | bytes accessed | tf_op | source)
XLA Modules:
  0.0 418.1 jit_solution(17247487201645518092)
XLA Ops:
  29.9 9.4 %collective-permute-done.refs_0_ = bf16[768,512]{1,0:T(8,128)(2,1)} collective-permute-done((bf16[768,512]{1,0:T(8,128)(2,1)}, bf16[768,512]{1,0:T(8,128)(2,1)}, u32[]{:S(2)}, u32[]{:S(2)}) %collective-permute-start) | collective-permute-done | bytes 786464 | tf_op jit(solution)/shard_map/ppermute | solution.py:29
  39.3 13.3 %collective-permute-done.11.refs_1_ = bf16[3,512,512]{2,1,0:T(8,128)(2,1)} collective-permute-done((bf16[3,512,512]{2,1,0:T(8,128)(2,1)}, bf16[3,512,512]{2,1,0:T(8,128)(2,1)}, u32[]{:S(2)}, u32[]{:S(2)}) %collective-permute-start.11) | collective-permute-done | bytes 1572896 | tf_op jit(solution)/shard_map/ppermute | solution.py:29
  53.9 8.8 %collective-permute-done.3 = bf16[512,512]{1,0:T(8,128)(2,1)S(1)} collective-permute-done((bf16[512,512]{1,0:T(8,128)(2,1)S(1)}, bf16[512,512]{1,0:T(8,128)(2,1)S(1)}, u32[]{:S(2)}, u32[]{:S(2)}) %collective-permute-start.3) | collective-permute-done | bytes 524320 | tf_op jit(solution)/shard_map/ppermute | solution.py:29
  62.7 10.2 %collective-permute-done.16 = bf16[512,512]{1,0:T(8,128)(2,1)S(1)} collective-permute-done((bf16[512,512]{1,0:T(8,128)(2,1)S(1)}, bf16[512,512]{1,0:T(8,128)(2,1)S(1)}, u32[]{:S(2)}, u32[]{:S(2)}) %collective-permute-start.16) | collective-permute-done | bytes 524320 | tf_op jit(solution)/shard_map/ppermute | solution.py:29
  82.2 23.2 %collective-permute-done.1.refs_1_ = bf16[768,512]{1,0:T(8,128)(2,1)S(1)} collective-permute-done((bf16[768,512]{1,0:T(8,128)(2,1)}, bf16[768,512]{1,0:T(8,128)(2,1)S(1)}, u32[]{:S(2)}, u32[]{:S(2)}) %collective-permute-start.1) | collective-permute-done | bytes 786464 | tf_op jit(solution)/shard_map/ppermute | solution.py:29
  108.1 14.1 %collective-permute-done.17 = bf16[512,512]{1,0:T(8,128)(2,1)S(1)} collective-permute-done((bf16[512,512]{1,0:T(8,128)(2,1)S(1)}, bf16[512,512]{1,0:T(8,128)(2,1)S(1)}, u32[]{:S(2)}, u32[]{:S(2)}) %collective-permute-start.17) | collective-permute-done | bytes 524320 | tf_op jit(solution)/shard_map/ppermute | solution.py:29
  122.2 5.6 %collective-permute-done.14 = bf16[512,512]{1,0:T(8,128)(2,1)S(1)} collective-permute-done((bf16[512,512]{1,0:T(8,128)(2,1)S(1)}, bf16[512,512]{1,0:T(8,128)(2,1)S(1)}, u32[]{:S(2)}, u32[]{:S(2)}) %collective-permute-start.14) | collective-permute-done | bytes 524320 | tf_op jit(solution)/shard_map/ppermute | solution.py:29
  130.9 3.5 collective-permute-start.2
  134.4 21.6 %collective-permute-done.5 = bf16[512,512]{1,0:T(8,128)(2,1)S(1)} collective-permute-done((bf16[512,512]{1,0:T(8,128)(2,1)S(1)}, bf16[512,512]{1,0:T(8,128)(2,1)S(1)}, u32[]{:S(2)}, u32[]{:S(2)}) %collective-permute-start.5) | collective-permute-done | bytes 524320 | tf_op jit(solution)/shard_map/ppermute | solution.py:29
  160.7 13.4 %shard_map.73.tokens = bf16[4096,1536]{1,0:T(8,128)(2,1)} custom-call(s32[8]{0:T(128)} %stack.158.order, s32[2]{0:T(128)} %pad_add_fusion.flags, bf16[768,4096]{1,0:T(8,128)(2,1)} %own.1, bf16[768,512]{1,0:T(8,128)(2,1)} %collective-permute-done.refs_0_, bf16[768,512]{1,0:T(8,128)(2,1)} %copy-done.4, bf16[768,512]{1,0:T(8,128)(2,1)} %collective-permute-done.2.refs_2_, ...), custom_call_target="tpu_custom_call" | custom-call | bytes 25165824 | tf_op jit(solution)/shard_map/pallas_call | solution.py:91
  176.7 5.1 %collective-permute-done.18 = bf16[512,512]{1,0:T(8,128)(2,1)S(1)} collective-permute-done((bf16[512,512]{1,0:T(8,128)(2,1)}, bf16[512,512]{1,0:T(8,128)(2,1)S(1)}, u32[]{:S(2)}, u32[]{:S(2)}) %collective-permute-start.18) | collective-permute-done | bytes 524320 | tf_op jit(solution)/shard_map/ppermute | solution.py:29
  181.8 10.9 %collective-permute-done.15 = bf16[512,512]{1,0:T(8,128)(2,1)S(1)} collective-permute-done((bf16[512,512]{1,0:T(8,128)(2,1)S(1)}, bf16[512,512]{1,0:T(8,128)(2,1)S(1)}, u32[]{:S(2)}, u32[]{:S(2)}) %collective-permute-start.15) | collective-permute-done | bytes 524320 | tf_op jit(solution)/shard_map/ppermute | solution.py:29
  200.3 4.1 collective-permute-start.19
  204.4 13.8 %shard_map.74.k = bf16[512,1536]{1,0:T(8,128)(2,1)} custom-call(bf16[4096,1536]{1,0:T(8,128)(2,1)} %shard_map.73.tokens, bf16[3,512,512]{2,1,0:T(8,128)(2,1)} %pad_maximum_fusion.1.refs_0_, bf16[3,512,512]{2,1,0:T(8,128)(2,1)} %collective-permute-done.11.refs_1_, bf16[6,512,512]{2,1,0:T(8,128)(2,1)} %all-gather.7.cloned.1.call-done.refs_2_), custom_call_target="tpu_custom_call" | custom-call | flops 6442450944 | bytes 22544384 | tf_op jit(solution)/shard_map/pallas_call | solution.py:121
  220.7 13.3 %shard_map.75.v = bf16[512,1536]{1,0:T(8,128)(2,1)} custom-call(bf16[4096,1536]{1,0:T(8,128)(2,1)} %shard_map.73.tokens, bf16[3,512,512]{2,1,0:T(8,128)(2,1)} %pad_maximum_fusion.1.refs_0_, bf16[3,512,512]{2,1,0:T(8,128)(2,1)} %collective-permute-done.11.refs_1_, bf16[6,512,512]{2,1,0:T(8,128)(2,1)} %all-gather.9.cloned.1.call-done.refs_2_), custom_call_target="tpu_custom_call" | custom-call | flops 6442450944 | bytes 22544384 | tf_op jit(solution)/shard_map/pallas_call | solution.py:121
  242.9 6.1 %collective-permute-done.20 = bf16[1024,256]{1,0:T(8,128)(2,1)S(1)} collective-permute-done((bf16[1024,256]{1,0:T(8,128)(2,1)}, bf16[1024,256]{1,0:T(8,128)(2,1)S(1)}, u32[]{:S(2)}, u32[]{:S(2)}) %collective-permute-start.20) | collective-permute-done | bytes 524320 | tf_op jit(solution)/shard_map/ppermute | solution.py:29
  256.3 14.2 %shard_map.76.q = bf16[512,1536]{1,0:T(8,128)(2,1)} custom-call(bf16[4096,1536]{1,0:T(8,128)(2,1)} %shard_map.73.tokens, bf16[3,512,512]{2,1,0:T(8,128)(2,1)} %pad_maximum_fusion.1.refs_0_, bf16[3,512,512]{2,1,0:T(8,128)(2,1)} %collective-permute-done.11.refs_1_, bf16[6,512,512]{2,1,0:T(8,128)(2,1)} %all-gather.5.cloned.1.call-done.refs_2_), custom_call_target="tpu_custom_call" | custom-call | flops 6442450944 | bytes 22544384 | tf_op jit(solution)/shard_map/pallas_call | solution.py:121
  276.1 14.1 %shard_map.77.filtered = f32[512,1536]{1,0:T(8,128)} custom-call(bf16[512,1536]{1,0:T(8,128)(2,1)} %shard_map.74.k, bf16[512,1536]{1,0:T(8,128)(2,1)} %shard_map.75.v, bf16[512,256]{1,0:T(8,128)(2,1)} %fusion.19.k_rim, bf16[512,256]{1,0:T(8,128)(2,1)} %fusion.20.v_rim, bf16[512,256]{1,0:T(8,128)(2,1)} %pad_maximum_fusion.9.before, ...), custom_call_target="tpu_custom_call" | custom-call | flops 446693376 | bytes 8388608 | tf_op jit(solution)/shard_map/pallas_call | solution.py:175
  291.0 20.1 %all-gather.11.cloned.1.call-done.refs_4_ = bf16[6,1024,256]{2,1,0:T(8,128)(2,1)} async-done(((bf16[3,1024,256]{2,1,0:T(8,128)(2,1)}), bf16[6,1024,256]{2,1,0:T(8,128)(2,1)}) %all-gather.11.cloned.1.call-update) | async-done | bytes 3145744 | tf_op jit(solution)/shard_map/all_gather | solution.py:71
  311.2 9.5 %shard_map.78.refs_0_ = bf16[1536,512]{1,0:T(8,128)(2,1)} custom-call(bf16[512,1536]{1,0:T(8,128)(2,1)} %shard_map.76.q, bf16[512,256]{1,0:T(8,128)(2,1)} %fusion.18.q_rim, f32[512,1536]{1,0:T(8,128)} %shard_map.77.filtered, f32[512,24]{1,0:T(8,128)} %pad.29.coefficients), custom_call_target="tpu_custom_call" | custom-call | flops 11010048 | bytes 6291456 | tf_op jit(solution)/shard_map/pallas_call | solution.py:203
  325.5 12.1 %shard_map.79 = (bf16[8,1536,128]{2,1,0:T(8,128)(2,1)}, bf16[8,1536,128]{2,1,0:T(8,128)(2,1)}) custom-call(s32[8]{0:T(128)} %stack.158.order, bf16[1536,512]{1,0:T(8,128)(2,1)} %shard_map.78.refs_0_, bf16[1536,512]{1,0:T(8,128)(2,1)} %copy-done.37, bf16[1,1024,256]{2,1,0:T(8,128)(2,1)} %bitcast.221, bf16[1,1024,256]{2,1,0:T(8,128)(2,1)} %bitcast.263, ...), custom_call_target="tpu_custom_call" | custom-call | flops 6442450944 | bytes 13631488 | tf_op jit(solution)/shard_map/pallas_call | solution.py:238
  340.4 5.2 %collective-permute-start.31 = (bf16[8,768,128]{2,1,0:T(8,128)(2,1)}, bf16[8,768,128]{2,1,0:T(8,128)(2,1)}, u32[]{:S(2)}, u32[]{:S(2)}) collective-permute-start(bf16[8,768,128]{2,1,0:T(8,128)(2,1)} %dynamic-slice_bitcast_fusion), channel_id=1, source_target_pairs={{0,8},{1,9},{2,10},{3,11},{4,12},{5,13},{6,14},{7,15},{8,0},{9,1},... | collective-permute-start | bytes 4718600 | tf_op jit(solution)/shard_map/ppermute | solution.py:29
  347.7 32.6 %collective-permute-done.31 = bf16[8,768,128]{2,1,0:T(8,128)(2,1)} collective-permute-done((bf16[8,768,128]{2,1,0:T(8,128)(2,1)}, bf16[8,768,128]{2,1,0:T(8,128)(2,1)}, u32[]{:S(2)}, u32[]{:S(2)}) %collective-permute-start.31) | collective-permute-done | bytes 1572896 | tf_op jit(solution)/shard_map/ppermute | solution.py:29
  386.8 14.2 %collective-permute-done.32 = bf16[8,384,128]{2,1,0:T(8,128)(2,1)S(1)} collective-permute-done((bf16[8,384,128]{2,1,0:T(8,128)(2,1)S(1)}, bf16[8,384,128]{2,1,0:T(8,128)(2,1)S(1)}, u32[]{:S(2)}, u32[]{:S(2)}) %collective-permute-start.32) | collective-permute-done | bytes 786464 | tf_op jit(solution)/shard_map/ppermute | solution.py:29
  (220 shorter events, 105.8 us)
Async XLA Ops:
  6.5 197.9 %all-gather.7.cloned.1.call-start = ((), (), s32[]{:S(2)}) async-start(), calls=%async_computation.1 | async-start | bytes 4718592 | tf_op jit(solution)/shard_map/all_gather | solution.py:71
  17.0 35.6 %collective-permute-start.11 = (bf16[3,512,512]{2,1,0:T(8,128)(2,1)}, bf16[3,512,512]{2,1,0:T(8,128)(2,1)}, u32[]{:S(2)}, u32[]{:S(2)}) collective-permute-start(bf16[3,512,512]{2,1,0:T(8,128)(2,1)} %pad_maximum_fusion.1.refs_0_), channel_id=1, source_target_pairs={{0,4},{1,5},{2,6},{3,7},{4,0},{5,1},{6,2},{7,3},{8,12},{9,13},{10,... | collective-permute-start | bytes 4718600 | tf_op jit(solution)/shard_map/ppermute | solution.py:29
  27.6 35.2 %collective-permute-start.3 = (bf16[512,512]{1,0:T(8,128)(2,1)S(1)}, bf16[512,512]{1,0:T(8,128)(2,1)S(1)}, u32[]{:S(2)}, u32[]{:S(2)}) collective-permute-start(bf16[512,512]{1,0:T(8,128)(2,1)S(1)} %bitcast.214), channel_id=1, source_target_pairs={{0,24},{1,25},{2,26},{3,27},{4,28},{5,29},{6,30},{7,31},{8,16},{9,... | collective-permute-start | bytes 1572872 | tf_op jit(solution)/shard_map/ppermute | solution.py:29
  27.6 45.3 %collective-permute-start.16 = (bf16[512,512]{1,0:T(8,128)(2,1)S(1)}, bf16[512,512]{1,0:T(8,128)(2,1)S(1)}, u32[]{:S(2)}, u32[]{:S(2)}) collective-permute-start(bf16[512,512]{1,0:T(8,128)(2,1)S(1)} %bitcast.209), channel_id=1, source_target_pairs={{0,16},{1,17},{2,18},{3,19},{4,20},{5,21},{6,22},{7,23},{8,24},{9,... | collective-permute-start | bytes 1572872 | tf_op jit(solution)/shard_map/ppermute | solution.py:29
  52.6 22.1 %collective-permute-start.13 = (bf16[512,512]{1,0:T(8,128)(2,1)S(1)}, bf16[512,512]{1,0:T(8,128)(2,1)S(1)}, u32[]{:S(2)}, u32[]{:S(2)}) collective-permute-start(bf16[512,512]{1,0:T(8,128)(2,1)S(1)} %bitcast.215), channel_id=1, source_target_pairs={{0,8},{1,9},{2,10},{3,11},{4,12},{5,13},{6,14},{7,15},{8,0},{9,1},... | collective-permute-start | bytes 1572872 | tf_op jit(solution)/shard_map/ppermute | solution.py:29
  76.0 144.6 %all-gather.9.cloned.1.call-start = ((), (), s32[]{:S(2)}) async-start(), calls=%async_computation.2 | async-start | bytes 4718592 | tf_op jit(solution)/shard_map/all_gather | solution.py:71
  76.1 29.3 %collective-permute-start.1 = (bf16[768,512]{1,0:T(8,128)(2,1)}, bf16[768,512]{1,0:T(8,128)(2,1)S(1)}, u32[]{:S(2)}, u32[]{:S(2)}) collective-permute-start(bf16[768,512]{1,0:T(8,128)(2,1)} %get-tuple-element.45), channel_id=1, source_target_pairs={{0,8},{1,9},{2,10},{3,11},{4,12},{5,13},{6,14},{7,15},{8,0},{9,1},... | collective-permute-start | bytes 2359304 | tf_op jit(solution)/shard_map/ppermute | solution.py:29
  78.5 26.9 %collective-permute-start.7 = (bf16[768,512]{1,0:T(8,128)(2,1)}, bf16[768,512]{1,0:T(8,128)(2,1)S(1)}, u32[]{:S(2)}, u32[]{:S(2)}) collective-permute-start(bf16[768,512]{1,0:T(8,128)(2,1)} %collective-permute-done.refs_0_), channel_id=1, source_target_pairs={{0,2},{1,3},{2,0},{3,1},{4,6},{5,7},{6,4},{7,5},{8,10},{9,11},{10,... | collective-permute-start | bytes 2359304 | tf_op jit(solution)/shard_map/ppermute | solution.py:29
  79.9 28.2 %collective-permute-start.4 = (bf16[512,512]{1,0:T(8,128)(2,1)S(1)}, bf16[512,512]{1,0:T(8,128)(2,1)S(1)}, u32[]{:S(2)}, u32[]{:S(2)}) collective-permute-start(bf16[512,512]{1,0:T(8,128)(2,1)S(1)} %bitcast.216), channel_id=1, source_target_pairs={{0,24},{1,25},{2,26},{3,27},{4,28},{5,29},{6,30},{7,31},{8,16},{9,... | collective-permute-start | bytes 1572872 | tf_op jit(solution)/shard_map/ppermute | solution.py:29
  80.0 42.2 %collective-permute-start.17 = (bf16[512,512]{1,0:T(8,128)(2,1)S(1)}, bf16[512,512]{1,0:T(8,128)(2,1)S(1)}, u32[]{:S(2)}, u32[]{:S(2)}) collective-permute-start(bf16[512,512]{1,0:T(8,128)(2,1)S(1)} %bitcast.207), channel_id=1, source_target_pairs={{0,16},{1,17},{2,18},{3,19},{4,20},{5,21},{6,22},{7,23},{8,24},{9,... | collective-permute-start | bytes 1572872 | tf_op jit(solution)/shard_map/ppermute | solution.py:29
  105.4 22.4 %collective-permute-start.14 = (bf16[512,512]{1,0:T(8,128)(2,1)S(1)}, bf16[512,512]{1,0:T(8,128)(2,1)S(1)}, u32[]{:S(2)}, u32[]{:S(2)}) collective-permute-start(bf16[512,512]{1,0:T(8,128)(2,1)S(1)} %bitcast.217), channel_id=1, source_target_pairs={{0,8},{1,9},{2,10},{3,11},{4,12},{5,13},{6,14},{7,15},{8,0},{9,1},... | collective-permute-start | bytes 1572872 | tf_op jit(solution)/shard_map/ppermute | solution.py:29
  129.3 127.1 %all-gather.5.cloned.1.call-start = ((), (), s32[]{:S(2)}) async-start(), calls=%async_computation | async-start | bytes 4718592 | tf_op jit(solution)/shard_map/all_gather | solution.py:71
  129.3 27.0 %collective-permute-start.8 = (bf16[768,512]{1,0:T(8,128)(2,1)S(1)}, bf16[768,512]{1,0:T(8,128)(2,1)S(1)}, u32[]{:S(2)}, u32[]{:S(2)}) collective-permute-start(bf16[768,512]{1,0:T(8,128)(2,1)S(1)} %collective-permute-done.1.refs_1_), channel_id=1, source_target_pairs={{0,2},{1,3},{2,0},{3,1},{4,6},{5,7},{6,4},{7,5},{8,10},{9,11},{10,... | collective-permute-start | bytes 2359304 | tf_op jit(solution)/shard_map/ppermute | solution.py:29
  130.8 25.1 %collective-permute-start.5 = (bf16[512,512]{1,0:T(8,128)(2,1)S(1)}, bf16[512,512]{1,0:T(8,128)(2,1)S(1)}, u32[]{:S(2)}, u32[]{:S(2)}) collective-permute-start(bf16[512,512]{1,0:T(8,128)(2,1)S(1)} %bitcast.212), channel_id=1, source_target_pairs={{0,24},{1,25},{2,26},{3,27},{4,28},{5,29},{6,30},{7,31},{8,16},{9,... | collective-permute-start | bytes 1572872 | tf_op jit(solution)/shard_map/ppermute | solution.py:29
  130.9 27.9 %collective-permute-start.2 = (bf16[768,512]{1,0:T(8,128)(2,1)}, bf16[768,512]{1,0:T(8,128)(2,1)}, u32[]{:S(2)}, u32[]{:S(2)}) collective-permute-start(bf16[768,512]{1,0:T(8,128)(2,1)} %collective-permute-done.refs_0_), channel_id=1, source_target_pairs={{0,1},{1,0},{2,3},{3,2},{4,5},{5,4},{6,7},{7,6},{8,9},{9,8},{10,11... | collective-permute-start | bytes 2359304 | tf_op jit(solution)/shard_map/ppermute | solution.py:29
  158.7 23.1 %collective-permute-start.18 = (bf16[512,512]{1,0:T(8,128)(2,1)}, bf16[512,512]{1,0:T(8,128)(2,1)S(1)}, u32[]{:S(2)}, u32[]{:S(2)}) collective-permute-start(bf16[512,512]{1,0:T(8,128)(2,1)} %bitcast.17), channel_id=1, source_target_pairs={{0,16},{1,17},{2,18},{3,19},{4,20},{5,21},{6,22},{7,23},{8,24},{9,... | collective-permute-start | bytes 1572872 | tf_op jit(solution)/shard_map/ppermute | solution.py:29
  194.1 117.0 %all-gather.11.cloned.1.call-start = ((), (), s32[]{:S(2)}) async-start(), calls=%async_computation.3 | async-start | bytes 4718592 | tf_op jit(solution)/shard_map/all_gather | solution.py:71
  199.7 34.5 %collective-permute-start.21 = (bf16[1024,256]{1,0:T(8,128)(2,1)S(1)}, bf16[1024,256]{1,0:T(8,128)(2,1)S(1)}, u32[]{:S(2)}, u32[]{:S(2)}) collective-permute-start(bf16[1024,256]{1,0:T(8,128)(2,1)S(1)} %bitcast.219), channel_id=1, source_target_pairs={{0,4},{1,5},{2,6},{3,7},{4,0},{5,1},{6,2},{7,3},{8,12},{9,13},{10,... | collective-permute-start | bytes 1572872 | tf_op jit(solution)/shard_map/ppermute | solution.py:29
  200.3 42.6 %collective-permute-start.19 = (bf16[1024,256]{1,0:T(8,128)(2,1)S(1)}, bf16[1024,256]{1,0:T(8,128)(2,1)S(1)}, u32[]{:S(2)}, u32[]{:S(2)}) collective-permute-start(bf16[1024,256]{1,0:T(8,128)(2,1)S(1)} %bitcast.220), channel_id=1, source_target_pairs={{0,16},{1,17},{2,18},{3,19},{4,20},{5,21},{6,22},{7,23},{8,24},{9,... | collective-permute-start | bytes 1572872 | tf_op jit(solution)/shard_map/ppermute | solution.py:29
  204.4 44.5 %collective-permute-start.20 = (bf16[1024,256]{1,0:T(8,128)(2,1)}, bf16[1024,256]{1,0:T(8,128)(2,1)S(1)}, u32[]{:S(2)}, u32[]{:S(2)}) collective-permute-start(bf16[1024,256]{1,0:T(8,128)(2,1)} %bitcast.39), channel_id=1, source_target_pairs={{0,24},{1,25},{2,26},{3,27},{4,28},{5,29},{6,30},{7,31},{8,16},{9,... | collective-permute-start | bytes 1572872 | tf_op jit(solution)/shard_map/ppermute | solution.py:29
  241.5 31.8 %collective-permute-start.25 = (bf16[144,512]{0,1:T(8,128)(2,1)}, bf16[144,512]{0,1:T(8,128)(2,1)S(1)}, u32[]{:S(2)}, u32[]{:S(2)}) collective-permute-start(bf16[144,512]{0,1:T(8,128)(2,1)} %pad_maximum_fusion.8), channel_id=1, source_target_pairs={{4,16},{5,17},{6,18},{7,19},{12,24},{13,25},{14,26},{15,27}} | collective-permute-start | bytes 442376 | tf_op jit(solution)/shard_map/ppermute | solution.py:29
  253.2 20.1 %collective-permute-start.26 = (bf16[2,144,512]{1,2,0:T(8,128)(2,1)S(1)}, bf16[2,144,512]{1,2,0:T(8,128)(2,1)S(1)}, u32[]{:S(2)}, u32[]{:S(2)}) collective-permute-start(bf16[2,144,512]{1,2,0:T(8,128)(2,1)S(1)} %pad_maximum_fusion.6), channel_id=1, source_target_pairs={{0,4},{1,5},{2,6},{3,7},{4,0},{5,1},{6,2},{7,3},{8,12},{9,13},{10,... | collective-permute-start | bytes 884744 | tf_op jit(solution)/shard_map/ppermute | solution.py:29
  340.4 40.0 %collective-permute-start.31 = (bf16[8,768,128]{2,1,0:T(8,128)(2,1)}, bf16[8,768,128]{2,1,0:T(8,128)(2,1)}, u32[]{:S(2)}, u32[]{:S(2)}) collective-permute-start(bf16[8,768,128]{2,1,0:T(8,128)(2,1)} %dynamic-slice_bitcast_fusion), channel_id=1, source_target_pairs={{0,8},{1,9},{2,10},{3,11},{4,12},{5,13},{6,14},{7,15},{8,0},{9,1},... | collective-permute-start | bytes 4718600 | tf_op jit(solution)/shard_map/ppermute | solution.py:29
  346.8 36.9 %collective-permute-start.28 = (bf16[16,384,128]{2,1,0:T(8,128)(2,1)}, bf16[16,384,128]{2,1,0:T(8,128)(2,1)}, u32[]{:S(2)}, u32[]{:S(2)}) collective-permute-start(bf16[16,384,128]{2,1,0:T(8,128)(2,1)} %dynamic-slice_bitcast_fusion.1), channel_id=1, source_target_pairs={{0,2},{1,3},{2,0},{3,1},{4,6},{5,7},{6,4},{7,5},{8,10},{9,11},{10,... | collective-permute-start | bytes 4718600 | tf_op jit(solution)/shard_map/ppermute | solution.py:29
  (55 other events, 473.9 us)
Sparse Core Ops, SparseCore 0:
  76.1 48.8 all-gather.6
  129.4 48.5 all-gather.8
  194.3 53.1 all-gather.4
  250.5 60.5 all-gather.10
